TPU v7x, 128 devices: a whole 4x4x4 slice. The times are simulated.
128 devices in a mesh: dp: 4 (over y), seq: 16 (over x, z), tensor: 2 (over core).
Axes of the slice: x: 4, y: 4, z: 4, core: 2. Of those that a mesh axis runs over, the one named last changes fastest.
Arguments:
- tokens: float32 [10240, 2560], P(('dp', 'seq')), may hold values from -6 to 6
- cotangent: float32 [10240, 2560], P(('dp', 'seq')), may hold values from -6 to 6
- w_query: float32 [2560, 2560], P(('dp', 'seq'), 'tensor'), may hold values from -0.125 to 0.125
- w_keyvalue: float32 [2560, 2, 256], P(('dp', 'seq')), may hold values from -0.125 to 0.125
- w_out: float32 [2560, 2560], P('tensor', ('dp', 'seq')), may hold values from -2.5 to 2.5
- w_gateup: float32 [2560, 2, 7680], P(('dp', 'seq'), None, 'tensor'), may hold values from -0.125 to 0.125
- w_down: float32 [7680, 2560], P('tensor', ('dp', 'seq')), may hold values from -0.09375 to 0.09375
- norm_scales: float32 [2, 2560], P(None, ('dp', 'seq')), may hold values from -0.8 to 0.8
- first_query: float32 [2560, 2560], P(('dp', 'seq'), 'tensor'), may hold values from -96 to 96
- first_keyvalue: float32 [2560, 2, 256], P(('dp', 'seq')), may hold values from -192 to 192
- first_out: float32 [2560, 2560], P('tensor', ('dp', 'seq')), may hold values from -5 to 5
- first_gateup: float32 [2560, 2, 7680], P(('dp', 'seq'), None, 'tensor'), may hold values from -32 to 32
- first_down: float32 [7680, 2560], P('tensor', ('dp', 'seq')), may hold values from -40 to 40
- first_scales: float32 [2, 2560], P(None, ('dp', 'seq')), may hold values from -112 to 112
- second_query: float32 [2560, 2560], P(('dp', 'seq'), 'tensor'), may hold values from 1228.8 to 4812.8
- second_keyvalue: float32 [2560, 2, 256], P(('dp', 'seq')), may hold values from 4812.8 to 19456
- second_out: float32 [2560, 2560], P('tensor', ('dp', 'seq')), may hold values from 2.5 to 10
- second_gateup: float32 [2560, 2, 7680], P(('dp', 'seq'), None, 'tensor'), may hold values from 133.12 to 542.72
- second_down: float32 [7680, 2560], P('tensor', ('dp', 'seq')), may hold values from 225.28 to 901.12
- second_scales: float32 [2, 2560], P(None, ('dp', 'seq')), may hold values from 1331.2 to 5427.2
Outputs:
- output: float32 [10240, 2560], P(('dp', 'seq'))
- grad_tokens: float32 [10240, 2560], P(('dp', 'seq'))
- new_query: float32 [2560, 2560], P(('dp', 'seq'), 'tensor')
- new_keyvalue: float32 [2560, 2, 256], P(('dp', 'seq'))
- new_out: float32 [2560, 2560], P('tensor', ('dp', 'seq'))
- new_gateup: float32 [2560, 2, 7680], P(('dp', 'seq'), None, 'tensor')
- new_down: float32 [7680, 2560], P('tensor', ('dp', 'seq'))
- new_scales: float32 [2, 2560], P(None, ('dp', 'seq'))
- new_first_query: float32 [2560, 2560], P(('dp', 'seq'), 'tensor')
- new_first_keyvalue: float32 [2560, 2, 256], P(('dp', 'seq'))
- new_first_out: float32 [2560, 2560], P('tensor', ('dp', 'seq'))
- new_first_gateup: float32 [2560, 2, 7680], P(('dp', 'seq'), None, 'tensor')
- new_first_down: float32 [7680, 2560], P('tensor', ('dp', 'seq'))
- new_first_scales: float32 [2, 2560], P(None, ('dp', 'seq'))
- new_second_query: float32 [2560, 2560], P(('dp', 'seq'), 'tensor')
- new_second_keyvalue: float32 [2560, 2, 256], P(('dp', 'seq'))
- new_second_out: float32 [2560, 2560], P('tensor', ('dp', 'seq'))
- new_second_gateup: float32 [2560, 2, 7680], P(('dp', 'seq'), None, 'tensor')
- new_second_down: float32 [7680, 2560], P('tensor', ('dp', 'seq'))
- new_second_scales: float32 [2, 2560], P(None, ('dp', 'seq'))
All inputs are finite; a program needn't handle non-finite values.
Results may differ from a plain program's by a relative error of at most 0.02.
Values may be sent and summed in bfloat16 or wider, within the bound.
A program may use at most 384 MiB of HBM per device.

v0:
```python
import jax
import jax.numpy as jnp
from jax import lax
from jax.sharding import PartitionSpec as P

D = 2560
H = 10
HD = 256
FF = 7680
WINDOW = 2048
STEP = 10


eps_norm = 1e-06
masked_fill = -1e30
first_decay = 0.9
second_decay = 0.95
adam_eps = 1e-08
weight_decay = 0.1
gain_rate = 0.2


def rotate(values, positions, direction):
    quarter = values.shape[-1] // 4
    frequency = 10000.0 ** (-jnp.arange(quarter, dtype=jnp.float32) / quarter)
    angles = positions.astype(jnp.float32)[:, None] * frequency[None, :]
    table_shape = (angles.shape[0],) + (1,) * (values.ndim - 2) + (quarter,)
    cos_table = jnp.cos(angles).reshape(table_shape)
    sin_table = direction * jnp.sin(angles).reshape(table_shape)
    lower_part = values[..., :quarter]
    upper_part = values[..., quarter : 2 * quarter]
    kept_part = values[..., 2 * quarter :]
    return jnp.concatenate(
        [
            lower_part * cos_table - upper_part * sin_table,
            upper_part * cos_table + lower_part * sin_table,
            kept_part,
        ],
        axis=-1,
    )


def rms_norm(values, offset):
    inverse = lax.rsqrt(jnp.mean(values * values, axis=-1, keepdims=True) + eps_norm)
    return values * inverse * (1.0 + offset)


def adam_update(weight, gradient, first_moment, second_moment, learn_rate, decay_rate):
    first_moment = first_decay * first_moment + (1.0 - first_decay) * gradient
    second_moment = second_decay * second_moment + (1.0 - second_decay) * gradient * gradient
    corrected = (
        first_moment
        / (1.0 - first_decay**STEP)
        / (jnp.sqrt(second_moment / (1.0 - second_decay**STEP)) + adam_eps)
    )
    return (weight - learn_rate * (corrected + decay_rate * weight), first_moment, second_moment)


def out_fan_in(seq_length):
    return max(1, H * HD * 4 // min(WINDOW, seq_length))


def contract_rows(left_side, right_side):
    return lax.dot_general(
        left_side, right_side, (((0,), (0,)), ((), ())), preferred_element_type=jnp.float32
    )


def times_transposed(left_side, right_side):
    return lax.dot_general(
        left_side, right_side, (((1,), (1,)), ((), ())), preferred_element_type=jnp.float32
    )


def activate(gate_part, upper_part):
    return jax.nn.gelu(gate_part, approximate=True) * upper_part


def per_device(
    tokens,
    cotangent,
    w_query,
    w_keyvalue,
    w_out,
    w_gateup,
    w_down,
    norm_scales,
    first_query,
    first_keyvalue,
    first_out,
    first_gateup,
    first_down,
    first_scales,
    second_query,
    second_keyvalue,
    second_out,
    second_gateup,
    second_down,
    second_scales,
):
    seq_count = lax.axis_size("seq")
    seq_index = lax.axis_index("seq")
    group_len = tokens.shape[0]
    seq_length = group_len * seq_count
    halo_groups = min(seq_count - 1, (WINDOW + group_len - 2) // group_len)
    key_count = (halo_groups + 1) * group_len
    query_low_w = w_query.astype(jnp.bfloat16)
    keyvalue_low_w = w_keyvalue.astype(jnp.bfloat16)
    out_low_w = w_out.astype(jnp.bfloat16)
    gateup_low_w = w_gateup.astype(jnp.bfloat16)
    down_low_w = w_down.astype(jnp.bfloat16)
    scales_low_w = norm_scales.astype(jnp.bfloat16)
    query_full, keyvalue_full, out_full, gateup_full, down_full, scales_full = (
        lax.all_gather(query_low_w, ("dp", "seq"), axis=0, tiled=True),
        lax.all_gather(keyvalue_low_w, ("dp", "seq"), axis=0, tiled=True),
        lax.all_gather(out_low_w, ("dp", "seq"), axis=1, tiled=True),
        lax.all_gather(gateup_low_w, ("dp", "seq"), axis=0, tiled=True),
        lax.all_gather(down_low_w, ("dp", "seq"), axis=1, tiled=True),
        lax.all_gather(scales_low_w, ("dp", "seq"), axis=1, tiled=True),
    )
    scale_one = scales_full[0].astype(jnp.float32)
    scale_two = scales_full[1].astype(jnp.float32)
    positions = seq_index * group_len + jnp.arange(group_len, dtype=jnp.int32)
    normed_one, norm_back_one = jax.vjp(rms_norm, tokens, scale_one)
    normed_one = normed_one.astype(jnp.bfloat16)
    head_count = query_full.shape[1] // HD
    query_raw = jnp.dot(normed_one, query_full, preferred_element_type=jnp.float32).reshape(
        group_len, head_count, HD
    )
    query_low = (rotate(query_raw, positions, 1.0) * HD ** (-0.5)).astype(jnp.bfloat16)
    keyvalue = jnp.einsum(
        "cd,dgh->cgh", normed_one, keyvalue_full, preferred_element_type=jnp.float32
    )
    keyvalue_low = jnp.stack(
        [rotate(keyvalue[:, 0], positions, 1.0), keyvalue[:, 1]], axis=1
    ).astype(jnp.bfloat16)
    whole_seq = lax.all_gather(keyvalue_low, "seq", axis=0, tiled=True)
    padded = jnp.concatenate(
        [jnp.zeros((halo_groups * group_len, 2, HD), jnp.bfloat16), whole_seq], axis=0
    )
    window_rows = lax.dynamic_slice_in_dim(padded, seq_index * group_len, key_count, 0)
    key_rows = window_rows[:, 0]
    value_rows = window_rows[:, 1]
    key_pos = (seq_index - halo_groups) * group_len + jnp.arange(key_count, dtype=jnp.int32)
    distance = positions[:, None] - key_pos[None, :]
    visible = (distance >= 0) & (distance < WINDOW) & (key_pos[None, :] >= 0)
    scores = jnp.einsum("chd,kd->hck", query_low, key_rows, preferred_element_type=jnp.float32)
    scores = jnp.where(visible[None], scores, masked_fill)
    maximum = jnp.max(scores, axis=-1, keepdims=True)
    exponent = jnp.exp(scores - maximum)
    row_total = jnp.sum(exponent, axis=-1, keepdims=True)
    log_total = maximum + jnp.log(row_total)
    prob_low = (exponent / row_total).astype(jnp.bfloat16)
    attended = jnp.einsum("hck,kd->chd", prob_low, value_rows, preferred_element_type=jnp.float32)
    attended_low = attended.reshape(group_len, head_count * HD).astype(jnp.bfloat16)
    attention_part = jnp.dot(attended_low, out_full, preferred_element_type=jnp.float32)
    residual = tokens + lax.psum(attention_part.astype(jnp.bfloat16), "tensor").astype(jnp.float32)
    normed_two, norm_back_two = jax.vjp(rms_norm, residual, scale_two)
    normed_two = normed_two.astype(jnp.bfloat16)
    gateup = jnp.einsum("cd,dgf->cgf", normed_two, gateup_full, preferred_element_type=jnp.float32)
    hidden, activate_back = jax.vjp(activate, gateup[:, 0], gateup[:, 1])
    hidden_low = hidden.astype(jnp.bfloat16)
    feed_part = jnp.dot(hidden_low, down_full, preferred_element_type=jnp.float32)
    output = residual + lax.psum(feed_part.astype(jnp.bfloat16), "tensor").astype(jnp.float32)
    grad_out_low = cotangent.astype(jnp.bfloat16)
    grad_down = contract_rows(hidden_low, grad_out_low)
    grad_hidden = times_transposed(grad_out_low, down_full)
    grad_gate, grad_upper = activate_back(grad_hidden)
    grad_gateup_low = jnp.stack([grad_gate, grad_upper], axis=1).astype(jnp.bfloat16)
    grad_gateup = jnp.einsum(
        "cd,cgf->dgf", normed_two, grad_gateup_low, preferred_element_type=jnp.float32
    )
    norm_part_two = jnp.einsum(
        "cgf,dgf->cd", grad_gateup_low, gateup_full, preferred_element_type=jnp.float32
    )
    normed_grad_two = lax.psum(norm_part_two.astype(jnp.bfloat16), "tensor").astype(jnp.float32)
    grad_resid_norm, grad_scale_two = norm_back_two(normed_grad_two)
    grad_residual = cotangent + grad_resid_norm
    down_shard, gateup_shard, scale_two_shard = (
        lax.psum_scatter(grad_down, ("dp", "seq"), scatter_dimension=1, tiled=True),
        lax.psum_scatter(grad_gateup, ("dp", "seq"), scatter_dimension=0, tiled=True),
        lax.psum_scatter(grad_scale_two, ("dp", "seq"), scatter_dimension=0, tiled=True),
    )
    grad_attn_low = grad_residual.astype(jnp.bfloat16)
    grad_out = contract_rows(attended_low, grad_attn_low)
    grad_att_low = (
        times_transposed(grad_attn_low, out_full)
        .reshape(group_len, head_count, HD)
        .astype(jnp.bfloat16)
    )
    scores = jnp.einsum("chd,kd->hck", query_low, key_rows, preferred_element_type=jnp.float32)
    probs = jnp.where(visible[None], jnp.exp(scores - log_total), 0.0)
    prob_low = probs.astype(jnp.bfloat16)
    grad_probs = jnp.einsum(
        "chd,kd->hck", grad_att_low, value_rows, preferred_element_type=jnp.float32
    )
    delta = jnp.sum(probs * grad_probs, axis=-1, keepdims=True)
    grad_scores_low = (probs * (grad_probs - delta)).astype(jnp.bfloat16)
    grad_query = jnp.einsum(
        "hck,kd->chd", grad_scores_low, key_rows, preferred_element_type=jnp.float32
    )
    grad_keys = jnp.einsum(
        "hck,chd->kd", grad_scores_low, query_low, preferred_element_type=jnp.float32
    )
    grad_values = jnp.einsum(
        "hck,chd->kd", prob_low, grad_att_low, preferred_element_type=jnp.float32
    )
    grad_window = jnp.stack([grad_keys, grad_values], axis=1)
    spread = jnp.zeros((halo_groups * group_len + seq_length, 2, HD), jnp.float32)
    spread = lax.dynamic_update_slice_in_dim(spread, grad_window, seq_index * group_len, 0)
    grad_own = lax.psum_scatter(
        spread[halo_groups * group_len :].astype(jnp.bfloat16),
        "seq",
        scatter_dimension=0,
        tiled=True,
    )
    grad_kv = lax.psum(grad_own, "tensor").astype(jnp.float32)
    grad_kv_low = jnp.stack([rotate(grad_kv[:, 0], positions, -1.0), grad_kv[:, 1]], axis=1).astype(
        jnp.bfloat16
    )
    grad_query_low = (
        rotate(grad_query * HD ** (-0.5), positions, -1.0)
        .reshape(group_len, head_count * HD)
        .astype(jnp.bfloat16)
    )
    tensor_part = lax.axis_index("tensor")
    kv_half = lax.dynamic_index_in_dim(grad_kv_low, tensor_part, 1, keepdims=False)
    weight_half = lax.dynamic_index_in_dim(keyvalue_full, tensor_part, 1, keepdims=False)
    grad_kv_half = contract_rows(normed_one, kv_half)
    grad_query_w = contract_rows(normed_one, grad_query_low)
    norm_part_one = times_transposed(grad_query_low, query_full) + times_transposed(
        kv_half, weight_half
    )
    normed_grad_one = lax.psum(norm_part_one.astype(jnp.bfloat16), "tensor").astype(jnp.float32)
    grad_tokens_norm, grad_scale_one = norm_back_one(normed_grad_one)
    grad_tokens = grad_residual + grad_tokens_norm
    query_shard, kv_half_shard, out_shard, scale_one_shard = (
        lax.psum_scatter(grad_query_w, ("dp", "seq"), scatter_dimension=0, tiled=True),
        lax.psum_scatter(grad_kv_half, ("dp", "seq"), scatter_dimension=0, tiled=True),
        lax.psum_scatter(grad_out, ("dp", "seq"), scatter_dimension=1, tiled=True),
        lax.psum_scatter(grad_scale_one, ("dp", "seq"), scatter_dimension=0, tiled=True),
    )
    keyvalue_shard = lax.all_gather(
        kv_half_shard[:, None, :].astype(jnp.bfloat16), "tensor", axis=1, tiled=True
    ).astype(jnp.float32)
    matrix_rate = 2.0 * D ** (-0.5)
    new_query, new_first_query, new_second_query = adam_update(
        w_query, query_shard, first_query, second_query, matrix_rate, weight_decay
    )
    new_keyvalue, new_first_keyvalue, new_second_keyvalue = adam_update(
        w_keyvalue, keyvalue_shard, first_keyvalue, second_keyvalue, matrix_rate, weight_decay
    )
    new_out, new_first_out, new_second_out = adam_update(
        w_out,
        out_shard,
        first_out,
        second_out,
        2.0 * out_fan_in(seq_length) ** (-0.5),
        weight_decay,
    )
    new_gateup, new_first_gateup, new_second_gateup = adam_update(
        w_gateup, gateup_shard, first_gateup, second_gateup, matrix_rate, weight_decay
    )
    new_down, new_first_down, new_second_down = adam_update(
        w_down, down_shard, first_down, second_down, 2.0 * (FF // 2) ** (-0.5), weight_decay
    )
    scale_grads = jnp.stack([scale_one_shard, scale_two_shard], axis=0)
    new_scales, new_first_scales, new_second_scales = adam_update(
        norm_scales, scale_grads, first_scales, second_scales, gain_rate, 0.0
    )
    return (
        output,
        grad_tokens,
        new_query,
        new_keyvalue,
        new_out,
        new_gateup,
        new_down,
        new_scales,
        new_first_query,
        new_first_keyvalue,
        new_first_out,
        new_first_gateup,
        new_first_down,
        new_first_scales,
        new_second_query,
        new_second_keyvalue,
        new_second_out,
        new_second_gateup,
        new_second_down,
        new_second_scales,
    )


def solution(mesh):
    in_specs = (
        P(("dp", "seq"), None),
        P(("dp", "seq"), None),
        P(("dp", "seq"), "tensor"),
        P(("dp", "seq"), None, None),
        P("tensor", ("dp", "seq")),
        P(("dp", "seq"), None, "tensor"),
        P("tensor", ("dp", "seq")),
        P(None, ("dp", "seq")),
        P(("dp", "seq"), "tensor"),
        P(("dp", "seq"), None, None),
        P("tensor", ("dp", "seq")),
        P(("dp", "seq"), None, "tensor"),
        P("tensor", ("dp", "seq")),
        P(None, ("dp", "seq")),
        P(("dp", "seq"), "tensor"),
        P(("dp", "seq"), None, None),
        P("tensor", ("dp", "seq")),
        P(("dp", "seq"), None, "tensor"),
        P("tensor", ("dp", "seq")),
        P(None, ("dp", "seq")),
    )
    out_specs = (
        P(("dp", "seq"), None),
        P(("dp", "seq"), None),
        P(("dp", "seq"), "tensor"),
        P(("dp", "seq"), None, None),
        P("tensor", ("dp", "seq")),
        P(("dp", "seq"), None, "tensor"),
        P("tensor", ("dp", "seq")),
        P(None, ("dp", "seq")),
        P(("dp", "seq"), "tensor"),
        P(("dp", "seq"), None, None),
        P("tensor", ("dp", "seq")),
        P(("dp", "seq"), None, "tensor"),
        P("tensor", ("dp", "seq")),
        P(None, ("dp", "seq")),
        P(("dp", "seq"), "tensor"),
        P(("dp", "seq"), None, None),
        P("tensor", ("dp", "seq")),
        P(("dp", "seq"), None, "tensor"),
        P("tensor", ("dp", "seq")),
        P(None, ("dp", "seq")),
    )
    return jax.shard_map(
        per_device, mesh=mesh, in_specs=in_specs, out_specs=out_specs, check_vma=False
    )
```

profile of v0, /device:TPU:1, one launch (start us, length us, event | category | flops | bytes accessed | tf_op | source)
XLA Modules:
  0.0 2613.3 jit_solution(3429259284350114194)
XLA Ops:
  11.3 149.9 %all-gather.1 = bf16[64,40,2]{1,2,0:T(2,128)(2,1)S(1)} all-gather(bf16[1,40,2]{1,2,0:T(2,128)(2,1)S(1)} %convert_bitcast_fusion), channel_id=1, replica_groups=mesh['dp'=4,'seq'=16,'tensor'=2] {'dp','seq'}, dimensions={0}, use_global_device_ids=true | all-gather | bytes 10400 | tf_op jit(solution)/shard_map/all_gather | solution.py:119
  179.0 56.0 %all-gather.11.cloned.1.call-done = bf16[2560,2,256]{2,0,1:T(8,128)(2,1)} async-done(((bf16[160,2,256]{2,0,1:T(8,128)(2,1)}), bf16[2560,2,256]{2,0,1:T(8,128)(2,1)}) %all-gather.11.cloned.1.call-update) | async-done | bytes 2621456 | tf_op jit(solution)/shard_map/all_gather | solution.py:137
  243.5 67.5 %all-gather.15.cloned.1.call-done = bf16[1280,2560]{0,1:T(8,128)(2,1)} async-done(((bf16[1280,40]{0,1:T(8,128)(2,1)}), bf16[1280,2560]{0,1:T(8,128)(2,1)}) %all-gather.15.cloned.1.call-update) | async-done | bytes 6553616 | tf_op jit(solution)/shard_map/all_gather | solution.py:116
  311.0 6.1 convolution_convert_fusion
  320.5 21.6 all-reduce.10.cloned.1.call-done
  343.6 183.2 %all-gather.17.cloned.1.call-done = bf16[2560,2,3840]{2,0,1:T(8,128)(2,1)} async-done(((bf16[40,2,3840]{2,0,1:T(8,128)(2,1)}), bf16[2560,2,3840]{2,0,1:T(8,128)(2,1)}) %all-gather.17.cloned.1.call-update) | async-done | bytes 39321616 | tf_op jit(solution)/shard_map/all_gather | solution.py:117
  526.8 18.1 fusion.89
  544.9 97.7 %all-gather.19.cloned.1.call-done = bf16[3840,2560]{0,1:T(8,128)(2,1)} async-done(((bf16[3840,40]{0,1:T(8,128)(2,1)}), bf16[3840,2560]{0,1:T(8,128)(2,1)}) %all-gather.19.cloned.1.call-update) | async-done | bytes 19660816 | tf_op jit(solution)/shard_map/all_gather | solution.py:118
  642.7 11.7 fusion.42
  654.3 20.3 fusion.13
  674.9 24.8 all-reduce.12.cloned.1.call-done
  719.8 11.5 convolution_convert_fusion.1
  731.3 62.0 %reduce-scatter.7.cloned.1.call-done = bf16[160,2,256]{2,0,1:T(8,128)(2,1)} async-done(((bf16[2560,2,256]{2,0,1:T(8,128)(2,1)}), bf16[160,2,256]{2,0,1:T(8,128)(2,1)}) %reduce-scatter.7.cloned.1.call-update) | async-done | bytes 163856 | tf_op jit(solution)/shard_map/reduce_scatter | solution.py:211
  796.7 23.8 all-reduce.14.cloned.1.call-done
  832.4 8.3 fusion.59
  840.8 6.7 fusion.131
  848.9 16.9 fusion.62
  867.1 28.5 %fusion.32 = f32[2560,2,3840]{2,0,1:T(8,128)} fusion(bf16[160,1,3840]{2,0,1:T(8,128)(2,1)} %get-tuple-element.111, bf16[160,1,3840]{2,0,1:T(8,128)(2,1)S(1)} %copy-done.28, f32[160,2560]{1,0:T(8,128)S(1)} %get-tuple-element.109, f32[2560]{0:T(1024)S(1)} %get-tuple-element.84, f32[160]{0:T(256)S(1)} %fusion.102), kind=kOutput, calls=%fused_computation.71 | convolution fusion | flops 6297600000 | bytes 82750080 | tf_op jit(solution)/shard_map/cd,cgf->dgf/dot_general | solution.py:170
  899.2 298.6 %all-reduce.3 = (f32[2560]{0:T(1024)S(1)}, f32[2560]{0:T(1024)S(1)}) all-reduce(f32[2560]{0:T(1024)S(1)} %get-tuple-element.82, f32[2560]{0:T(1024)S(1)} %get-tuple-element.80), channel_id=10, replica_groups=mesh['dp'=4,'seq'=16,'tensor'=2] {'dp','seq'}, use_global_device_ids=true, to_apply=%region_21.22.clone | all-reduce | flops 5120 | bytes 40960
  1203.8 52.1 %all-gather = bf16[40,512]{1,0:T(8,128)(2,1)S(1)} all-gather(bf16[40,256]{1,0:T(8,128)(2,1)S(1)} %convert_element_type.153), channel_id=2, replica_groups=mesh['dp'=4,'seq'=16,'tensor'=2] {'tensor'}, dimensions={1}, use_global_device_ids=true | all-gather | bytes 61440 | tf_op jit(solution)/shard_map/all_gather | solution.py:243
  1256.9 288.3 %reduce-scatter.13.cloned.1.call-done = f32[1280,40]{0,1:T(8,128)} async-done(((f32[1280,2560]{0,1:T(8,128)}), f32[1280,40]{0,1:T(8,128)}) %reduce-scatter.13.cloned.1.call-update) | async-done | bytes 204816 | tf_op jit(solution)/shard_map/reduce_scatter | solution.py:240
  1547.1 376.1 %reduce-scatter.9.cloned.1.call-done = f32[40,1280]{1,0:T(8,128)} async-done(((f32[2560,1280]{1,0:T(8,128)}), f32[40,1280]{1,0:T(8,128)}) %reduce-scatter.9.cloned.1.call-update) | async-done | bytes 204816 | tf_op jit(solution)/shard_map/reduce_scatter | solution.py:238
  1925.0 320.4 %reduce-scatter.17.cloned.1.call-done = f32[3840,40]{0,1:T(8,128)} async-done(((f32[3840,2560]{0,1:T(8,128)}), f32[3840,40]{0,1:T(8,128)}) %reduce-scatter.17.cloned.1.call-update) | async-done | bytes 614416 | tf_op jit(solution)/shard_map/reduce_scatter | solution.py:180
  2248.4 350.4 %reduce-scatter.15.cloned.1.call-done = f32[40,2,3840]{2,0,1:T(8,128)} async-done(((f32[2560,2,3840]{2,0,1:T(8,128)}), f32[40,2,3840]{2,0,1:T(8,128)}) %reduce-scatter.15.cloned.1.call-update) | async-done | bytes 1228816 | tf_op jit(solution)/shard_map/reduce_scatter | solution.py:181
  (219 shorter events, 97.1 us)
Async XLA Ops:
  7.2 156.1 %all-gather.9.cloned.1.call-start = ((), (), s32[]{:S(2)}) async-start(), calls=%async_computation.6 | async-start | bytes 2662400 | tf_op jit(solution)/shard_map/all_gather | solution.py:115
  8.9 159.7 %all-gather.13.cloned.1.call-start = ((), (), s32[]{:S(2)}) async-start(), calls=%async_computation.8 | async-start | bytes 6656000 | tf_op jit(solution)/shard_map/all_gather | solution.py:114
  10.6 224.4 %all-gather.11.cloned.1.call-start = ((), (), s32[]{:S(2)}) async-start(), calls=%async_computation.7 | async-start | bytes 2785280 | tf_op jit(solution)/shard_map/all_gather | solution.py:137
  167.3 143.7 %all-gather.15.cloned.1.call-start = ((), (), s32[]{:S(2)}) async-start(), calls=%async_computation.9 | async-start | bytes 6656000 | tf_op jit(solution)/shard_map/all_gather | solution.py:116
  168.0 174.1 %all-reduce.10.cloned.1.call-start = ((), (), s32[]{:S(2)}) async-start(), calls=%async_computation.10 | async-start | bytes 1638400 | tf_op jit(solution)/shard_map/psum | solution.py:157
  317.2 209.7 %all-gather.17.cloned.1.call-start = ((), (), s32[]{:S(2)}) async-start(), calls=%async_computation.11 | async-start | bytes 39936000 | tf_op jit(solution)/shard_map/all_gather | solution.py:117
  318.1 324.5 %all-gather.19.cloned.1.call-start = ((), (), s32[]{:S(2)}) async-start(), calls=%async_computation.12 | async-start | bytes 19968000 | tf_op jit(solution)/shard_map/all_gather | solution.py:118
  320.0 379.6 %all-reduce.12.cloned.1.call-start = ((), (), s32[]{:S(2)}) async-start(), calls=%async_computation.13 | async-start | bytes 1638400 | tf_op jit(solution)/shard_map/psum | solution.py:176
  674.6 118.7 %reduce-scatter.7.cloned.1.call-start = ((), (), s32[]{:S(2)}) async-start(), calls=%async_computation.14 | async-start | bytes 2785280 | tf_op jit(solution)/shard_map/reduce_scatter | solution.py:211
  718.6 101.9 %all-reduce.14.cloned.1.call-start = ((), (), s32[]{:S(2)}) async-start(), calls=%async_computation.15 | async-start | bytes 327680 | tf_op jit(solution)/shard_map/psum | solution.py:217
  793.3 104.1 %all-reduce.16.cloned.1.call-start = ((), (), s32[]{:S(2)}) async-start(), calls=%async_computation.21 | async-start | bytes 3276800 | tf_op jit(solution)/shard_map/psum | solution.py:164
  829.2 373.8 %reduce-scatter.11.cloned.1.call-start = ((), (), s32[]{:S(2)}) async-start(), calls=%async_computation.17 | async-start | bytes 2662400 | tf_op jit(solution)/shard_map/reduce_scatter | solution.py:239
  831.4 713.9 %reduce-scatter.13.cloned.1.call-start = ((), (), s32[]{:S(2)}) async-start(), calls=%async_computation.18 | async-start | bytes 13312000 | tf_op jit(solution)/shard_map/reduce_scatter | solution.py:240
  840.7 1082.4 %reduce-scatter.9.cloned.1.call-start = ((), (), s32[]{:S(2)}) async-start(), calls=%async_computation.16 | async-start | bytes 13312000 | tf_op jit(solution)/shard_map/reduce_scatter | solution.py:238
  847.5 1398.0 %reduce-scatter.17.cloned.1.call-start = ((), (), s32[]{:S(2)}) async-start(), calls=%async_computation.20 | async-start | bytes 39936000 | tf_op jit(solution)/shard_map/reduce_scatter | solution.py:180
  865.8 1732.9 %reduce-scatter.15.cloned.1.call-start = ((), (), s32[]{:S(2)}) async-start(), calls=%async_computation.19 | async-start | bytes 79872000 | tf_op jit(solution)/shard_map/reduce_scatter | solution.py:181
  1201.2 344.0 %copy-start.31 = (f32[1280,40]{0,1:T(8,128)S(1)}, f32[1280,40]{0,1:T(8,128)}, u32[]{:S(2)}) copy-start(f32[1280,40]{0,1:T(8,128)} %param.24) | copy-start | bytes 614404
  1201.2 344.0 %copy-start.34 = (f32[1280,40]{0,1:T(8,128)S(1)}, f32[1280,40]{0,1:T(8,128)}, u32[]{:S(2)}) copy-start(f32[1280,40]{0,1:T(8,128)} %param.30) | copy-start | bytes 614404
  1202.9 720.3 %copy-start.32 = (f32[40,1280]{1,0:T(8,128)S(1)}, f32[40,1280]{1,0:T(8,128)}, u32[]{:S(2)}) copy-start(f32[40,1280]{1,0:T(8,128)} %param.22) | copy-start | bytes 614404
  1202.9 720.3 %copy-start.36 = (f32[40,1280]{1,0:T(8,128)S(1)}, f32[40,1280]{1,0:T(8,128)}, u32[]{:S(2)}) copy-start(f32[40,1280]{1,0:T(8,128)} %param.28) | copy-start | bytes 614404
  1202.9 720.3 %copy-start.37 = (f32[40,1280]{1,0:T(8,128)S(1)}, f32[40,1280]{1,0:T(8,128)}, u32[]{:S(2)}) copy-start(f32[40,1280]{1,0:T(8,128)} %param.34) | copy-start | bytes 614404
  1202.9 1042.5 %copy-start.22 = (f32[3840,40]{0,1:T(8,128)S(1)}, f32[3840,40]{0,1:T(8,128)}, u32[]{:S(2)}) copy-start(f32[3840,40]{0,1:T(8,128)} %param.26) | copy-start | bytes 1843204
  1925.0 673.7 %copy-start.17 = (f32[40,2,3840]{2,1,0:T(2,128)S(1)}, f32[40,2,3840]{2,1,0:T(2,128)}, u32[]{:S(2)}) copy-start(f32[40,2,3840]{2,1,0:T(2,128)} %param.25) | copy-start | bytes 3686404
  1925.0 673.7 %copy-start.29 = (f32[40,2,3840]{2,1,0:T(2,128)S(1)}, f32[40,2,3840]{2,1,0:T(2,128)}, u32[]{:S(2)}) copy-start(f32[40,2,3840]{2,1,0:T(2,128)} %param.31) | copy-start | bytes 3686404
  (44 other events, 2280.3 us)
Sparse Core Ops, SparseCore 0:
  11.5 68.6 all-gather.8
  83.7 71.7 all-gather.12
  167.4 67.4 all-gather.10
  238.3 72.6 all-gather.14
  317.3 24.8 all-reduce.9
  345.4 181.3 all-gather.16
  530.2 112.4 all-gather.18
  674.8 24.8 all-reduce.11
  718.7 74.5 reduce-scatter.6
  795.6 24.8 all-reduce.13
  829.3 27.4 all-reduce.15
  859.1 305.9 reduce-scatter.10
  1167.5 377.7 reduce-scatter.12
  1547.5 375.5 reduce-scatter.8
  1928.1 317.3 reduce-scatter.16
  2251.2 347.5 reduce-scatter.14
where the time goes:
time: 2620 us; the launch traced here: 2610 us
  waiting for transfers between devices  1870 us (71%)
  blocking collectives  501 us (19%)
  matrix products  164 us (6%)
  other arithmetic  37 us (1%)
    reduce_scatter x1, waiting for transfers between devices, per_device(): lax.psum_scatter(grad_query_w, ('dp', 'seq'), scatter_dimension=0, tiled=...  376 us
    reduce_scatter x1, waiting for transfers between devices, per_device(): lax.psum_scatter(grad_gateup, ('dp', 'seq'), scatter_dimension=0, tiled=T...  350 us
    reduce_scatter x1, waiting for transfers between devices, per_device(): lax.psum_scatter(grad_down, ('dp', 'seq'), scatter_dimension=1, tiled=True)  320 us
    unnamed x1, blocking collectives  299 us
    reduce_scatter x1, waiting for transfers between devices, per_device(): lax.psum_scatter(grad_out, ('dp', 'seq'), scatter_dimension=1, tiled=True)  288 us
    all_gather x1, waiting for transfers between devices, per_device(): lax.all_gather(gateup_low_w, ('dp', 'seq'), axis=0, tiled=True)  183 us
    all_gather x1, blocking collectives, per_device(): lax.all_gather(scales_low_w, ('dp', 'seq'), axis=1, tiled=True)  150 us
    all_gather x1, waiting for transfers between devices, per_device(): lax.all_gather(down_low_w, ('dp', 'seq'), axis=1, tiled=True)  97.7 us
  transfers between devices with their start and end apart: 16, of which 12 were waited for; matrix products, arithmetic and copies ran while one was open for 5% of the time, Pallas kernels for 0%

commit v1 on v0

v1 whole, which is shorter than its diff:
```python
import functools

import jax
import jax.numpy as jnp
from jax import lax
from jax.experimental import pallas as pl
from jax.experimental.pallas import tpu as pltpu
from jax.sharding import Mesh
from jax.sharding import PartitionSpec as P

D = 2560
H = 10
HD = 256
FF = 7680
WINDOW = 2048
STEP = 10

eps_norm = 1e-06
masked_fill = -1e30
first_decay = 0.9
second_decay = 0.95
adam_eps = 1e-08
weight_decay = 0.1
gain_rate = 0.2

MESH = pl.DeviceIdType.MESH
LOW = jnp.bfloat16
F32 = jnp.float32
RING = 4
BLOCK = 160
HALF = BLOCK // 2
PART = 48
OWN = 40
PAD = 48
MAIN = 896
TAIL = 64


def step(axis, distance):
    return lax.rem(lax.axis_index(axis) + (RING + distance), RING)


def sibling():
    return {"tensor": 1 - lax.axis_index("tensor")}


def greet(peers):
    barrier = pltpu.get_barrier_semaphore()
    for peer in peers:
        pl.semaphore_signal(barrier, inc=1, device_id=peer, device_id_type=MESH)
    pl.semaphore_wait(barrier, len(peers))


class Sender:
    def __init__(self, send_sem, recv_sem):
        self.send_sem, self.recv_sem, self.count = send_sem, recv_sem, 0

    def copy(self, src, dst, peer):
        one = pltpu.make_async_remote_copy(
            src_ref=src,
            dst_ref=dst,
            send_sem=self.send_sem.at[self.count],
            recv_sem=self.recv_sem.at[self.count],
            device_id=peer,
            device_id_type=MESH,
        )
        self.count += 1
        one.start()
        return one


def comm_call(kernel, ident, copies, out_shape, out_spaces, scratch, *operands, in_spaces=None):
    in_spaces = in_spaces or [pl.ANY] * len(operands)
    return pl.pallas_call(
        kernel,
        out_shape=out_shape,
        in_specs=[pl.BlockSpec(memory_space=space) for space in in_spaces],
        out_specs=jax.tree.map(lambda space: pl.BlockSpec(memory_space=space), out_spaces),
        scratch_shapes=[
            pltpu.SemaphoreType.DMA((copies,)),
            pltpu.SemaphoreType.DMA((copies,)),
            pltpu.SemaphoreType.DMA((2,)),
            *scratch,
        ],
        compiler_params=pltpu.CompilerParams(
            collective_id=ident, has_side_effects=True, vmem_limit_bytes=48 * 1024 * 1024
        ),
    )(*operands)


def exchange_kernel(x_ref, o_ref, send_sem, recv_sem, local_sem):
    me = lax.axis_index("z")
    greet([{"z": step("z", d)} for d in (1, 2, 3)])
    sender = Sender(send_sem, recv_sem)
    copies = [
        sender.copy(x_ref.at[step("z", d)], o_ref.at[me], {"z": step("z", d)}) for d in (2, 1, 3)
    ]
    own = pltpu.make_async_copy(x_ref.at[me], o_ref.at[me], local_sem.at[0])
    own.start()
    own.wait()
    for copy in copies:
        copy.wait()


def exchange_z(x, ident):
    return comm_call(
        exchange_kernel, ident, 3, jax.ShapeDtypeStruct(x.shape, x.dtype), pl.ANY, [], x
    )


def swap_kernel(x_ref, o_ref, send_sem, recv_sem, local_sem):
    greet([sibling()])
    Sender(send_sem, recv_sem).copy(x_ref, o_ref, sibling()).wait()


def swap_cores(x, ident):
    return comm_call(swap_kernel, ident, 1, jax.ShapeDtypeStruct(x.shape, x.dtype), pl.ANY, [], x)


def gather_kernel(x_ref, o_ref, send_sem, recv_sem, local_sem):
    me, left, right, far = (step("z", d) for d in (0, -1, 1, 2))
    base = pl.multiple_of(lax.axis_index("tensor") * HALF, 16)
    half = pl.ds(base, HALF)
    first = pl.ds(base, PART)
    last = pl.ds(pl.multiple_of(base + PART, 16), HALF - PART)
    greet([{"z": left}, {"z": right}, sibling()])
    sender = Sender(send_sem, recv_sem)
    to_right = sender.copy(x_ref.at[half], o_ref.at[me, half], {"z": right})
    to_left = sender.copy(x_ref.at[half], o_ref.at[me, half], {"z": left})
    own = pltpu.make_async_copy(x_ref, o_ref.at[me], local_sem.at[0])
    own.start()
    to_right.wait_recv()
    on_right = sender.copy(o_ref.at[left, first], o_ref.at[left, first], {"z": right})
    share_left = sender.copy(o_ref.at[left, half], o_ref.at[left, half], sibling())
    to_left.wait_recv()
    on_left = sender.copy(o_ref.at[right, last], o_ref.at[right, last], {"z": left})
    share_right = sender.copy(o_ref.at[right, half], o_ref.at[right, half], sibling())
    on_right.wait_recv()
    on_left.wait_recv()
    share_far = sender.copy(o_ref.at[far, half], o_ref.at[far, half], sibling())
    own.wait()
    for copy in (share_left, share_right, share_far):
        copy.wait()
    for copy in (to_right, to_left, on_right, on_left):
        copy.wait_send()


def gather_z(x, ident):
    shape = jax.ShapeDtypeStruct((RING,) + x.shape, x.dtype)
    return comm_call(gather_kernel, ident, 7, shape, pl.ANY, [], x).reshape(-1, x.shape[1])


def reduce_kernel(
    p_ref, o_ref, send_sem, recv_sem, local_sem, other, total, part_a, part_b, from_left, from_right
):
    me, left, right, far = (step("z", d) for d in (0, -1, 1, 2))
    core = lax.axis_index("tensor")
    mine = pl.ds(pl.multiple_of(core * HALF, 16), HALF)
    theirs = pl.ds(pl.multiple_of((1 - core) * HALF, 16), HALF)
    greet([{"z": left}, {"z": right}, sibling()])
    sender = Sender(send_sem, recv_sem)
    shares = [
        sender.copy(p_ref.at[block, theirs], other.at[slot], sibling())
        for slot, block in enumerate((far, right, left, me))
    ]

    def both(slot, block):
        return p_ref[block, mine].astype(F32) + other[slot].astype(F32)

    shares[0].wait_recv()
    total[0] = both(0, far).astype(LOW)
    far_right = sender.copy(total.at[0, pl.ds(0, PART)], part_a, {"z": right})
    far_left = sender.copy(total.at[0, pl.ds(PART, HALF - PART)], part_b, {"z": left})
    shares[1].wait_recv()
    summed = both(1, right)
    far_right.wait_recv()
    total[1, :PART] = (summed[:PART] + part_a[...].astype(F32)).astype(LOW)
    total[1, PART:] = summed[PART:].astype(LOW)
    to_right = sender.copy(total.at[1], from_left, {"z": right})
    shares[2].wait_recv()
    summed = both(2, left)
    far_left.wait_recv()
    total[2, :PART] = summed[:PART].astype(LOW)
    total[2, PART:] = (summed[PART:] + part_b[...].astype(F32)).astype(LOW)
    to_left = sender.copy(total.at[2], from_right, {"z": left})
    shares[3].wait_recv()
    to_right.wait_recv()
    to_left.wait_recv()
    o_ref[mine, :] = both(3, me) + from_left[...].astype(F32) + from_right[...].astype(F32)
    share = sender.copy(o_ref.at[mine], o_ref.at[mine], sibling())
    share.wait()
    for copy in (*shares, far_right, far_left, to_right, to_left):
        copy.wait_send()


def reduce_z(x, ident):
    columns = x.shape[1]
    return comm_call(
        reduce_kernel,
        ident,
        9,
        jax.ShapeDtypeStruct((BLOCK, columns), F32),
        pltpu.VMEM,
        [
            pltpu.VMEM((4, HALF, columns), LOW),
            pltpu.VMEM((3, HALF, columns), LOW),
            pltpu.VMEM((PART, columns), LOW),
            pltpu.VMEM((HALF - PART, columns), LOW),
            pltpu.VMEM((HALF, columns), LOW),
            pltpu.VMEM((HALF, columns), LOW),
        ],
        x.reshape(RING, BLOCK, columns),
        in_spaces=[pltpu.VMEM],
    )


def plane_peers(axes):
    return [{axis: step(axis, d)} for axis in axes for d in (-1, 1)]


def plane_gather_kernel(axes, share, x_ref, o_ref, send_sem, recv_sem, local_sem):
    out = o_ref.at[lax.axis_index("tensor")] if share else o_ref
    a, b = (lax.axis_index(axis) for axis in axes)
    greet(plane_peers(axes) + ([sibling()] if share else []))
    sender = Sender(send_sem, recv_sem)
    own = pltpu.make_async_copy(x_ref, out.at[a, b], local_sem.at[0])
    own.start()
    waits = []
    state = []
    for which, axis in enumerate(axes):
        rows = pl.ds(which * HALF, HALF)
        place = (lambda i, r: out.at[i, b, r]) if which == 0 else (lambda i, r: out.at[a, i, r])
        me = (a, b)[which]
        to_right = sender.copy(x_ref.at[rows], place(me, rows), {axis: step(axis, 1)})
        to_left = sender.copy(x_ref.at[rows], place(me, rows), {axis: step(axis, -1)})
        state.append((axis, which, place, to_right, to_left))
        waits += [to_right, to_left]
    passed = []
    for axis, which, place, to_right, to_left in state:
        first = pl.ds(which * HALF, PART)
        last = pl.ds(which * HALF + PART, HALF - PART)
        left, right = step(axis, -1), step(axis, 1)
        to_right.wait_recv()
        on_right = sender.copy(place(left, first), place(left, first), {axis: right})
        to_left.wait_recv()
        on_left = sender.copy(place(right, last), place(right, last), {axis: left})
        passed.append((on_right, on_left))
        waits += [on_right, on_left]
    own.wait()
    state = []
    for which, axis in enumerate(axes):
        other = axes[1 - which]
        rows = pl.ds(which * HALF, HALF)
        if which == 0:
            place = lambda i, lo, n, rows=rows: out.at[pl.ds(lo, n), i, rows]
        else:
            place = lambda i, lo, n, rows=rows: out.at[i, pl.ds(lo, n), rows]
        me = (b, a)[which]
        for copy in passed[which]:
            copy.wait_recv()
        to_right = sender.copy(place(me, 0, 4), place(me, 0, 4), {other: step(other, 1)})
        to_left = sender.copy(place(me, 0, 4), place(me, 0, 4), {other: step(other, -1)})
        state.append((other, place, to_right, to_left))
        waits += [to_right, to_left]
    ends = []
    for other, place, to_right, to_left in state:
        left, right = step(other, -1), step(other, 1)
        to_right.wait_recv()
        on_right = sender.copy(place(left, 0, 2), place(left, 0, 2), {other: right})
        to_left.wait_recv()
        on_left = sender.copy(place(right, 2, 2), place(right, 2, 2), {other: left})
        ends += [on_right, on_left]
    for copy in ends:
        copy.wait_recv()
    if share:
        last = sender.copy(out, out, sibling())
        last.wait()
    for copy in waits + ends:
        copy.wait_send()


def gather_plane(x, axes, ident, share=False):
    shape = ((2,) if share else ()) + (RING, RING) + x.shape
    return comm_call(
        functools.partial(plane_gather_kernel, axes, share),
        ident,
        17,
        jax.ShapeDtypeStruct(shape, x.dtype),
        pl.ANY,
        [],
        x,
    )


def plane_reduce_kernel(
    axes, g_ref, o_ref, send_sem, recv_sem, local_sem, far_one, side_one, sum_one, far_two, side_two
):
    place_a, place_b = (lax.axis_index(axis) for axis in axes)
    greet(plane_peers(axes))
    sender = Sender(send_sem, recv_sem)
    copies = []

    def start(*args):
        copies.append(sender.copy(*args))
        return copies[-1]

    def block(which, i, lo, n):
        rows = pl.ds(which * HALF, HALF)
        return g_ref.at[i, pl.ds(lo, n), rows] if which == 0 else g_ref.at[pl.ds(lo, n), i, rows]

    first = []
    for which, axis in enumerate(axes):
        far, right, left = step(axis, 2), {axis: step(axis, 1)}, {axis: step(axis, -1)}
        first.append(
            (
                start(block(which, far, 0, 2), far_one.at[which, 0], right),
                start(block(which, far, 2, 2), far_one.at[which, 1], left),
            )
        )
    sides = []
    for which, axis in enumerate(axes):
        right, left = step(axis, 1), step(axis, -1)
        plain_right = start(block(which, right, 2, 2), side_one.at[which, 0, pl.ds(2, 2)], {axis: right})
        plain_left = start(block(which, left, 0, 2), side_one.at[which, 1, pl.ds(0, 2)], {axis: left})
        sides.append([plain_right, plain_left])
    for which, axis in enumerate(axes):
        right, left = step(axis, 1), step(axis, -1)
        first[which][0].wait_recv()
        sum_one[which, 0] = (
            block(which, right, 0, 2)[...].astype(F32) + far_one[which, 0].astype(F32)
        ).astype(LOW)
        sides[which].append(
            start(sum_one.at[which, 0], side_one.at[which, 0, pl.ds(0, 2)], {axis: right})
        )
        first[which][1].wait_recv()
        sum_one[which, 1] = (
            block(which, left, 2, 2)[...].astype(F32) + far_one[which, 1].astype(F32)
        ).astype(LOW)
        sides[which].append(
            start(sum_one.at[which, 1], side_one.at[which, 1, pl.ds(2, 2)], {axis: left})
        )
    second = []
    own = []

    def summed(which, i):
        me = (place_a, place_b)[which]
        rows = pl.ds(which * HALF, HALF)
        ref = g_ref.at[me, i, rows] if which == 0 else g_ref.at[i, me, rows]
        return (
            ref[...].astype(F32)
            + side_one[which, 0, i].astype(F32)
            + side_one[which, 1, i].astype(F32)
        )

    for which, axis in enumerate(axes):
        other = axes[1 - which]
        right, left = {other: step(other, 1)}, {other: step(other, -1)}
        for copy in sides[which]:
            copy.wait_recv()
        far_two[which, 0] = summed(which, step(other, 2)).astype(LOW)
        second.append(
            (
                start(far_two.at[which, 0, pl.ds(0, PART)], far_two.at[which, 1, pl.ds(0, PART)], right),
                start(
                    far_two.at[which, 0, pl.ds(PART, HALF - PART)],
                    far_two.at[which, 1, pl.ds(PART, HALF - PART)],
                    left,
                ),
            )
        )
    last = []
    for which, axis in enumerate(axes):
        other = axes[1 - which]
        right, left = step(other, 1), step(other, -1)
        total = summed(which, right)
        second[which][0].wait_recv()
        side_two[which, 0, :PART] = (
            total[:PART] + far_two[which, 1, :PART].astype(F32)
        ).astype(LOW)
        side_two[which, 0, PART:] = total[PART:].astype(LOW)
        last.append(start(side_two.at[which, 0], side_two.at[which, 2], {other: right}))
        total = summed(which, left)
        second[which][1].wait_recv()
        side_two[which, 1, :PART] = total[:PART].astype(LOW)
        side_two[which, 1, PART:] = (
            total[PART:] + far_two[which, 1, PART:].astype(F32)
        ).astype(LOW)
        last.append(start(side_two.at[which, 1], side_two.at[which, 3], {other: left}))
    for which, axis in enumerate(axes):
        other = axes[1 - which]
        last[2 * which].wait_recv()
        last[2 * which + 1].wait_recv()
        o_ref[which * HALF : (which + 1) * HALF] = (
            summed(which, lax.axis_index(other))
            + side_two[which, 2].astype(F32)
            + side_two[which, 3].astype(F32)
        )
    for copy in copies:
        copy.wait_send()


def reduce_plane(x, axes, ident):
    columns = x.shape[1]
    return comm_call(
        functools.partial(plane_reduce_kernel, axes),
        ident,
        20,
        jax.ShapeDtypeStruct((BLOCK, columns), F32),
        pltpu.VMEM,
        [
            pltpu.VMEM((2, 2, 2, HALF, columns), LOW),
            pltpu.VMEM((2, 2, 4, HALF, columns), LOW),
            pltpu.VMEM((2, 2, 2, HALF, columns), LOW),
            pltpu.VMEM((2, 2, HALF, columns), LOW),
            pltpu.VMEM((2, 4, HALF, columns), LOW),
        ],
        x.reshape(RING, RING, BLOCK, columns),
        in_spaces=[pltpu.VMEM],
    )


def rotate(values, positions, direction):
    quarter = values.shape[-1] // 4
    frequency = 10000.0 ** (-jnp.arange(quarter, dtype=F32) / quarter)
    angles = positions.astype(F32)[:, None] * frequency[None, :]
    table_shape = (angles.shape[0],) + (1,) * (values.ndim - 2) + (quarter,)
    cos_table = jnp.cos(angles).reshape(table_shape)
    sin_table = direction * jnp.sin(angles).reshape(table_shape)
    lower_part = values[..., :quarter]
    upper_part = values[..., quarter : 2 * quarter]
    kept_part = values[..., 2 * quarter :]
    return jnp.concatenate(
        [
            lower_part * cos_table - upper_part * sin_table,
            upper_part * cos_table + lower_part * sin_table,
            kept_part,
        ],
        axis=-1,
    )


def inverse_rms(values):
    return lax.rsqrt(jnp.mean(values * values, axis=-1, keepdims=True) + eps_norm)


def rms_back(grad, gain, unit, inverse):
    scaled = grad * gain
    return inverse * (scaled - unit * jnp.mean(scaled * unit, axis=-1, keepdims=True))


def adam_update(weight, gradient, first_moment, second_moment, learn_rate, decay_rate):
    first_moment = first_decay * first_moment + (1.0 - first_decay) * gradient
    second_moment = second_decay * second_moment + (1.0 - second_decay) * gradient * gradient
    corrected = (
        first_moment
        / (1.0 - first_decay**STEP)
        / (jnp.sqrt(second_moment / (1.0 - second_decay**STEP)) + adam_eps)
    )
    return (weight - learn_rate * (corrected + decay_rate * weight), first_moment, second_moment)


def out_fan_in(seq_length):
    return max(1, H * HD * 4 // min(WINDOW, seq_length))


def dot(left_side, right_side, contract):
    return lax.dot_general(
        left_side, right_side, ((contract[:1], contract[1:]), ((), ())), preferred_element_type=F32
    )


def activate(gate_part, upper_part):
    return jax.nn.gelu(gate_part, approximate=True) * upper_part


def quarters(rows):
    return rows.reshape(OWN, RING, -1).transpose(1, 0, 2)


def whole(slices):
    return slices.transpose(1, 0, 2).reshape(slices.shape[1], -1)


def pad_to(x, axis, size):
    widths = [(0, 0)] * x.ndim
    widths[axis] = (0, size - x.shape[axis])
    return jnp.pad(x, widths)


def per_device(
    tokens,
    cotangent,
    w_query,
    w_keyvalue,
    w_out,
    w_gateup,
    w_down,
    norm_scales,
    first_query,
    first_keyvalue,
    first_out,
    first_gateup,
    first_down,
    first_scales,
    second_query,
    second_keyvalue,
    second_out,
    second_gateup,
    second_down,
    second_scales,
):
    core = lax.axis_index("tensor")
    seq_index = lax.axis_index("x") * RING + lax.axis_index("z")
    positions = seq_index * BLOCK + jnp.arange(BLOCK, dtype=jnp.int32)
    seq_length = BLOCK * RING * RING
    head_count = H // 2

    keyvalue_part = lax.dynamic_index_in_dim(w_keyvalue, core, 1, keepdims=False)
    scale_columns = jnp.broadcast_to(norm_scales.T[None], (RING, OWN, 2))
    attn_rows = jnp.concatenate(
        [quarters(w_query), quarters(keyvalue_part), quarters(w_out.T), scale_columns], axis=2
    ).astype(LOW)
    attn_rows = pad_to(pad_to(attn_rows, 2, 768), 1, PAD)
    gateup = w_gateup.astype(LOW).reshape(OWN, 2, RING, MAIN + TAIL).transpose(2, 0, 1, 3)
    feed_rows = jnp.concatenate(
        [
            gateup[..., :MAIN].reshape(RING, OWN, 2 * MAIN),
            gateup[..., MAIN:].reshape(RING, OWN, 2 * TAIL),
            quarters(w_down.T).astype(LOW),
        ],
        axis=2,
    )
    feed_rows = pad_to(pad_to(feed_rows, 2, 2944), 1, PAD)
    attn_mine = exchange_z(attn_rows, 1)[:, :OWN].reshape(BLOCK, 768)
    feed_mine = exchange_z(feed_rows, 2)[:, :OWN].reshape(BLOCK, 2944)
    feed_full = lax.all_gather(feed_mine, ("dp", "x"), axis=0, tiled=True)
    attn_full = gather_plane(attn_mine, ("dp", "x"), 3).reshape(D, 768)
    gateup_full = feed_full[:, : 2 * (MAIN + TAIL)]
    down_full = feed_full[:, 2 * (MAIN + TAIL) : 3 * (MAIN + TAIL)]
    qkv_full = attn_full[:, :384]
    out_full = attn_full[:, 384:704]
    gains = 1.0 + attn_full[:, 704:706].astype(F32).T
    gain_one, gain_two = gains[0], gains[1]

    inverse_one = inverse_rms(tokens)
    unit_one = tokens * inverse_one
    unit_all = gather_z(unit_one.astype(LOW), 4)
    dy_all = gather_z(cotangent.astype(LOW), 5)
    normed_one = (unit_all.astype(F32) * gain_one).astype(LOW)
    qkv_slice = dot(normed_one, qkv_full, (1, 0)).astype(LOW).reshape(RING, BLOCK, 384)
    qkv = exchange_z(qkv_slice, 6).astype(F32)
    query_raw = whole(qkv[..., :320]).reshape(BLOCK, head_count, HD)
    query_low = (rotate(query_raw, positions, 1.0) * HD ** (-0.5)).astype(LOW)
    keyvalue_raw = whole(qkv[..., 320:])
    keyvalue_low = jnp.where(
        core == 0, rotate(keyvalue_raw, positions, 1.0), keyvalue_raw
    ).astype(LOW)
    keyvalue_all = gather_plane(keyvalue_low, ("x", "z"), 7, share=True).reshape(2, seq_length, HD)
    key_rows, value_rows = keyvalue_all[0], keyvalue_all[1]
    key_pos = jnp.arange(seq_length, dtype=jnp.int32)
    distance = positions[:, None] - key_pos[None, :]
    visible = (distance >= 0) & (distance < WINDOW)
    scores = jnp.einsum("chd,kd->hck", query_low, key_rows, preferred_element_type=F32)
    scores = jnp.where(visible[None], scores, masked_fill)
    maximum = jnp.max(scores, axis=-1, keepdims=True)
    exponent = jnp.exp(scores - maximum)
    row_total = jnp.sum(exponent, axis=-1, keepdims=True)
    log_total = maximum + jnp.log(row_total)
    prob_low = (exponent / row_total).astype(LOW)
    attended = jnp.einsum("hck,kd->chd", prob_low, value_rows, preferred_element_type=F32)
    attended_low = attended.reshape(BLOCK, RING, 320).astype(LOW).transpose(1, 0, 2)
    attended_slice = exchange_z(attended_low, 8).reshape(-1, 320)
    out_part = dot(attended_slice, out_full, (1, 1)).astype(LOW)
    residual = tokens + reduce_z(out_part, 9)
    inverse_two = inverse_rms(residual)
    unit_two = residual * inverse_two
    normed_two = gather_z((unit_two * gain_two).astype(LOW), 10)

    gateup = dot(normed_two, gateup_full, (1, 0))
    gate = jnp.concatenate([gateup[:, :MAIN], gateup[:, 2 * MAIN : 2 * MAIN + TAIL]], axis=1)
    upper = jnp.concatenate([gateup[:, MAIN : 2 * MAIN], gateup[:, 2 * MAIN + TAIL :]], axis=1)
    hidden, activate_back = jax.vjp(activate, gate, upper)
    hidden_low = hidden.astype(LOW)
    grad_down = dot(dy_all, hidden_low, (0, 0)).astype(LOW)
    down_sum = lax.psum_scatter(grad_down, ("dp", "x"), scatter_dimension=0, tiled=True)
    grad_hidden = dot(dy_all, down_full, (1, 0))
    grad_gate, grad_upper = activate_back(grad_hidden)
    grad_gateup_low = jnp.concatenate(
        [grad_gate[:, :MAIN], grad_upper[:, :MAIN], grad_gate[:, MAIN:], grad_upper[:, MAIN:]], axis=1
    ).astype(LOW)
    norm_part_two = dot(grad_gateup_low, gateup_full, (1, 1)).astype(LOW)
    grad_gateup = dot(normed_two, grad_gateup_low, (0, 0)).astype(LOW)
    gateup_sum = lax.psum_scatter(grad_gateup, ("dp", "x"), scatter_dimension=0, tiled=True)
    normed_grad_two = reduce_z(norm_part_two, 11)
    feed_part = dot(hidden_low, down_full, (1, 1)).astype(LOW)
    output = residual + reduce_z(feed_part, 12)
    grad_scale_two = jnp.sum(normed_grad_two * unit_two, axis=0)
    grad_residual = cotangent + rms_back(normed_grad_two, gain_two, unit_two, inverse_two)

    grad_attn = gather_z(grad_residual.astype(LOW), 13)
    grad_out = dot(grad_attn, attended_slice, (0, 0)).astype(LOW)
    grad_att_slice = dot(grad_attn, out_full, (1, 0)).astype(LOW).reshape(RING, BLOCK, 320)
    grad_att_low = whole(exchange_z(grad_att_slice, 14)).reshape(BLOCK, head_count, HD)
    scores = jnp.einsum("chd,kd->hck", query_low, key_rows, preferred_element_type=F32)
    probs = jnp.where(visible[None], jnp.exp(scores - log_total), 0.0)
    prob_low = probs.astype(LOW)
    grad_probs = jnp.einsum("chd,kd->hck", grad_att_low, value_rows, preferred_element_type=F32)
    delta = jnp.sum(probs * grad_probs, axis=-1, keepdims=True)
    grad_scores_low = (probs * (grad_probs - delta)).astype(LOW)
    grad_query = jnp.einsum("hck,kd->chd", grad_scores_low, key_rows, preferred_element_type=F32)
    grad_keys = jnp.einsum("hck,chd->kd", grad_scores_low, query_low, preferred_element_type=F32)
    grad_values = jnp.einsum("hck,chd->kd", prob_low, grad_att_low, preferred_element_type=F32)
    pair = jnp.stack([grad_keys, grad_values]).astype(LOW)
    mine = lax.dynamic_index_in_dim(pair, core, 0, keepdims=False)
    theirs = swap_cores(lax.dynamic_index_in_dim(pair, 1 - core, 0, keepdims=False), 15)
    both = (mine.astype(F32) + theirs.astype(F32)).astype(LOW)
    grad_kv = reduce_plane(both, ("x", "z"), 16)
    grad_kv_low = jnp.where(core == 0, rotate(grad_kv, positions, -1.0), grad_kv).astype(LOW)
    grad_query_low = rotate(grad_query * HD ** (-0.5), positions, -1.0).astype(LOW)
    grad_qkv = jnp.concatenate(
        [grad_query_low.reshape(BLOCK, RING, 320), grad_kv_low.reshape(BLOCK, RING, 64)], axis=2
    ).transpose(1, 0, 2)
    grad_qkv_slice = exchange_z(grad_qkv, 17).reshape(-1, 384)
    norm_part_one = dot(grad_qkv_slice, qkv_full, (1, 1)).astype(LOW)
    normed_grad_one = reduce_z(norm_part_one, 18)
    grad_qkv_w = dot(normed_one, grad_qkv_slice, (0, 0)).astype(LOW)
    grad_scale_one = jnp.sum(normed_grad_one * unit_one, axis=0)
    grad_tokens = grad_residual + rms_back(normed_grad_one, gain_one, unit_one, inverse_one)

    grad_scales = jnp.stack([grad_scale_one, grad_scale_two], axis=1).astype(LOW)
    attn_grads = jnp.concatenate([grad_qkv_w, grad_out, pad_to(grad_scales, 1, 64)], axis=1)
    attn_sum = reduce_plane(attn_grads, ("dp", "x"), 19).astype(LOW)

    def to_owners(rows, ident):
        rows = pad_to(rows.reshape(RING, OWN, -1), 1, PAD)
        return exchange_z(rows, ident)[:, :OWN].astype(F32)

    down_shard = whole(to_owners(down_sum, 20)).T
    gateup_shard = to_owners(gateup_sum, 21)
    gateup_shard = jnp.concatenate(
        [
            gateup_shard[..., : 2 * MAIN].reshape(RING, OWN, 2, MAIN),
            gateup_shard[..., 2 * MAIN :].reshape(RING, OWN, 2, TAIL),
        ],
        axis=3,
    ).transpose(1, 2, 0, 3).reshape(OWN, 2, -1)
    attn_shard = to_owners(attn_sum, 22)
    query_shard = whole(attn_shard[..., :320])
    kv_half = whole(attn_shard[..., 320:384])
    out_shard = whole(attn_shard[..., 384:704]).T
    scale_grads = jnp.sum(attn_shard[..., 704:706], axis=0).T
    kv_other = swap_cores(pad_to(kv_half, 0, PAD).astype(LOW), 23)[:OWN].astype(F32)
    keyvalue_shard = jnp.stack(
        [jnp.where(core == 0, kv_half, kv_other), jnp.where(core == 0, kv_other, kv_half)], axis=1
    )

    matrix_rate = 2.0 * D ** (-0.5)
    out_rate = 2.0 * out_fan_in(seq_length) ** (-0.5)
    down_rate = 2.0 * (FF // 2) ** (-0.5)
    triples = [
        adam_update(w_query, query_shard, first_query, second_query, matrix_rate, weight_decay),
        adam_update(
            w_keyvalue, keyvalue_shard, first_keyvalue, second_keyvalue, matrix_rate, weight_decay
        ),
        adam_update(w_out, out_shard, first_out, second_out, out_rate, weight_decay),
        adam_update(w_gateup, gateup_shard, first_gateup, second_gateup, matrix_rate, weight_decay),
        adam_update(w_down, down_shard, first_down, second_down, down_rate, weight_decay),
        adam_update(norm_scales, scale_grads, first_scales, second_scales, gain_rate, 0.0),
    ]
    return (output, grad_tokens, *(triple[i] for i in range(3) for triple in triples))


def solution(mesh):
    split = Mesh(
        mesh.devices.reshape(RING, RING, RING, 2), ("dp", "x", "z", "tensor")
    )
    rows = ("dp", "x", "z")
    matrices = (
        P(rows, "tensor"),
        P(rows, None, None),
        P("tensor", rows),
        P(rows, None, "tensor"),
        P("tensor", rows),
        P(None, rows),
    )
    in_specs = (P(rows, None), P(rows, None), *matrices, *matrices, *matrices)
    out_specs = in_specs
    return jax.shard_map(
        per_device, mesh=split, in_specs=in_specs, out_specs=out_specs, check_vma=False
    )
```

time: 2620 us -> 621 us (0.24)
  waiting for transfers between devices: 1870 us -> 0.05 us
  blocking collectives: 501 us -> 0 us
  Pallas kernels: 0 us -> 398 us
  matrix products: 164 us -> 83.9 us
  local copies, waits for them, and re-layouts: 21.7 us -> 79.1 us
    reduce_scatter x6 -> x2, waiting for transfers between devices: 1400 us -> 0.01 us  [the longest x1 0.01 us: per_device(): lax.psum_scatter(grad_down, ('dp', 'x'), scatter_dimension=0, tiled=True)]
    all_gather x6 -> x1, waiting for transfers between devices: 404 us -> 0.01 us  [per_device(): feed_full = lax.all_gather(feed_mine, ('dp', 'x'), axis=0, tiled=True)]
    pallas_call x0 -> x23, Pallas kernels: none -> 398 us  [comm_call(): pl.pallas_call(kernel, out_shape=out_shape, in_specs=[pl.BlockSpec(memory...]
    unnamed x1 -> x0, blocking collectives: 299 us -> none
    all_gather x2 -> x0, blocking collectives: 202 us -> none  [the longest x1 150 us: per_device(): lax.all_gather(scales_low_w, ('dp', 'seq'), axis=1, tiled=True)]
    dot_general x17 -> x14, matrix products: 155 us -> 70.6 us  [the longest x12 66.4 us: dot(): lax.dot_general(left_side, right_side, ((contract[:1], contract[1:]), (()...]
    psum x4 -> x0, waiting for transfers between devices: 70.2 us -> none  [the longest x1 24.8 us: per_device(): lax.psum(norm_part_two.astype(jnp.bfloat16), 'tensor').astype(jnp.float32)]
  transfers between devices with their start and end apart: 16 -> 3, of which waited for: 12 -> 0; matrix products, arithmetic and copies ran while one was open for 5% -> 21% of each run, Pallas kernels for 0% -> 60%
where the time goes in v1:
time: 621 us; the launch traced here: 616 us
  Pallas kernels  398 us (64%)
  matrix products  83.9 us (14%)
  local copies, waits for them, and re-layouts  79.1 us (13%)
  other arithmetic  38.9 us (6%)
  between operations  15.6 us (3%)
    pallas_call x23, Pallas kernels, comm_call(): pl.pallas_call(kernel, out_shape=out_shape, in_specs=[pl.BlockSpec(memory...  398 us
    dot_general x12, matrix products, dot(): lax.dot_general(left_side, right_side, ((contract[:1], contract[1:]), (()...  66.4 us
    unnamed x132, local copies, waits for them, and re-layouts  35.2 us
    sub x6, other arithmetic, adam_update(): weight - learn_rate * (corrected + decay_rate * weight)  15 us
  transfers between devices with their start and end apart: 3, of which 0 were waited for; matrix products, arithmetic and copies ran while one was open for 21% of the time, Pallas kernels for 60%

profile of v1, /device:TPU:1, one launch (start us, length us, event | category | flops | bytes accessed | tf_op | source)
XLA Modules:
  0.0 615.5 jit_solution(8454946884495401601)
XLA Ops:
  12.1 17.6 %shard_map.355 = bf16[4,48,2944]{2,1,0:T(8,128)(2,1)S(1)} custom-call(bf16[4,48,2944]{2,1,0:T(8,128)(2,1)S(1)} %pad.39.x_ref), custom_call_target="tpu_custom_call" | custom-call | tf_op jit(solution)/shard_map/pallas_call | solution.py:74
  38.1 40.5 %shard_map.349 = bf16[4,4,160,768]{3,2,1,0:T(8,128)(2,1)S(1)} custom-call(bf16[160,768]{1,0:T(8,128)(2,1)S(1)} %bitcast.221), custom_call_target="tpu_custom_call" | custom-call | tf_op jit(solution)/shard_map/pallas_call | solution.py:74
  81.6 23.7 %shard_map.347 = bf16[4,160,2560]{2,1,0:T(8,128)(2,1)S(1)} custom-call(bf16[160,2560]{1,0:T(8,128)(2,1)S(1)} %multiply_convert_fusion.4.x_ref), custom_call_target="tpu_custom_call" | custom-call | tf_op jit(solution)/shard_map/pallas_call | solution.py:74
  110.7 9.9 %shard_map.350 = bf16[4,160,384]{2,1,0:T(8,128)(2,1)S(1)} custom-call(bf16[4,160,384]{2,1,0:T(8,128)(2,1)S(1)} %bitcast.224), custom_call_target="tpu_custom_call" | custom-call | tf_op jit(solution)/shard_map/pallas_call | solution.py:74
  122.7 29.1 %shard_map.351 = bf16[2,4,4,160,256]{4,3,2,1,0:T(8,128)(2,1)S(1)} custom-call(bf16[160,256]{1,0:T(8,128)(2,1)S(1)} %fusion.93.x_ref), custom_call_target="tpu_custom_call" | custom-call | tf_op jit(solution)/shard_map/pallas_call | solution.py:74
  168.8 9.0 %shard_map.352 = bf16[4,160,320]{2,1,0:T(8,128)(2,1)S(1)} custom-call(bf16[4,160,320]{2,1,0:T(8,128)(2,1)S(1)} %bitcast.219), custom_call_target="tpu_custom_call" | custom-call | tf_op jit(solution)/shard_map/pallas_call | solution.py:74
  181.5 24.3 %shard_map.353 = f32[160,2560]{1,0:T(8,128)S(1)} custom-call(bf16[4,160,2560]{2,1,0:T(8,128)(2,1)S(1)} %bitcast.212), custom_call_target="tpu_custom_call" | custom-call | tf_op jit(solution)/shard_map/pallas_call | solution.py:74
  206.3 21.5 %shard_map.354 = bf16[4,160,2560]{2,1,0:T(8,128)(2,1)S(1)} custom-call(bf16[160,2560]{1,0:T(8,128)(2,1)S(1)} %multiply_convert_fusion.3.x_ref), custom_call_target="tpu_custom_call" | custom-call | tf_op jit(solution)/shard_map/pallas_call | solution.py:74
  227.9 20.4 %shard_map.357 = bf16[4,160,2560]{2,1,0:T(8,128)(2,1)S(1)} custom-call(bf16[160,2560]{1,0:T(8,128)(2,1)S(1)} %convert_element_type.196.x_ref), custom_call_target="tpu_custom_call" | custom-call | tf_op jit(solution)/shard_map/pallas_call | solution.py:74
  250.1 9.7 %fusion.2 = f32[640,1920]{1,0:T(8,128)S(1)} fusion(bf16[640,2560]{1,0:T(8,128)(2,1)S(1)} %bitcast.214, bf16[2560,2944]{1,0:T(8,128)(2,1)} %all-gather.2.cloned.1.call-done), kind=kOutput, calls=%fused_computation.3 | convolution fusion | flops 6291456000 | bytes 18022400 | tf_op jit(solution)/shard_map/dot_general | solution.py:467
  261.9 8.8 %fusion.44 = (bf16[640,960]{1,0:T(8,128)(2,1)}, bf16[640,960]{1,0:T(8,128)(2,1)}, bf16[640,960]{1,0:T(8,128)(2,1)S(1)}) fusion(f32[640,64]{1,0:T(8,128)S(1)} %get-tuple-element.133, f32[640,896]{1,0:T(8,128)S(1)} %get-tuple-element.131, f32[640,64]{1,0:T(8,128)S(1)} %get-tuple-element.134, f32[640,896]{1,0:T(8,128)S(1)} %get-tuple-element.132, ...), kind=kOutput, calls=%fused_computation.66 | convolution fusion | flops 3162931200 | bytes 17121280 | tf_op jit(solution)/shard_map/dot_general | solution.py:467
  277.6 7.9 %copy.194 = bf16[2560,960]{1,0:T(8,128)(2,1)} copy(bf16[2560,960]{0,1:T(8,128)(2,1)} %fusion.13) | data formatting | bytes 9830400
  295.8 12.4 %convolution_convert_fusion = bf16[2560,1920]{1,0:T(8,128)(2,1)} fusion(bf16[640,2560]{1,0:T(8,128)(2,1)S(1)} %bitcast.215, bf16[640,1920]{1,0:T(8,128)(2,1)} %concatenate.45), kind=kOutput, calls=%fused_computation | convolution fusion | flops 6296371200 | bytes 15564800 | tf_op jit(solution)/shard_map/dot_general | solution.py:467
  309.9 9.7 %fusion.14 = bf16[640,2560]{1,0:T(8,128)(2,1)S(1)} fusion(bf16[640,1920]{1,0:T(8,128)(2,1)S(1)} %copy-done.31, bf16[2560,2944]{1,0:T(8,128)(2,1)} %all-gather.2.cloned.1.call-done), kind=kOutput, calls=%fused_computation.24 | convolution fusion | flops 6293094400 | bytes 15564800 | tf_op jit(solution)/shard_map/dot_general | solution.py:467
  319.6 24.5 %shard_map.358 = f32[160,2560]{1,0:T(8,128)S(1)} custom-call(bf16[4,160,2560]{2,1,0:T(8,128)(2,1)S(1)} %bitcast.210), custom_call_target="tpu_custom_call" | custom-call | tf_op jit(solution)/shard_map/pallas_call | solution.py:74
  350.5 24.3 %shard_map.356 = f32[160,2560]{1,0:T(8,128)S(1)} custom-call(bf16[4,160,2560]{2,1,0:T(8,128)(2,1)S(1)} %bitcast.209), custom_call_target="tpu_custom_call" | custom-call | tf_op jit(solution)/shard_map/pallas_call | solution.py:74
  378.7 21.9 %shard_map.359 = bf16[4,160,2560]{2,1,0:T(8,128)(2,1)S(1)} custom-call(bf16[160,2560]{1,0:T(8,128)(2,1)S(1)} %get-tuple-element.124.x_ref), custom_call_target="tpu_custom_call" | custom-call | tf_op jit(solution)/shard_map/pallas_call | solution.py:74
  404.1 9.1 %shard_map.360 = bf16[4,160,320]{2,1,0:T(8,128)(2,1)S(1)} custom-call(bf16[4,160,320]{2,1,0:T(8,128)(2,1)S(1)} %bitcast.218), custom_call_target="tpu_custom_call" | custom-call | tf_op jit(solution)/shard_map/pallas_call | solution.py:74
  435.8 21.4 %shard_map.362 = f32[160,256]{1,0:T(8,128)S(1)} custom-call(bf16[4,4,160,256]{3,2,1,0:T(8,128)(2,1)S(1)} %bitcast.208), custom_call_target="tpu_custom_call" | custom-call | tf_op jit(solution)/shard_map/pallas_call | solution.py:74
  463.0 7.0 %shard_map.363 = bf16[4,160,384]{2,1,0:T(8,128)(2,1)S(1)} custom-call(bf16[4,160,384]{2,1,0:T(8,128)(2,1)S(1)} %maximum_bitcast_fusion.1.x_ref), custom_call_target="tpu_custom_call" | custom-call | tf_op jit(solution)/shard_map/pallas_call | solution.py:74
  473.4 25.9 %shard_map.364 = f32[160,2560]{1,0:T(8,128)S(1)} custom-call(bf16[4,160,2560]{2,1,0:T(8,128)(2,1)S(1)} %bitcast.211), custom_call_target="tpu_custom_call" | custom-call | tf_op jit(solution)/shard_map/pallas_call | solution.py:74
  515.4 26.8 %shard_map.365 = f32[160,768]{1,0:T(8,128)S(1)} custom-call(bf16[4,4,160,768]{3,2,1,0:T(8,128)(2,1)S(1)} %bitcast.202), custom_call_target="tpu_custom_call" | custom-call | tf_op jit(solution)/shard_map/pallas_call | solution.py:74
  573.1 8.3 %shard_map.369 = bf16[4,48,960]{2,1,0:T(8,128)(2,1)S(1)} custom-call(bf16[4,48,960]{2,1,0:T(8,128)(2,1)S(1)} %pad.44.x_ref), custom_call_target="tpu_custom_call" | custom-call | tf_op jit(solution)/shard_map/pallas_call | solution.py:74
  585.2 11.6 %shard_map.368 = bf16[4,48,1920]{2,1,0:T(8,128)(2,1)S(1)} custom-call(bf16[4,48,1920]{2,1,0:T(8,128)(2,1)S(1)} %pad.43.x_ref), custom_call_target="tpu_custom_call" | custom-call | tf_op jit(solution)/shard_map/pallas_call | solution.py:74
  (290 shorter events, 174.4 us)
Async XLA Ops:
  7.2 242.9 %all-gather.2.cloned.1.call-start = ((), (), s32[]{:S(2)}) async-start(), calls=%async_computation.2 | async-start | bytes 16015360 | tf_op jit(solution)/shard_map/all_gather | solution.py:536
  12.0 18.8 %copy-start.55 = (f32[2,40]{1,0:T(2,128)S(1)}, f32[2,40]{1,0:T(2,128)}, u32[]{:S(2)}) copy-start(f32[2,40]{1,0:T(2,128)} %param.27) | copy-start | bytes 964
  12.0 18.9 %copy-start.38 = (f32[1280,40]{0,1:T(8,128)S(1)}, f32[1280,40]{0,1:T(8,128)}, u32[]{:S(2)}) copy-start(f32[1280,40]{0,1:T(8,128)} %param.24) | copy-start | bytes 614404
  12.1 19.1 %copy-start.37 = (f32[40,1280]{1,0:T(8,128)S(1)}, f32[40,1280]{1,0:T(8,128)}, u32[]{:S(2)}) copy-start(f32[40,1280]{1,0:T(8,128)} %param.22) | copy-start | bytes 614404
  30.7 541.2 %reduce-scatter.7.cloned.1.call-start = ((), (), s32[]{:S(2)}) async-start(), calls=%async_computation.4 | async-start | bytes 5570560 | tf_op jit(solution)/shard_map/reduce_scatter | solution.py:585
  81.5 23.9 %copy-start.53 = (f32[160]{0:T(256)}, f32[160]{0:T(256)S(1)}, u32[]{:S(2)}) copy-start(f32[160]{0:T(256)S(1)} %add_rsqrt_fusion.1) | copy-start | bytes 1924
  122.1 29.7 %copy-start.25 = (f32[4,160,384]{2,1,0:T(8,128)S(1)}, f32[4,160,384]{2,1,0:T(8,128)}, u32[]{:S(2)}) copy-start(f32[4,160,384]{2,1,0:T(8,128)} %copy-done.24) | copy-start | bytes 2949124
  181.4 24.4 %copy-start.14 = (f32[160,2560]{1,0:T(8,128)S(1)}, f32[160,2560]{1,0:T(8,128)}, u32[]{:S(2)}) copy-start(f32[160,2560]{1,0:T(8,128)} %param.20) | copy-start | bytes 4915204
  206.1 21.8 %copy-start.16 = (f32[160,2560]{1,0:T(8,128)}, f32[160,2560]{1,0:T(8,128)S(1)}, u32[]{:S(2)}) copy-start(f32[160,2560]{1,0:T(8,128)S(1)} %get-tuple-element.127) | copy-start | bytes 4915204
  206.3 21.5 %copy-start.21 = (f32[160,2560]{1,0:T(8,128)S(1)}, f32[160,2560]{1,0:T(8,128)}, u32[]{:S(2)}) copy-start(f32[160,2560]{1,0:T(8,128)} %param.21) | copy-start | bytes 4915204
  285.5 298.6 %reduce-scatter.5.cloned.1.call-start = ((), (), s32[]{:S(2)}) async-start(), calls=%async_computation.3 | async-start | bytes 10444800 | tf_op jit(solution)/shard_map/reduce_scatter | solution.py:593
  319.6 24.5 %copy-start.60 = (bf16[640,960]{1,0:T(8,128)(2,1)S(1)}, bf16[640,960]{1,0:T(8,128)(2,1)}, u32[]{:S(2)}) copy-start(bf16[640,960]{1,0:T(8,128)(2,1)} %copy-done.59) | copy-start | bytes 3686404
  350.4 24.3 %copy-start.17 = (f32[160,2560]{1,0:T(8,128)S(1)}, f32[160,2560]{1,0:T(8,128)}, u32[]{:S(2)}) copy-start(f32[160,2560]{1,0:T(8,128)} %copy-done.16) | copy-start | bytes 4915204
  378.7 23.6 %copy-start.5 = (bf16[4,4,160,768]{3,2,1,0:T(8,128)(2,1)S(1)}, bf16[4,4,160,768]{3,2,1,0:T(8,128)(2,1)}, u32[]{:S(2)}) copy-start(bf16[4,4,160,768]{3,2,1,0:T(8,128)(2,1)} %copy-done.3) | copy-start | bytes 11796484
  414.2 14.1 %slice-start = ((s8[8192000]{0:T(1024)(128)(4,1)}), s8[4194304]{0:T(1024)(128)(4,1)S(1)}, s32[]{:S(2)}) async-start(s8[8192000]{0:T(1024)(128)(4,1)} %bitcast.225), calls=%async_computation.5 | async-start | bytes 8388608
  435.8 22.2 %copy-start.35 = (bf16[1,4,4,160,256]{4,3,2,1,0:T(8,128)(2,1)S(1)}, bf16[1,4,4,160,256]{4,3,2,1,0:T(8,128)(2,1)}, u32[]{:S(2)}) copy-start(bf16[1,4,4,160,256]{4,3,2,1,0:T(8,128)(2,1)} %copy-done.34) | copy-start | bytes 3932164
  473.4 26.0 %copy-start.15 = (f32[160,2560]{1,0:T(8,128)S(1)}, f32[160,2560]{1,0:T(8,128)}, u32[]{:S(2)}) copy-start(f32[160,2560]{1,0:T(8,128)} %param.20) | copy-start | bytes 4915204
  473.4 26.0 %copy-start.51 = (f32[2560]{0:T(1024)S(1)}, f32[2560]{0:T(1024)}, u32[]{:S(2)}) copy-start(f32[2560]{0:T(1024)} %copy-done.50) | copy-start | bytes 30724
  473.4 26.0 %copy-start.54 = (f32[160]{0:T(256)S(1)}, f32[160]{0:T(256)}, u32[]{:S(2)}) copy-start(f32[160]{0:T(256)} %copy-done.53) | copy-start | bytes 1924
  473.4 26.5 %copy-start.11 = (bf16[4,160,320]{2,1,0:T(8,128)(2,1)S(1)}, bf16[4,160,320]{2,1,0:T(8,128)(2,1)}, u32[]{:S(2)}) copy-start(bf16[4,160,320]{2,1,0:T(8,128)(2,1)} %copy-done.10) | copy-start | bytes 1228804
  549.5 15.9 %copy-start.56 = (f32[2,40]{1,0:T(2,128)S(1)}, f32[2,40]{1,0:T(2,128)}, u32[]{:S(2)}) copy-start(f32[2,40]{1,0:T(2,128)} %param.27) | copy-start | bytes 964
  549.5 15.9 %copy-start.57 = (f32[2,40]{1,0:T(2,128)S(1)}, f32[2,40]{1,0:T(2,128)}, u32[]{:S(2)}) copy-start(f32[2,40]{1,0:T(2,128)} %param.33) | copy-start | bytes 964
  549.5 15.9 %copy-start.58 = (f32[2,40]{1,0:T(2,128)S(1)}, f32[2,40]{1,0:T(2,128)}, u32[]{:S(2)}) copy-start(f32[2,40]{1,0:T(2,128)} %param.39) | copy-start | bytes 964
  572.0 10.6 %copy-start.42 = (f32[3840,40]{0,1:T(8,128)S(1)}, f32[3840,40]{0,1:T(8,128)}, u32[]{:S(2)}) copy-start(f32[3840,40]{0,1:T(8,128)} %param.38) | copy-start | bytes 1843204
  (42 other events, 152.6 us)
Sparse Core Ops, SparseCore 0:
  30.9 121.5 all-gather.1
  285.6 75.8 reduce-scatter.6
  365.0 92.7 reduce-scatter.4

commit v2 on v1

--- a/solution.py
+++ b/solution.py
@@ -49,6 +49,12 @@
     for peer in peers:
         pl.semaphore_signal(barrier, inc=1, device_id=peer, device_id_type=MESH)
     pl.semaphore_wait(barrier, len(peers))
+
+
+def dot(left_side, right_side, contract):
+    return lax.dot_general(
+        left_side, right_side, ((contract[:1], contract[1:]), ((), ())), preferred_element_type=F32
+    )
 
 
 class Sender:
@@ -419,6 +425,451 @@
     )
 
 
+class Mover:
+    def __init__(self, send_sem, recv_sem):
+        self.send_sem, self.recv_sem, self.pending = send_sem, recv_sem, []
+
+    def copy(self, src, dst, peer):
+        index = len(self.pending)
+        one = pltpu.make_async_remote_copy(
+            src_ref=src,
+            dst_ref=dst,
+            send_sem=self.send_sem.at[index],
+            recv_sem=self.recv_sem.at[index],
+            device_id=peer,
+            device_id_type=MESH,
+        )
+        one.start()
+        self.pending.append(one)
+        return one
+
+    def finish(self):
+        for one in self.pending:
+            one.wait_send()
+
+
+def advance(steps):
+    next(steps, None)
+
+
+def exchange_steps(mover, src, dst):
+    me = lax.axis_index("z")
+    copies = [
+        mover.copy(src.at[step("z", d)], dst.at[me], {"z": step("z", d)}) for d in (2, 1, 3)
+    ]
+    yield
+    for copy in copies:
+        copy.wait_recv()
+
+
+def core_rows():
+    base = pl.multiple_of(lax.axis_index("tensor") * HALF, 16)
+    return (
+        pl.ds(base, HALF),
+        pl.ds(base, PART),
+        pl.ds(pl.multiple_of(base + PART, 16), HALF - PART),
+        pl.ds(pl.multiple_of(HALF - base, 16), HALF),
+    )
+
+
+def gather_steps(mover, x, out):
+    me, left, right, far = (step("z", d) for d in (0, -1, 1, 2))
+    half, first, last, _ = core_rows()
+    to_right = mover.copy(x.at[half], out.at[me, half], {"z": right})
+    to_left = mover.copy(x.at[half], out.at[me, half], {"z": left})
+    yield
+    to_right.wait_recv()
+    on_right = mover.copy(out.at[left, first], out.at[left, first], {"z": right})
+    shares = [mover.copy(out.at[left, half], out.at[left, half], sibling())]
+    to_left.wait_recv()
+    on_left = mover.copy(out.at[right, last], out.at[right, last], {"z": left})
+    shares.append(mover.copy(out.at[right, half], out.at[right, half], sibling()))
+    yield
+    on_right.wait_recv()
+    on_left.wait_recv()
+    shares.append(mover.copy(out.at[far, half], out.at[far, half], sibling()))
+    yield
+    for copy in shares:
+        copy.wait_recv()
+
+
+def cut_rows(which, cut):
+    base, size = (0, cut) if which == 0 else (cut, BLOCK - cut)
+    part = -(-size // 32) * 16
+    return pl.ds(base, size), pl.ds(base, part), pl.ds(base + part, size - part)
+
+
+def plane_gather_steps(mover, axes, x, out, cut=HALF, order=(0, 1), share=False):
+    a, b = (lax.axis_index(axis) for axis in axes)
+    state = {}
+    for which, axis in enumerate(axes):
+        rows = cut_rows(which, cut)[0]
+        place = (lambda i, r: out.at[i, b, r]) if which == 0 else (lambda i, r: out.at[a, i, r])
+        me = (a, b)[which]
+        to_right = mover.copy(x.at[rows], place(me, rows), {axis: step(axis, 1)})
+        to_left = mover.copy(x.at[rows], place(me, rows), {axis: step(axis, -1)})
+        state[which] = (axis, place, to_right, to_left)
+    yield
+    passed = {}
+    for which in order:
+        axis, place, to_right, to_left = state[which]
+        _, first, last = cut_rows(which, cut)
+        left, right = step(axis, -1), step(axis, 1)
+        to_right.wait_recv()
+        on_right = mover.copy(place(left, first), place(left, first), {axis: right})
+        to_left.wait_recv()
+        on_left = mover.copy(place(right, last), place(right, last), {axis: left})
+        passed[which] = (on_right, on_left)
+    yield
+    state = {}
+    shares = []
+
+    def give(piece):
+        if share:
+            shares.append(mover.copy(piece, piece, sibling()))
+
+    for which in order:
+        axis, other = axes[which], axes[1 - which]
+        rows = cut_rows(which, cut)[0]
+        if which == 0:
+            place = lambda i, lo, n, rows=rows: out.at[pl.ds(lo, n), i, rows]
+        else:
+            place = lambda i, lo, n, rows=rows: out.at[i, pl.ds(lo, n), rows]
+        me = (b, a)[which]
+        for copy in passed[which]:
+            copy.wait_recv()
+        to_right = mover.copy(place(me, 0, 4), place(me, 0, 4), {other: step(other, 1)})
+        to_left = mover.copy(place(me, 0, 4), place(me, 0, 4), {other: step(other, -1)})
+        give(place(me, 0, 4))
+        state[which] = (other, place, to_right, to_left)
+        yield
+    ends = []
+    for which in order:
+        other, place, to_right, to_left = state[which]
+        left, right = step(other, -1), step(other, 1)
+        to_right.wait_recv()
+        ends.append(mover.copy(place(left, 0, 2), place(left, 0, 2), {other: right}))
+        give(place(left, 0, 4))
+        to_left.wait_recv()
+        ends.append(mover.copy(place(right, 2, 2), place(right, 2, 2), {other: left}))
+        give(place(right, 0, 4))
+        yield
+    for copy in ends:
+        copy.wait_recv()
+    for which in order:
+        other, place, _, _ = state[which]
+        give(place(step(other, 2), 0, 4))
+    for copy in shares:
+        copy.wait_recv()
+
+
+def lanes(shape):
+    return lax.broadcasted_iota(jnp.int32, shape, len(shape) - 1)
+
+
+def turn(values, cos, sin):
+    return values * cos + pltpu.roll(values, 64, 1) * sin
+
+
+def whole_rows(blocks, stage, dst):
+    for i in range(RING):
+        stage[i * OWN : (i + 1) * OWN] = blocks[i].astype(F32)[:OWN]
+    dst[...] = stage[...].astype(LOW)
+
+
+def first_kernel(
+    attn_rows,
+    feed_rows,
+    tokens,
+    dy,
+    cos_ref,
+    sin_ref,
+    cos_kv,
+    sin_kv,
+    feed_full,
+    attn_full,
+    normed_one,
+    dy_all,
+    query,
+    keyvalue,
+    log_total,
+    att_slice,
+    residual,
+    normed_two,
+    send_sem,
+    recv_sem,
+    local_sem,
+    attn_got,
+    attn_mine,
+    attn_stage,
+    feed_got,
+    feed_mine,
+    feed_stage,
+    unit_low,
+    unit_all,
+    gain_ref,
+    qkv_send,
+    qkv_got,
+    kv_own,
+    scores,
+    attended,
+    att_send,
+    part,
+    other,
+    total,
+    part_a,
+    part_b,
+    from_left,
+    from_right,
+    normed_low,
+):
+    z, x, y, core = (lax.axis_index(axis) for axis in ("z", "x", "dp", "tensor"))
+    left, right, far = (step("z", d) for d in (-1, 1, 2))
+    half, _, _, their_half = core_rows()
+    plane = ("dp", "x")
+    greet(
+        [{"z": step("z", d)} for d in (1, 2, 3)] + plane_peers(("dp", "x")) + [sibling()]
+    )
+    mover = Mover(send_sem, recv_sem)
+
+    attn_swap = exchange_steps(mover, attn_rows, attn_got)
+    advance(attn_swap)
+    values = tokens[...]
+    unit = values * lax.rsqrt(jnp.mean(values * values, axis=-1, keepdims=True) + eps_norm)
+    unit_low[...] = unit.astype(LOW)
+    unit_gather = gather_steps(mover, unit_low, unit_all)
+    advance(unit_gather)
+    feed_swap = exchange_steps(mover, feed_rows, feed_got)
+    advance(feed_swap)
+    unit_all[z] = unit_low[...]
+    attn_got[z] = attn_rows[z]
+    advance(attn_swap)
+    whole_rows(attn_got, attn_stage, attn_mine)
+    attn_gather = plane_gather_steps(mover, plane, attn_mine, attn_full)
+    advance(attn_gather)
+    attn_full[y, x] = attn_mine[...]
+    advance(unit_gather)
+    advance(attn_gather)
+    advance(attn_gather)
+    advance(attn_gather)
+    feed_got[z] = feed_rows[z]
+    advance(unit_gather)
+    advance(feed_swap)
+    whole_rows(feed_got, feed_stage, feed_mine)
+    feed_own = pltpu.make_async_copy(feed_mine, feed_full.at[y, x], local_sem.at[0])
+    feed_own.start()
+    advance(attn_gather)
+    advance(attn_gather)
+    feed_gather = plane_gather_steps(mover, plane, feed_mine, feed_full, cut=64, order=(1, 0))
+    advance(feed_gather)
+    dy_gather = gather_steps(mover, dy, dy_all)
+    advance(dy_gather)
+    dy_own = pltpu.make_async_copy(dy, dy_all.at[z], local_sem.at[1])
+    dy_own.start()
+    advance(unit_gather)
+    advance(attn_gather)
+
+    scale_cols = attn_full[:, :, :, 640:768].reshape(D, 128)
+    pick = (lanes((8, 128)) == 64 + lax.broadcasted_iota(jnp.int32, (8, 128), 0)).astype(LOW)
+    gain_ref[...] = 1.0 + dot(pick, scale_cols, (1, 1))
+    qkv_weight = attn_full[:, :, :, :384].reshape(D, 384)
+    copies = []
+    for d in (2, 1, 3, 0):
+        block = step("z", d)
+        normed = (unit_all[block].astype(F32) * gain_ref[0:1, :]).astype(LOW)
+        normed_one[block] = normed
+        qkv_send[block] = dot(normed, qkv_weight, (1, 0)).astype(LOW)
+        if d:
+            copies.append(mover.copy(qkv_send.at[block], qkv_got.at[z], {"z": block}))
+    qkv_got[z] = qkv_send[z]
+    advance(feed_gather)
+    feed_own.wait()
+    for copy in copies:
+        copy.wait_recv()
+    low_lanes = lanes((BLOCK, 128)) < TAIL
+    cos, sin = cos_ref[...], sin_ref[...]
+
+    def joined(i, offset):
+        one, two = (qkv_got[i + k, :, 256:384].astype(F32) for k in (0, 1))
+        if offset == 0:
+            return jnp.where(low_lanes, one, pltpu.roll(two, TAIL, 1))
+        return jnp.where(low_lanes, pltpu.roll(one, TAIL, 1), two)
+
+    kv_own[:, :128] = turn(joined(0, 1), cos_kv[...], sin_kv[...]).astype(LOW)
+    kv_own[:, 128:] = joined(2, 1).astype(LOW)
+    kv_mine = keyvalue.at[core]
+    kv_gather = plane_gather_steps(mover, ("x", "z"), kv_own, kv_mine, share=True)
+    advance(kv_gather)
+    keyvalue[core, x, z] = kv_own[...]
+    scale = HD ** (-0.5)
+    for h in range(4):
+        first = qkv_got[h, :, :128].astype(F32)
+        query[h, :, :128] = (turn(first, cos, sin) * scale).astype(LOW)
+        query[h, :, 128:] = (qkv_got[h, :, 128:256].astype(F32) * scale).astype(LOW)
+    query[4, :, :128] = (turn(joined(0, 0), cos, sin) * scale).astype(LOW)
+    query[4, :, 128:] = (joined(2, 0) * scale).astype(LOW)
+    advance(kv_gather)
+    advance(feed_gather)
+    advance(kv_gather)
+    advance(kv_gather)
+    advance(kv_gather)
+    advance(kv_gather)
+    advance(feed_gather)
+    advance(dy_gather)
+    advance(kv_gather)
+
+    start = (x * RING + z) * BLOCK
+    chunk = RING * BLOCK
+
+    def one_head(h, carry):
+        queries = query[h]
+        top = jnp.full((BLOCK, 1), masked_fill, F32)
+        for k in range(RING):
+            rows = keyvalue[0, k].reshape(chunk, HD)
+            tile = dot(queries, rows, (1, 1))
+            gap = (start - k * chunk) + (
+                lax.broadcasted_iota(jnp.int32, tile.shape, 0) - lanes(tile.shape)
+            )
+            tile = jnp.where((gap >= 0) & (gap < WINDOW), tile, masked_fill)
+            scores[:, k * chunk : (k + 1) * chunk] = tile
+            top = jnp.maximum(top, jnp.max(tile, axis=-1, keepdims=True))
+        sums = jnp.zeros((BLOCK, 1), F32)
+        for k in range(RING):
+            tile = jnp.exp(scores[:, k * chunk : (k + 1) * chunk] - top)
+            scores[:, k * chunk : (k + 1) * chunk] = tile
+            sums = sums + jnp.sum(tile, axis=-1, keepdims=True)
+        inverse = 1.0 / sums
+        result = jnp.zeros((BLOCK, HD), F32)
+        for k in range(RING):
+            low = (scores[:, k * chunk : (k + 1) * chunk] * inverse).astype(LOW)
+            result = result + dot(low, keyvalue[1, k].reshape(chunk, HD), (1, 0))
+        attended[h] = result
+        log_total[h] = jnp.broadcast_to(top + jnp.log(sums), (BLOCK, 128))
+        return carry
+
+    lax.fori_loop(0, 5, one_head, 0)
+    for j in range(RING):
+        att_send[j, :, :256] = attended[j].astype(LOW)
+        tile = attended[4, :, (j // 2) * 128 : (j // 2 + 1) * 128]
+        tile = pltpu.roll(tile, TAIL, 1) if j % 2 else tile
+        att_send[j, :, 256:] = jnp.where(low_lanes, tile, 0.0).astype(LOW)
+    att_swap = exchange_steps(mover, att_send, att_slice)
+    advance(att_swap)
+    att_slice[z] = att_send[z]
+    advance(dy_gather)
+    advance(att_swap)
+
+    out_weight = attn_full[:, :, :, 384:].reshape(D, 384)
+    blocks = (far, right, left, z)
+    shares = []
+    for slot, block in enumerate(blocks):
+        part[block] = dot(att_slice[block], out_weight, (1, 1)).astype(LOW)
+        shares.append(mover.copy(part.at[block, their_half], other.at[slot], sibling()))
+
+    def both(slot):
+        return part[blocks[slot], half].astype(F32) + other[slot].astype(F32)
+
+    shares[0].wait_recv()
+    total[0] = both(0).astype(LOW)
+    far_right = mover.copy(total.at[0, pl.ds(0, PART)], part_a, {"z": right})
+    far_left = mover.copy(total.at[0, pl.ds(PART, HALF - PART)], part_b, {"z": left})
+    shares[1].wait_recv()
+    shares[2].wait_recv()
+    far_right.wait_recv()
+    summed = both(1)
+    total[1, :PART] = (summed[:PART] + part_a[...].astype(F32)).astype(LOW)
+    total[1, PART:] = summed[PART:].astype(LOW)
+    to_right = mover.copy(total.at[1], from_left, {"z": right})
+    far_left.wait_recv()
+    summed = both(2)
+    total[2, :PART] = summed[:PART].astype(LOW)
+    total[2, PART:] = (summed[PART:] + part_b[...].astype(F32)).astype(LOW)
+    to_left = mover.copy(total.at[2], from_right, {"z": left})
+    shares[3].wait_recv()
+    to_right.wait_recv()
+    to_left.wait_recv()
+    rows = tokens[half, :] + (
+        both(3) + from_left[...].astype(F32) + from_right[...].astype(F32)
+    )
+    residual[half, :] = rows
+    res_share = mover.copy(residual.at[half], residual.at[half], sibling())
+
+    def normed_rows(rows):
+        unit = rows * lax.rsqrt(jnp.mean(rows * rows, axis=-1, keepdims=True) + eps_norm)
+        return (unit * gain_ref[1:2, :]).astype(LOW)
+
+    normed_low[half, :] = normed_rows(rows)
+    normed_gather = gather_steps(mover, normed_low, normed_two)
+    advance(normed_gather)
+    res_share.wait_recv()
+    normed_low[their_half, :] = normed_rows(residual[their_half, :])
+    normed_two[z] = normed_low[...]
+    advance(normed_gather)
+    advance(feed_gather)
+    advance(normed_gather)
+    advance(feed_gather)
+    advance(dy_gather)
+    advance(normed_gather)
+    advance(feed_gather)
+    dy_own.wait()
+    mover.finish()
+
+
+def run_first(*operands):
+    out = {
+        "feed_full": ((RING, RING, BLOCK, 2944), LOW, pl.ANY),
+        "attn_full": ((RING, RING, BLOCK, 768), LOW, pltpu.VMEM),
+        "normed_one": ((RING, BLOCK, D), LOW, pltpu.VMEM),
+        "dy_all": ((RING, BLOCK, D), LOW, pl.ANY),
+        "query": ((5, BLOCK, HD), LOW, pltpu.VMEM),
+        "keyvalue": ((2, RING, RING, BLOCK, HD), LOW, pltpu.VMEM),
+        "log_total": ((5, BLOCK, 128), F32, pltpu.VMEM),
+        "att_slice": ((RING, BLOCK, 384), LOW, pltpu.VMEM),
+        "residual": ((BLOCK, D), F32, pltpu.VMEM),
+        "normed_two": ((RING, BLOCK, D), LOW, pltpu.VMEM),
+    }
+    spaces = [pltpu.VMEM, pltpu.VMEM, pltpu.VMEM, pl.ANY] + [pltpu.VMEM] * 4
+    copies = 120
+    results = pl.pallas_call(
+        first_kernel,
+        out_shape=[jax.ShapeDtypeStruct(shape, kind) for shape, kind, _ in out.values()],
+        in_specs=[pl.BlockSpec(memory_space=space) for space in spaces],
+        out_specs=[pl.BlockSpec(memory_space=space) for _, _, space in out.values()],
+        scratch_shapes=[
+            pltpu.SemaphoreType.DMA((copies,)),
+            pltpu.SemaphoreType.DMA((copies,)),
+            pltpu.SemaphoreType.DMA((2,)),
+            pltpu.VMEM((RING, PAD, 768), LOW),
+            pltpu.VMEM((BLOCK, 768), LOW),
+            pltpu.VMEM((BLOCK, 768), F32),
+            pltpu.VMEM((RING, PAD, 2944), LOW),
+            pltpu.VMEM((BLOCK, 2944), LOW),
+            pltpu.VMEM((BLOCK, 2944), F32),
+            pltpu.VMEM((BLOCK, D), LOW),
+            pltpu.VMEM((RING, BLOCK, D), LOW),
+            pltpu.VMEM((8, D), F32),
+            pltpu.VMEM((RING, BLOCK, 384), LOW),
+            pltpu.VMEM((RING, BLOCK, 384), LOW),
+            pltpu.VMEM((BLOCK, HD), LOW),
+            pltpu.VMEM((BLOCK, RING * RING * BLOCK), F32),
+            pltpu.VMEM((5, BLOCK, HD), F32),
+            pltpu.VMEM((RING, BLOCK, 384), LOW),
+            pltpu.VMEM((RING, BLOCK, D), LOW),
+            pltpu.VMEM((4, HALF, D), LOW),
+            pltpu.VMEM((3, HALF, D), LOW),
+            pltpu.VMEM((PART, D), LOW),
+            pltpu.VMEM((HALF - PART, D), LOW),
+            pltpu.VMEM((HALF, D), LOW),
+            pltpu.VMEM((HALF, D), LOW),
+            pltpu.VMEM((BLOCK, D), LOW),
+        ],
+        compiler_params=pltpu.CompilerParams(
+            collective_id=1, has_side_effects=True, vmem_limit_bytes=60 * 1024 * 1024
+        ),
+    )(*operands)
+    return dict(zip(out, results, strict=True))
+
+
 def rotate(values, positions, direction):
     quarter = values.shape[-1] // 4
     frequency = 10000.0 ** (-jnp.arange(quarter, dtype=F32) / quarter)
@@ -463,18 +914,26 @@
     return max(1, H * HD * 4 // min(WINDOW, seq_length))
 
 
-def dot(left_side, right_side, contract):
-    return lax.dot_general(
-        left_side, right_side, ((contract[:1], contract[1:]), ((), ())), preferred_element_type=F32
-    )
-
-
 def activate(gate_part, upper_part):
     return jax.nn.gelu(gate_part, approximate=True) * upper_part
 
 
 def quarters(rows):
     return rows.reshape(OWN, RING, -1).transpose(1, 0, 2)
+
+
+def head_quarters(rows):
+    split = rows.reshape(rows.shape[0], 5, HD)
+    last = split[:, 4].reshape(-1, RING, TAIL)
+    return jnp.concatenate([split[:, :4], last], axis=2).transpose(1, 0, 2)
+
+
+def whole_heads(slices):
+    slices = slices.transpose(1, 0, 2)
+    rows = slices.shape[0]
+    return jnp.concatenate(
+        [slices[..., :HD].reshape(rows, -1), slices[..., HD:].reshape(rows, -1)], axis=1
+    )
 
 
 def whole(slices):
@@ -518,7 +977,8 @@
     keyvalue_part = lax.dynamic_index_in_dim(w_keyvalue, core, 1, keepdims=False)
     scale_columns = jnp.broadcast_to(norm_scales.T[None], (RING, OWN, 2))
     attn_rows = jnp.concatenate(
-        [quarters(w_query), quarters(keyvalue_part), quarters(w_out.T), scale_columns], axis=2
+        [head_quarters(w_query), quarters(keyvalue_part), head_quarters(w_out.T), scale_columns],
+        axis=2,
     ).astype(LOW)
     attn_rows = pad_to(pad_to(attn_rows, 2, 768), 1, PAD)
     gateup = w_gateup.astype(LOW).reshape(OWN, 2, RING, MAIN + TAIL).transpose(2, 0, 1, 3)
@@ -531,50 +991,38 @@
         axis=2,
     )
     feed_rows = pad_to(pad_to(feed_rows, 2, 2944), 1, PAD)
-    attn_mine = exchange_z(attn_rows, 1)[:, :OWN].reshape(BLOCK, 768)
-    feed_mine = exchange_z(feed_rows, 2)[:, :OWN].reshape(BLOCK, 2944)
-    feed_full = lax.all_gather(feed_mine, ("dp", "x"), axis=0, tiled=True)
-    attn_full = gather_plane(attn_mine, ("dp", "x"), 3).reshape(D, 768)
+    frequency = 10000.0 ** (-jnp.arange(TAIL, dtype=F32) / TAIL)
+    angles = positions.astype(F32)[:, None] * frequency[None, :]
+    cos_table = jnp.tile(jnp.cos(angles), (1, 2))
+    sin_table = jnp.concatenate([-jnp.sin(angles), jnp.sin(angles)], axis=1)
+    cos_kv = jnp.where(core == 0, cos_table, 1.0)
+    sin_kv = jnp.where(core == 0, sin_table, 0.0)
+    first = run_first(
+        attn_rows, feed_rows, tokens, cotangent.astype(LOW), cos_table, sin_table, cos_kv, sin_kv
+    )
+    feed_full = first["feed_full"].reshape(D, 2944)
+    attn_full = first["attn_full"].reshape(D, 768)
     gateup_full = feed_full[:, : 2 * (MAIN + TAIL)]
     down_full = feed_full[:, 2 * (MAIN + TAIL) : 3 * (MAIN + TAIL)]
     qkv_full = attn_full[:, :384]
     out_full = attn_full[:, 384:704]
     gains = 1.0 + attn_full[:, 704:706].astype(F32).T
     gain_one, gain_two = gains[0], gains[1]
-
     inverse_one = inverse_rms(tokens)
     unit_one = tokens * inverse_one
-    unit_all = gather_z(unit_one.astype(LOW), 4)
-    dy_all = gather_z(cotangent.astype(LOW), 5)
-    normed_one = (unit_all.astype(F32) * gain_one).astype(LOW)
-    qkv_slice = dot(normed_one, qkv_full, (1, 0)).astype(LOW).reshape(RING, BLOCK, 384)
-    qkv = exchange_z(qkv_slice, 6).astype(F32)
-    query_raw = whole(qkv[..., :320]).reshape(BLOCK, head_count, HD)
-    query_low = (rotate(query_raw, positions, 1.0) * HD ** (-0.5)).astype(LOW)
-    keyvalue_raw = whole(qkv[..., 320:])
-    keyvalue_low = jnp.where(
-        core == 0, rotate(keyvalue_raw, positions, 1.0), keyvalue_raw
-    ).astype(LOW)
-    keyvalue_all = gather_plane(keyvalue_low, ("x", "z"), 7, share=True).reshape(2, seq_length, HD)
-    key_rows, value_rows = keyvalue_all[0], keyvalue_all[1]
+    dy_all = first["dy_all"].reshape(-1, D)
+    normed_one = first["normed_one"].reshape(-1, D)
+    query_low = first["query"]
+    key_rows, value_rows = first["keyvalue"].reshape(2, seq_length, HD)
+    log_total = first["log_total"][:, :, :1]
+    attended_slice = first["att_slice"].reshape(-1, 384)[:, :320]
+    residual = first["residual"]
+    normed_two = first["normed_two"].reshape(-1, D)
     key_pos = jnp.arange(seq_length, dtype=jnp.int32)
     distance = positions[:, None] - key_pos[None, :]
     visible = (distance >= 0) & (distance < WINDOW)
-    scores = jnp.einsum("chd,kd->hck", query_low, key_rows, preferred_element_type=F32)
-    scores = jnp.where(visible[None], scores, masked_fill)
-    maximum = jnp.max(scores, axis=-1, keepdims=True)
-    exponent = jnp.exp(scores - maximum)
-    row_total = jnp.sum(exponent, axis=-1, keepdims=True)
-    log_total = maximum + jnp.log(row_total)
-    prob_low = (exponent / row_total).astype(LOW)
-    attended = jnp.einsum("hck,kd->chd", prob_low, value_rows, preferred_element_type=F32)
-    attended_low = attended.reshape(BLOCK, RING, 320).astype(LOW).transpose(1, 0, 2)
-    attended_slice = exchange_z(attended_low, 8).reshape(-1, 320)
-    out_part = dot(attended_slice, out_full, (1, 1)).astype(LOW)
-    residual = tokens + reduce_z(out_part, 9)
     inverse_two = inverse_rms(residual)
     unit_two = residual * inverse_two
-    normed_two = gather_z((unit_two * gain_two).astype(LOW), 10)
 
     gateup = dot(normed_two, gateup_full, (1, 0))
     gate = jnp.concatenate([gateup[:, :MAIN], gateup[:, 2 * MAIN : 2 * MAIN + TAIL]], axis=1)
@@ -600,15 +1048,15 @@
     grad_attn = gather_z(grad_residual.astype(LOW), 13)
     grad_out = dot(grad_attn, attended_slice, (0, 0)).astype(LOW)
     grad_att_slice = dot(grad_attn, out_full, (1, 0)).astype(LOW).reshape(RING, BLOCK, 320)
-    grad_att_low = whole(exchange_z(grad_att_slice, 14)).reshape(BLOCK, head_count, HD)
-    scores = jnp.einsum("chd,kd->hck", query_low, key_rows, preferred_element_type=F32)
+    grad_att_low = whole_heads(exchange_z(grad_att_slice, 14)).reshape(BLOCK, head_count, HD)
+    scores = jnp.einsum("hcd,kd->hck", query_low, key_rows, preferred_element_type=F32)
     probs = jnp.where(visible[None], jnp.exp(scores - log_total), 0.0)
     prob_low = probs.astype(LOW)
     grad_probs = jnp.einsum("chd,kd->hck", grad_att_low, value_rows, preferred_element_type=F32)
     delta = jnp.sum(probs * grad_probs, axis=-1, keepdims=True)
     grad_scores_low = (probs * (grad_probs - delta)).astype(LOW)
     grad_query = jnp.einsum("hck,kd->chd", grad_scores_low, key_rows, preferred_element_type=F32)
-    grad_keys = jnp.einsum("hck,chd->kd", grad_scores_low, query_low, preferred_element_type=F32)
+    grad_keys = jnp.einsum("hck,hcd->kd", grad_scores_low, query_low, preferred_element_type=F32)
     grad_values = jnp.einsum("hck,chd->kd", prob_low, grad_att_low, preferred_element_type=F32)
     pair = jnp.stack([grad_keys, grad_values]).astype(LOW)
     mine = lax.dynamic_index_in_dim(pair, core, 0, keepdims=False)
@@ -618,8 +1066,9 @@
     grad_kv_low = jnp.where(core == 0, rotate(grad_kv, positions, -1.0), grad_kv).astype(LOW)
     grad_query_low = rotate(grad_query * HD ** (-0.5), positions, -1.0).astype(LOW)
     grad_qkv = jnp.concatenate(
-        [grad_query_low.reshape(BLOCK, RING, 320), grad_kv_low.reshape(BLOCK, RING, 64)], axis=2
-    ).transpose(1, 0, 2)
+        [head_quarters(grad_query_low.reshape(BLOCK, -1)), grad_kv_low.reshape(BLOCK, RING, TAIL).transpose(1, 0, 2)],
+        axis=2,
+    )
     grad_qkv_slice = exchange_z(grad_qkv, 17).reshape(-1, 384)
     norm_part_one = dot(grad_qkv_slice, qkv_full, (1, 1)).astype(LOW)
     normed_grad_one = reduce_z(norm_part_one, 18)
@@ -645,9 +1094,9 @@
         axis=3,
     ).transpose(1, 2, 0, 3).reshape(OWN, 2, -1)
     attn_shard = to_owners(attn_sum, 22)
-    query_shard = whole(attn_shard[..., :320])
+    query_shard = whole_heads(attn_shard[..., :320])
     kv_half = whole(attn_shard[..., 320:384])
-    out_shard = whole(attn_shard[..., 384:704]).T
+    out_shard = whole_heads(attn_shard[..., 384:704]).T
     scale_grads = jnp.sum(attn_shard[..., 704:706], axis=0).T
     kv_other = swap_cores(pad_to(kv_half, 0, PAD).astype(LOW), 23)[:OWN].astype(F32)
     keyvalue_shard = jnp.stack(

time: 621 us -> 563 us (0.907)
  Pallas kernels: 398 us -> 360 us
  local copies, waits for them, and re-layouts: 79.1 us -> 56.8 us
    pallas_call x23 -> x13, Pallas kernels: 398 us -> 194 us  [comm_call(): pl.pallas_call(kernel, out_shape=out_shape, in_specs=[pl.BlockSpec(memory...]
    pallas_call x0 -> x1, Pallas kernels: none -> 166 us  [run_first(): pl.pallas_call(first_kernel, out_shape=[jax.ShapeDtypeStruct(shape, kind)...]
    unnamed x132 -> x98, local copies, waits for them, and re-layouts: 35.2 us -> 17.4 us
    dot_general x12 -> x10, matrix products: 66.4 us -> 64 us  [dot(): lax.dot_general(left_side, right_side, ((contract[:1], contract[1:]), (()...]
  transfers between devices with their start and end apart: 3 -> 2, of which waited for: 0 -> 0; matrix products, arithmetic and copies ran while one was open for 21% -> 21% of each run, Pallas kernels for 60% -> 33%
where the time goes in v2:
time: 563 us; the launch traced here: 555 us
  Pallas kernels  360 us (64%)
  matrix products  81.1 us (14%)
  local copies, waits for them, and re-layouts  56.8 us (10%)
  other arithmetic  41.7 us (7%)
  between operations  15.8 us (3%)
    pallas_call x13, Pallas kernels, comm_call(): pl.pallas_call(kernel, out_shape=out_shape, in_specs=[pl.BlockSpec(memory...  194 us
    pallas_call x1, Pallas kernels, run_first(): pl.pallas_call(first_kernel, out_shape=[jax.ShapeDtypeStruct(shape, kind)...  166 us
    dot_general x10, matrix products, dot(): lax.dot_general(left_side, right_side, ((contract[:1], contract[1:]), (()...  64 us
    unnamed x98, local copies, waits for them, and re-layouts  17.4 us
    sub x6, other arithmetic, adam_update(): weight - learn_rate * (corrected + decay_rate * weight)  13.7 us
  transfers between devices with their start and end apart: 2, of which 0 were waited for; matrix products, arithmetic and copies ran while one was open for 21% of the time, Pallas kernels for 33%

profile of v2, /device:TPU:1, one launch (start us, length us, event | category | flops | bytes accessed | tf_op | source)
XLA Modules:
  0.0 555.2 jit_solution(5607952296065075745)
XLA Ops:
  20.2 166.1 %shard_map.347 = (bf16[4,4,160,2944]{3,2,1,0:T(8,128)(2,1)}, bf16[4,4,160,768]{3,2,1,0:T(8,128)(2,1)}, bf16[4,160,2560]{2,1,0:T(8,128)(2,1)}, bf16[4,160,2560]{2...) custom-call(bf16[4,48,768]{2,1,0:T(8,128)(2,1)} %pad.37.attn_rows, ...), custom_call_target="tpu_custom_call" | custom-call | tf_op jit(solution)/shard_map/pallas_call | solution.py:833
  186.3 10.7 %fusion.2 = f32[640,1920]{1,0:T(8,128)S(1)} fusion(bf16[640,2560]{1,0:T(8,128)(2,1)} %bitcast.198, bf16[2560,2944]{1,0:T(8,128)(2,1)} %bitcast.194), kind=kOutput, calls=%fused_computation.3 | convolution fusion | flops 6291456000 | bytes 18022400 | tf_op jit(solution)/shard_map/dot_general | solution.py:55
  199.2 8.6 %multiply_convert_fusion = (bf16[640,960]{1,0:T(8,128)(2,1)}, bf16[640,960]{1,0:T(8,128)(2,1)S(1)}, bf16[640,960]{1,0:T(8,128)(2,1)S(1)}) fusion(f32[640,64]{1,0:T(8,128)S(1)} %get-tuple-element.153, f32[640,896]{1,0:T(8,128)S(1)} %get-tuple-element.151, f32[640,64]{1,0:T(8,128)S(1)} %get-tuple-element.154, f32[640,896]{1,0:T(8,128)S(1)} %get-tuple-element.152, ...), kind=kOutput, calls=%fused_computation.46 | convolution fusion | flops 3162931200 | bytes 17121280 | tf_op jit(solution)/shard_map/dot_general | solution.py:55
  208.8 6.5 %convolution_convert_fusion.1 = bf16[2560,960]{1,0:T(8,128)(2,1)} fusion(bf16[640,2560]{1,0:T(8,128)(2,1)S(1)} %bitcast.201, bf16[640,960]{1,0:T(8,128)(2,1)S(1)} %get-tuple-element.150), kind=kOutput, calls=%fused_computation.11 | convolution fusion | flops 3148185600 | bytes 9420800 | tf_op jit(solution)/shard_map/dot_general | solution.py:55
  221.8 12.9 %convolution_convert_fusion = bf16[2560,1920]{1,0:T(8,128)(2,1)} fusion(bf16[640,2560]{1,0:T(8,128)(2,1)} %bitcast.199, bf16[640,1920]{1,0:T(8,128)(2,1)} %concatenate.63), kind=kOutput, calls=%fused_computation | convolution fusion | flops 6296371200 | bytes 15564800 | tf_op jit(solution)/shard_map/dot_general | solution.py:55
  234.8 10.7 %fusion.7 = bf16[640,2560]{1,0:T(8,128)(2,1)S(1)} fusion(bf16[640,1920]{1,0:T(8,128)(2,1)} %concatenate.63, bf16[2560,2944]{1,0:T(8,128)(2,1)} %bitcast.196), kind=kOutput, calls=%fused_computation.12 | convolution fusion | flops 6293094400 | bytes 15564800 | tf_op jit(solution)/shard_map/dot_general | solution.py:55
  249.6 24.5 %shard_map.349 = f32[160,2560]{1,0:T(8,128)S(1)} custom-call(bf16[4,160,2560]{2,1,0:T(8,128)(2,1)S(1)} %bitcast.161), custom_call_target="tpu_custom_call" | custom-call | tf_op jit(solution)/shard_map/pallas_call | solution.py:80
  274.1 6.5 %convolution_convert_fusion.3 = bf16[640,2560]{1,0:T(8,128)(2,1)S(1)} fusion(bf16[640,960]{1,0:T(8,128)(2,1)S(1)} %copy-done.43, bf16[2560,2944]{1,0:T(8,128)(2,1)} %bitcast.197), kind=kOutput, calls=%fused_computation.14 | convolution fusion | flops 3147366400 | bytes 9748480 | tf_op jit(solution)/shard_map/dot_general | solution.py:55
  280.6 25.6 %shard_map.348 = f32[160,2560]{1,0:T(8,128)S(1)} custom-call(bf16[4,160,2560]{2,1,0:T(8,128)(2,1)S(1)} %bitcast.162), custom_call_target="tpu_custom_call" | custom-call | tf_op jit(solution)/shard_map/pallas_call | solution.py:80
  310.4 20.5 %shard_map.350 = bf16[4,160,2560]{2,1,0:T(8,128)(2,1)S(1)} custom-call(bf16[160,2560]{1,0:T(8,128)(2,1)S(1)} %get-tuple-element.144.x_ref), custom_call_target="tpu_custom_call" | custom-call | tf_op jit(solution)/shard_map/pallas_call | solution.py:80
  334.5 9.9 %shard_map.351 = bf16[4,160,320]{2,1,0:T(8,128)(2,1)S(1)} custom-call(bf16[4,160,320]{2,1,0:T(8,128)(2,1)S(1)} %bitcast.166), custom_call_target="tpu_custom_call" | custom-call | tf_op jit(solution)/shard_map/pallas_call | solution.py:80
  349.5 5.6 %fusion.4 = (f32[5,160]{1,0:T(8,128)S(1)}, f32[5,160,2560]{2,1,0:T(8,128)}) fusion(f32[2560,160,5]{0,1,2:T(8,128)S(1)} %fusion.61, f32[5,160]{1,0:T(8,128)S(1)} %slice_reduce_fusion, bf16[5,160,256]{2,1,0:T(8,128)(2,1)S(1)} %copy-done.25, bf16[2560,256,1]{1,0,2:T(8,128)(2,1)S(1)} %bitcast.170, pred[160,2560]{1,0:T(8,128)(4,1)S(1)} %fusion.39), kind=kOutput, calls=%fused_computation.7 | convolution fusion | flops 1056767232 | bytes 18520320 | tf_op jit(solution)/shard_map/hcd,kd->hck/dot_general | solution.py:1052
  355.1 6.4 %fusion.6 = bf16[5,160,2560]{2,1,0:T(8,128)(2,1)S(1)} fusion(f32[5,160,2560]{2,1,0:T(8,128)} %get-tuple-element.171, f32[2560,160,5]{0,1,2:T(8,128)} %copy-done.3, f32[5,160]{1,0:T(8,128)S(1)} %get-tuple-element.170), kind=kLoop, calls=%fused_computation.9 | loop fusion | flops 6144000 | bytes 20483200 | tf_op jit(solution)/shard_map/convert_element_type | solution.py:1057
  368.3 5.3 fusion.19
  378.1 17.4 %shard_map.353 = f32[160,256]{1,0:T(8,128)S(1)} custom-call(bf16[4,4,160,256]{3,2,1,0:T(8,128)(2,1)S(1)} %bitcast.160), custom_call_target="tpu_custom_call" | custom-call | tf_op jit(solution)/shard_map/pallas_call | solution.py:80
  396.4 6.7 %shard_map.354 = bf16[4,160,384]{2,1,0:T(8,128)(2,1)S(1)} custom-call(bf16[4,160,384]{2,1,0:T(8,128)(2,1)S(1)} %pad_maximum_fusion.3.x_ref), custom_call_target="tpu_custom_call" | custom-call | tf_op jit(solution)/shard_map/pallas_call | solution.py:80
  406.6 26.8 %shard_map.355 = f32[160,2560]{1,0:T(8,128)S(1)} custom-call(bf16[4,160,2560]{2,1,0:T(8,128)(2,1)S(1)} %bitcast.163), custom_call_target="tpu_custom_call" | custom-call | tf_op jit(solution)/shard_map/pallas_call | solution.py:80
  441.3 6.3 %copy.170 = bf16[2560,768]{1,0:T(8,128)(2,1)} copy(bf16[2560,768]{0,1:T(8,128)(2,1)} %pad_maximum_fusion) | data formatting | bytes 7864320 | tf_op jit(solution)/shard_map/concatenate | solution.py:1080
  449.7 27.8 %shard_map.356 = f32[160,768]{1,0:T(8,128)S(1)} custom-call(bf16[4,4,160,768]{3,2,1,0:T(8,128)(2,1)S(1)} %bitcast.159), custom_call_target="tpu_custom_call" | custom-call | tf_op jit(solution)/shard_map/pallas_call | solution.py:80
  477.6 6.4 %shard_map.357 = bf16[4,48,768]{2,1,0:T(8,128)(2,1)S(1)} custom-call(bf16[4,48,768]{2,1,0:T(8,128)(2,1)S(1)} %pad.41.x_ref), custom_call_target="tpu_custom_call" | custom-call | tf_op jit(solution)/shard_map/pallas_call | solution.py:80
  487.2 5.0 shard_map.358
  511.9 8.3 %shard_map.360 = bf16[4,48,960]{2,1,0:T(8,128)(2,1)S(1)} custom-call(bf16[4,48,960]{2,1,0:T(8,128)(2,1)S(1)} %pad.44.x_ref), custom_call_target="tpu_custom_call" | custom-call | tf_op jit(solution)/shard_map/pallas_call | solution.py:80
  524.3 11.6 %shard_map.359 = bf16[4,48,1920]{2,1,0:T(8,128)(2,1)S(1)} custom-call(bf16[4,48,1920]{2,1,0:T(8,128)(2,1)S(1)} %pad.43.x_ref), custom_call_target="tpu_custom_call" | custom-call | tf_op jit(solution)/shard_map/pallas_call | solution.py:80
  540.9 6.9 %multiply_subtract_fusion = (f32[40,2,3840]{2,1,0:T(2,128)}, f32[40,2,3840]{2,1,0:T(2,128)}, f32[40,2,3840]{2,1,0:T(2,128)}) fusion(f32[40,2,3840]{2,1,0:T(2,128)S(1)} %copy-done.10, f32[40,2,3840]{2,1,0:T(2,128)} %reshape.332, f32[40,2,3840]{2,1,0:T(2,128)} %param.31, f32[40,2,3840]{2,1,0:T(2,128)} %param.37), kind=kLoop, calls=%fused_computation.79 | loop fusion | flops 4608000 | bytes 8601600 | tf_op jit(solution)/shard_map/sub | solution.py:910
  (242 shorter events, 96.6 us)
Async XLA Ops:
  7.2 2.7 copy-start.9
  7.2 503.6 %reduce-scatter.5.cloned.1.call-start = ((), (), s32[]{:S(2)}) async-start(), calls=%async_computation.3 | async-start | bytes 5570560 | tf_op jit(solution)/shard_map/reduce_scatter | solution.py:1033
  7.3 6.1 %copy-start.36 = (f32[64]{0:T(128)}, f32[64]{0:T(128)S(1)}, u32[]{:S(2)}) copy-start(f32[64]{0:T(128)S(1)} %multiply_power_fusion) | copy-start | bytes 772
  14.6 4.2 copy-start.22
  207.7 9.9 %copy-start.17 = (bf16[640,960]{1,0:T(8,128)(2,1)}, bf16[640,960]{1,0:T(8,128)(2,1)S(1)}, u32[]{:S(2)}) copy-start(bf16[640,960]{1,0:T(8,128)(2,1)S(1)} %get-tuple-element.149) | copy-start | bytes 3686404
  215.3 307.9 %reduce-scatter.3.cloned.1.call-start = ((), (), s32[]{:S(2)}) async-start(), calls=%async_computation.2 | async-start | bytes 10444800 | tf_op jit(solution)/shard_map/reduce_scatter | solution.py:1041
  249.6 24.5 %copy-start.43 = (bf16[640,960]{1,0:T(8,128)(2,1)S(1)}, bf16[640,960]{1,0:T(8,128)(2,1)}, u32[]{:S(2)}) copy-start(bf16[640,960]{1,0:T(8,128)(2,1)} %copy-done.42) | copy-start | bytes 3686404
  280.6 25.6 %copy-start.5 = (f32[160,2560]{1,0:T(8,128)S(1)}, f32[160,2560]{1,0:T(8,128)}, u32[]{:S(2)}) copy-start(f32[160,2560]{1,0:T(8,128)} %get-tuple-element.30) | copy-start | bytes 4915204
  306.3 127.3 %copy-start.33 = (f32[2560]{0:T(1024)}, f32[2560]{0:T(1024)S(1)}, u32[]{:S(2)}) copy-start(f32[2560]{0:T(1024)S(1)} %get-tuple-element.124) | copy-start | bytes 30724
  310.4 22.3 %copy-start.35 = (bf16[4,4,160,768]{3,2,1,0:T(8,128)(2,1)S(1)}, bf16[4,4,160,768]{3,2,1,0:T(8,128)(2,1)}, u32[]{:S(2)}) copy-start(bf16[4,4,160,768]{3,2,1,0:T(8,128)(2,1)} %get-tuple-element.34) | copy-start | bytes 11796484
  344.4 3.2 copy-start.13
  349.0 6.1 %copy-start.3 = (f32[2560,160,5]{0,1,2:T(8,128)}, f32[2560,160,5]{0,1,2:T(8,128)S(1)}, u32[]{:S(2)}) copy-start(f32[2560,160,5]{0,1,2:T(8,128)S(1)} %fusion.61) | copy-start | bytes 24576004
  364.0 4.3 copy-start.16
  377.4 18.1 %copy-start.37 = (f32[64]{0:T(128)S(1)}, f32[64]{0:T(128)}, u32[]{:S(2)}) copy-start(f32[64]{0:T(128)} %copy-done.36) | copy-start | bytes 772
  378.1 18.2 %slice-start = ((bf16[160,5,256]{2,0,1:T(8,128)(2,1)}), bf16[160,4,256]{2,0,1:T(8,128)(2,1)S(1)}, s32[]{:S(2)}) async-start(bf16[160,5,256]{2,0,1:T(8,128)(2,1)} %copy-done.16), calls=%async_computation.4 | async-start | bytes 655360 | tf_op jit(solution)/shard_map/slice | solution.py:928
  406.5 26.8 %copy-start.4 = (f32[160,2560]{1,0:T(8,128)S(1)}, f32[160,2560]{1,0:T(8,128)}, u32[]{:S(2)}) copy-start(f32[160,2560]{1,0:T(8,128)} %tokens.1) | copy-start | bytes 4915204
  496.3 10.0 %copy-start.18 = (f32[1280,40]{0,1:T(8,128)S(1)}, f32[1280,40]{0,1:T(8,128)}, u32[]{:S(2)}) copy-start(f32[1280,40]{0,1:T(8,128)} %param.24) | copy-start | bytes 614404
  496.3 10.0 %copy-start.32 = (f32[40,256]{1,0:T(8,128)S(1)}, f32[40,256]{1,0:T(8,128)}, u32[]{:S(2)}) copy-start(f32[40,256]{1,0:T(8,128)} %reshape.328) | copy-start | bytes 122884
  499.3 9.0 %copy-start.19 = (f32[40,1280]{1,0:T(8,128)S(1)}, f32[40,1280]{1,0:T(8,128)}, u32[]{:S(2)}) copy-start(f32[40,1280]{1,0:T(8,128)} %param.22) | copy-start | bytes 614404
  499.3 9.0 %copy-start.29 = (f32[40,1280]{1,0:T(8,128)S(1)}, f32[40,1280]{1,0:T(8,128)}, u32[]{:S(2)}) copy-start(f32[40,1280]{1,0:T(8,128)} %param.28) | copy-start | bytes 614404
  499.3 9.0 %copy-start.30 = (f32[40,1280]{1,0:T(8,128)S(1)}, f32[40,1280]{1,0:T(8,128)}, u32[]{:S(2)}) copy-start(f32[40,1280]{1,0:T(8,128)} %param.34) | copy-start | bytes 614404
  501.2 8.0 %copy-start.8 = (f32[160,2560]{1,0:T(8,128)S(1)}, f32[160,2560]{1,0:T(8,128)}, u32[]{:S(2)}) copy-start(f32[160,2560]{1,0:T(8,128)} %get-tuple-element.145) | copy-start | bytes 4915204
  501.2 8.0 %copy-start.34 = (f32[2560]{0:T(1024)S(1)}, f32[2560]{0:T(1024)}, u32[]{:S(2)}) copy-start(f32[2560]{0:T(1024)} %copy-done.33) | copy-start | bytes 30724
  537.5 3.5 copy-start.10
  (23 other events, 36.0 us)
Sparse Core Ops, SparseCore 0:
  215.4 77.4 reduce-scatter.4
  296.4 88.3 reduce-scatter.2

commit v3 on v2

v3 whole, which is shorter than its diff:
```python
import jax
import jax.numpy as jnp
from jax import lax
from jax.experimental import pallas as pl
from jax.experimental.pallas import tpu as pltpu
from jax.sharding import Mesh
from jax.sharding import PartitionSpec as P

D = 2560
H = 10
HD = 256
FF = 7680
WINDOW = 2048
STEP = 10

eps_norm = 1e-06
masked_fill = -1e30
first_decay = 0.9
second_decay = 0.95
adam_eps = 1e-08
weight_decay = 0.1
gain_rate = 0.2

MESH = pl.DeviceIdType.MESH
LOW = jnp.bfloat16
F32 = jnp.float32
RING = 4
BLOCK = 160
HALF = BLOCK // 2
PART = 48
OWN = 40
PAD = 48
MAIN = 896
TAIL = 64


def step(axis, distance):
    return lax.rem(lax.axis_index(axis) + (RING + distance), RING)


def sibling():
    return {"tensor": 1 - lax.axis_index("tensor")}


def greet(peers):
    barrier = pltpu.get_barrier_semaphore()
    for peer in peers:
        pl.semaphore_signal(barrier, inc=1, device_id=peer, device_id_type=MESH)
    pl.semaphore_wait(barrier, len(peers))


def dot(left_side, right_side, contract):
    return lax.dot_general(
        left_side, right_side, ((contract[:1], contract[1:]), ((), ())), preferred_element_type=F32
    )


class Mover:
    def __init__(self, send_sem, recv_sem):
        self.send_sem, self.recv_sem, self.pending = send_sem, recv_sem, []

    def copy(self, src, dst, peer):
        index = len(self.pending)
        one = pltpu.make_async_remote_copy(
            src_ref=src,
            dst_ref=dst,
            send_sem=self.send_sem.at[index],
            recv_sem=self.recv_sem.at[index],
            device_id=peer,
            device_id_type=MESH,
        )
        one.start()
        self.pending.append(one)
        return one

    def finish(self):
        for one in self.pending:
            one.wait_send()


def advance(steps):
    next(steps, None)


def plane_peers(axes):
    return [{axis: step(axis, d)} for axis in axes for d in (-1, 1)]


def swap_kernel(x_ref, o_ref, send_sem, recv_sem):
    greet([sibling()])
    mover = Mover(send_sem, recv_sem)
    mover.copy(x_ref, o_ref, sibling()).wait_recv()
    mover.finish()


def swap_cores(x, ident):
    return pl.pallas_call(
        swap_kernel,
        out_shape=jax.ShapeDtypeStruct(x.shape, x.dtype),
        in_specs=[pl.BlockSpec(memory_space=pltpu.VMEM)],
        out_specs=pl.BlockSpec(memory_space=pltpu.VMEM),
        scratch_shapes=[pltpu.SemaphoreType.DMA((1,)), pltpu.SemaphoreType.DMA((1,))],
        compiler_params=pltpu.CompilerParams(collective_id=ident, has_side_effects=True),
    )(x)


def exchange_steps(mover, src, dst):
    me = lax.axis_index("z")
    copies = [
        mover.copy(src.at[step("z", d)], dst.at[me], {"z": step("z", d)}) for d in (2, 1, 3)
    ]
    yield
    for copy in copies:
        copy.wait_recv()


def core_rows():
    base = pl.multiple_of(lax.axis_index("tensor") * HALF, 16)
    return (
        pl.ds(base, HALF),
        pl.ds(base, PART),
        pl.ds(pl.multiple_of(base + PART, 16), HALF - PART),
        pl.ds(pl.multiple_of(HALF - base, 16), HALF),
    )


def gather_steps(mover, x, out):
    me, left, right, far = (step("z", d) for d in (0, -1, 1, 2))
    half, first, last, _ = core_rows()
    to_right = mover.copy(x.at[half], out.at[me, half], {"z": right})
    to_left = mover.copy(x.at[half], out.at[me, half], {"z": left})
    yield
    to_right.wait_recv()
    on_right = mover.copy(out.at[left, first], out.at[left, first], {"z": right})
    shares = [mover.copy(out.at[left, half], out.at[left, half], sibling())]
    to_left.wait_recv()
    on_left = mover.copy(out.at[right, last], out.at[right, last], {"z": left})
    shares.append(mover.copy(out.at[right, half], out.at[right, half], sibling()))
    yield
    on_right.wait_recv()
    on_left.wait_recv()
    shares.append(mover.copy(out.at[far, half], out.at[far, half], sibling()))
    yield
    for copy in shares:
        copy.wait_recv()


def cut_rows(which, cut):
    base, size = (0, cut) if which == 0 else (cut, BLOCK - cut)
    part = -(-size // 32) * 16
    return pl.ds(base, size), pl.ds(base, part), pl.ds(base + part, size - part)


def plane_gather_steps(mover, axes, x, out, cut=HALF, order=(0, 1), share=False):
    a, b = (lax.axis_index(axis) for axis in axes)
    state = {}
    for which, axis in enumerate(axes):
        rows = cut_rows(which, cut)[0]
        place = (lambda i, r: out.at[i, b, r]) if which == 0 else (lambda i, r: out.at[a, i, r])
        me = (a, b)[which]
        to_right = mover.copy(x.at[rows], place(me, rows), {axis: step(axis, 1)})
        to_left = mover.copy(x.at[rows], place(me, rows), {axis: step(axis, -1)})
        state[which] = (axis, place, to_right, to_left)
    yield
    passed = {}
    for which in order:
        axis, place, to_right, to_left = state[which]
        _, first, last = cut_rows(which, cut)
        left, right = step(axis, -1), step(axis, 1)
        to_right.wait_recv()
        on_right = mover.copy(place(left, first), place(left, first), {axis: right})
        to_left.wait_recv()
        on_left = mover.copy(place(right, last), place(right, last), {axis: left})
        passed[which] = (on_right, on_left)
    yield
    state = {}
    shares = []

    def give(piece):
        if share:
            shares.append(mover.copy(piece, piece, sibling()))

    for which in order:
        axis, other = axes[which], axes[1 - which]
        rows = cut_rows(which, cut)[0]
        if which == 0:
            place = lambda i, lo, n, rows=rows: out.at[pl.ds(lo, n), i, rows]
        else:
            place = lambda i, lo, n, rows=rows: out.at[i, pl.ds(lo, n), rows]
        me = (b, a)[which]
        for copy in passed[which]:
            copy.wait_recv()
        to_right = mover.copy(place(me, 0, 4), place(me, 0, 4), {other: step(other, 1)})
        to_left = mover.copy(place(me, 0, 4), place(me, 0, 4), {other: step(other, -1)})
        give(place(me, 0, 4))
        state[which] = (other, place, to_right, to_left)
        yield
    ends = []
    for which in order:
        other, place, to_right, to_left = state[which]
        left, right = step(other, -1), step(other, 1)
        to_right.wait_recv()
        ends.append(mover.copy(place(left, 0, 2), place(left, 0, 2), {other: right}))
        give(place(left, 0, 4))
        to_left.wait_recv()
        ends.append(mover.copy(place(right, 2, 2), place(right, 2, 2), {other: left}))
        give(place(right, 0, 4))
        yield
    for copy in ends:
        copy.wait_recv()
    for which in order:
        other, place, _, _ = state[which]
        give(place(step(other, 2), 0, 4))
    for copy in shares:
        copy.wait_recv()


def lanes(shape):
    return lax.broadcasted_iota(jnp.int32, shape, len(shape) - 1)


def turn(values, cos, sin):
    return values * cos + pltpu.roll(values, 64, 1) * sin


def whole_rows(blocks, stage, dst):
    for i in range(RING):
        stage[i * OWN : (i + 1) * OWN] = blocks[i].astype(F32)[:OWN]
    dst[...] = stage[...].astype(LOW)


def first_kernel(
    attn_rows,
    feed_rows,
    tokens,
    dy,
    cos_ref,
    sin_ref,
    cos_kv,
    sin_kv,
    feed_full,
    attn_full,
    normed_one,
    dy_all,
    query,
    keyvalue,
    log_total,
    att_slice,
    residual,
    normed_two,
    attended,
    gain_ref,
    send_sem,
    recv_sem,
    local_sem,
    attn_got,
    attn_mine,
    attn_stage,
    feed_got,
    feed_mine,
    feed_stage,
    unit_low,
    unit_all,
    qkv_send,
    qkv_got,
    kv_own,
    scores,
    att_send,
    part,
    other,
    total,
    part_a,
    part_b,
    from_left,
    from_right,
    normed_low,
):
    z, x, y, core = (lax.axis_index(axis) for axis in ("z", "x", "dp", "tensor"))
    left, right, far = (step("z", d) for d in (-1, 1, 2))
    half, _, _, their_half = core_rows()
    plane = ("dp", "x")
    greet(
        [{"z": step("z", d)} for d in (1, 2, 3)] + plane_peers(("dp", "x")) + [sibling()]
    )
    mover = Mover(send_sem, recv_sem)

    attn_swap = exchange_steps(mover, attn_rows, attn_got)
    advance(attn_swap)
    values = tokens[...]
    unit = values * lax.rsqrt(jnp.mean(values * values, axis=-1, keepdims=True) + eps_norm)
    unit_low[...] = unit.astype(LOW)
    unit_gather = gather_steps(mover, unit_low, unit_all)
    advance(unit_gather)
    feed_swap = exchange_steps(mover, feed_rows, feed_got)
    advance(feed_swap)
    unit_all[z] = unit_low[...]
    attn_got[z] = attn_rows[z]
    advance(attn_swap)
    whole_rows(attn_got, attn_stage, attn_mine)
    attn_gather = plane_gather_steps(mover, plane, attn_mine, attn_full)
    advance(attn_gather)
    attn_full[y, x] = attn_mine[...]
    advance(unit_gather)
    advance(attn_gather)
    advance(attn_gather)
    advance(attn_gather)
    feed_got[z] = feed_rows[z]
    advance(unit_gather)
    advance(feed_swap)
    whole_rows(feed_got, feed_stage, feed_mine)
    feed_own = pltpu.make_async_copy(feed_mine, feed_full.at[y, x], local_sem.at[0])
    feed_own.start()
    advance(attn_gather)
    advance(attn_gather)
    feed_gather = plane_gather_steps(mover, plane, feed_mine, feed_full, cut=64, order=(1, 0))
    advance(feed_gather)
    dy_gather = gather_steps(mover, dy, dy_all)
    advance(dy_gather)
    dy_own = pltpu.make_async_copy(dy, dy_all.at[z], local_sem.at[1])
    dy_own.start()
    advance(unit_gather)
    advance(attn_gather)

    scale_cols = attn_full[:, :, :, 640:768].reshape(D, 128)
    pick = (lanes((8, 128)) == 64 + lax.broadcasted_iota(jnp.int32, (8, 128), 0)).astype(LOW)
    gain_ref[...] = 1.0 + dot(pick, scale_cols, (1, 1))
    qkv_weight = attn_full[:, :, :, :384].reshape(D, 384)
    copies = []
    for d in (2, 1, 3, 0):
        block = step("z", d)
        normed = (unit_all[block].astype(F32) * gain_ref[0:1, :]).astype(LOW)
        normed_one[block] = normed
        qkv_send[block] = dot(normed, qkv_weight, (1, 0)).astype(LOW)
        if d:
            copies.append(mover.copy(qkv_send.at[block], qkv_got.at[z], {"z": block}))
    qkv_got[z] = qkv_send[z]
    advance(feed_gather)
    feed_own.wait()
    for copy in copies:
        copy.wait_recv()
    low_lanes = lanes((BLOCK, 128)) < TAIL
    cos, sin = cos_ref[...], sin_ref[...]

    def joined(i, offset):
        one, two = (qkv_got[i + k, :, 256:384].astype(F32) for k in (0, 1))
        if offset == 0:
            return jnp.where(low_lanes, one, pltpu.roll(two, TAIL, 1))
        return jnp.where(low_lanes, pltpu.roll(one, TAIL, 1), two)

    kv_own[:, :128] = turn(joined(0, 1), cos_kv[...], sin_kv[...]).astype(LOW)
    kv_own[:, 128:] = joined(2, 1).astype(LOW)
    kv_mine = keyvalue.at[core]
    kv_gather = plane_gather_steps(mover, ("x", "z"), kv_own, kv_mine, share=True)
    advance(kv_gather)
    keyvalue[core, x, z] = kv_own[...]
    scale = HD ** (-0.5)
    for h in range(4):
        first = qkv_got[h, :, :128].astype(F32)
        query[h, :, :128] = (turn(first, cos, sin) * scale).astype(LOW)
        query[h, :, 128:] = (qkv_got[h, :, 128:256].astype(F32) * scale).astype(LOW)
    query[4, :, :128] = (turn(joined(0, 0), cos, sin) * scale).astype(LOW)
    query[4, :, 128:] = (joined(2, 0) * scale).astype(LOW)
    advance(kv_gather)
    advance(feed_gather)
    advance(kv_gather)
    advance(kv_gather)
    advance(kv_gather)
    advance(kv_gather)
    advance(feed_gather)
    advance(dy_gather)
    advance(kv_gather)

    start = (x * RING + z) * BLOCK
    chunk = RING * BLOCK

    def one_head(h, carry):
        queries = query[h]
        top = jnp.full((BLOCK, 1), masked_fill, F32)
        for k in range(RING):
            rows = keyvalue[0, k].reshape(chunk, HD)
            tile = dot(queries, rows, (1, 1))
            gap = (start - k * chunk) + (
                lax.broadcasted_iota(jnp.int32, tile.shape, 0) - lanes(tile.shape)
            )
            tile = jnp.where((gap >= 0) & (gap < WINDOW), tile, masked_fill)
            scores[:, k * chunk : (k + 1) * chunk] = tile
            top = jnp.maximum(top, jnp.max(tile, axis=-1, keepdims=True))
        sums = jnp.zeros((BLOCK, 1), F32)
        for k in range(RING):
            tile = jnp.exp(scores[:, k * chunk : (k + 1) * chunk] - top)
            scores[:, k * chunk : (k + 1) * chunk] = tile
            sums = sums + jnp.sum(tile, axis=-1, keepdims=True)
        inverse = 1.0 / sums
        result = jnp.zeros((BLOCK, HD), F32)
        for k in range(RING):
            low = (scores[:, k * chunk : (k + 1) * chunk] * inverse).astype(LOW)
            result = result + dot(low, keyvalue[1, k].reshape(chunk, HD), (1, 0))
        attended[h] = result
        log_total[h] = jnp.broadcast_to(top + jnp.log(sums), (BLOCK, 128))
        return carry

    lax.fori_loop(0, 5, one_head, 0)
    for j in range(RING):
        att_send[j, :, :256] = attended[j].astype(LOW)
        tile = attended[4, :, (j // 2) * 128 : (j // 2 + 1) * 128]
        tile = pltpu.roll(tile, TAIL, 1) if j % 2 else tile
        att_send[j, :, 256:] = jnp.where(low_lanes, tile, 0.0).astype(LOW)
    att_swap = exchange_steps(mover, att_send, att_slice)
    advance(att_swap)
    att_slice[z] = att_send[z]
    advance(dy_gather)
    advance(att_swap)

    out_weight = attn_full[:, :, :, 384:].reshape(D, 384)
    blocks = (far, right, left, z)
    shares = []
    for slot, block in enumerate(blocks):
        part[block] = dot(att_slice[block], out_weight, (1, 1)).astype(LOW)
        shares.append(mover.copy(part.at[block, their_half], other.at[slot], sibling()))

    def both(slot):
        return part[blocks[slot], half].astype(F32) + other[slot].astype(F32)

    shares[0].wait_recv()
    total[0] = both(0).astype(LOW)
    far_right = mover.copy(total.at[0, pl.ds(0, PART)], part_a, {"z": right})
    far_left = mover.copy(total.at[0, pl.ds(PART, HALF - PART)], part_b, {"z": left})
    shares[1].wait_recv()
    shares[2].wait_recv()
    far_right.wait_recv()
    summed = both(1)
    total[1, :PART] = (summed[:PART] + part_a[...].astype(F32)).astype(LOW)
    total[1, PART:] = summed[PART:].astype(LOW)
    to_right = mover.copy(total.at[1], from_left, {"z": right})
    far_left.wait_recv()
    summed = both(2)
    total[2, :PART] = summed[:PART].astype(LOW)
    total[2, PART:] = (summed[PART:] + part_b[...].astype(F32)).astype(LOW)
    to_left = mover.copy(total.at[2], from_right, {"z": left})
    shares[3].wait_recv()
    to_right.wait_recv()
    to_left.wait_recv()
    rows = tokens[half, :] + (
        both(3) + from_left[...].astype(F32) + from_right[...].astype(F32)
    )
    residual[half, :] = rows
    res_share = mover.copy(residual.at[half], residual.at[half], sibling())

    def normed_rows(rows):
        unit = rows * lax.rsqrt(jnp.mean(rows * rows, axis=-1, keepdims=True) + eps_norm)
        return (unit * gain_ref[1:2, :]).astype(LOW)

    normed_low[half, :] = normed_rows(rows)
    normed_gather = gather_steps(mover, normed_low, normed_two)
    advance(normed_gather)
    res_share.wait_recv()
    normed_low[their_half, :] = normed_rows(residual[their_half, :])
    normed_two[z] = normed_low[...]
    advance(normed_gather)
    advance(feed_gather)
    advance(normed_gather)
    advance(feed_gather)
    advance(dy_gather)
    advance(normed_gather)
    advance(feed_gather)
    dy_own.wait()
    mover.finish()


def run_first(*operands):
    out = {
        "feed_full": ((RING, RING, BLOCK, 2944), LOW, pl.ANY),
        "attn_full": ((RING, RING, BLOCK, 768), LOW, pltpu.VMEM),
        "normed_one": ((RING, BLOCK, D), LOW, pltpu.VMEM),
        "dy_all": ((RING, BLOCK, D), LOW, pl.ANY),
        "query": ((5, BLOCK, HD), LOW, pltpu.VMEM),
        "keyvalue": ((2, RING, RING, BLOCK, HD), LOW, pltpu.VMEM),
        "log_total": ((5, BLOCK, 128), F32, pltpu.VMEM),
        "att_slice": ((RING, BLOCK, 384), LOW, pltpu.VMEM),
        "residual": ((BLOCK, D), F32, pltpu.VMEM),
        "normed_two": ((RING, BLOCK, D), LOW, pltpu.VMEM),
        "attended": ((5, BLOCK, HD), F32, pltpu.VMEM),
        "gains": ((8, D), F32, pltpu.VMEM),
    }
    spaces = [pltpu.VMEM, pltpu.VMEM, pltpu.VMEM, pl.ANY] + [pltpu.VMEM] * 4
    copies = 120
    results = pl.pallas_call(
        first_kernel,
        out_shape=[jax.ShapeDtypeStruct(shape, kind) for shape, kind, _ in out.values()],
        in_specs=[pl.BlockSpec(memory_space=space) for space in spaces],
        out_specs=[pl.BlockSpec(memory_space=space) for _, _, space in out.values()],
        scratch_shapes=[
            pltpu.SemaphoreType.DMA((copies,)),
            pltpu.SemaphoreType.DMA((copies,)),
            pltpu.SemaphoreType.DMA((2,)),
            pltpu.VMEM((RING, PAD, 768), LOW),
            pltpu.VMEM((BLOCK, 768), LOW),
            pltpu.VMEM((BLOCK, 768), F32),
            pltpu.VMEM((RING, PAD, 2944), LOW),
            pltpu.VMEM((BLOCK, 2944), LOW),
            pltpu.VMEM((BLOCK, 2944), F32),
            pltpu.VMEM((BLOCK, D), LOW),
            pltpu.VMEM((RING, BLOCK, D), LOW),
            pltpu.VMEM((RING, BLOCK, 384), LOW),
            pltpu.VMEM((RING, BLOCK, 384), LOW),
            pltpu.VMEM((BLOCK, HD), LOW),
            pltpu.VMEM((BLOCK, RING * RING * BLOCK), F32),
            pltpu.VMEM((RING, BLOCK, 384), LOW),
            pltpu.VMEM((RING, BLOCK, D), LOW),
            pltpu.VMEM((4, HALF, D), LOW),
            pltpu.VMEM((3, HALF, D), LOW),
            pltpu.VMEM((PART, D), LOW),
            pltpu.VMEM((HALF - PART, D), LOW),
            pltpu.VMEM((HALF, D), LOW),
            pltpu.VMEM((HALF, D), LOW),
            pltpu.VMEM((BLOCK, D), LOW),
        ],
        compiler_params=pltpu.CompilerParams(
            collective_id=1, has_side_effects=True, vmem_limit_bytes=60 * 1024 * 1024
        ),
    )(*operands)
    return dict(zip(out, results, strict=True))


def plane_reduce_steps(mover, axes, g, bufs, res, loads=None):
    far, side, near, far_two, side_two = bufs
    places = [lax.axis_index(axis) for axis in axes]

    def block(which, i, lo, n):
        rows = pl.ds(which * HALF, HALF)
        return g.at[i, pl.ds(lo, n), rows] if which == 0 else g.at[pl.ds(lo, n), i, rows]

    locals_ = []

    def load(src, dst):
        locals_.append(pltpu.make_async_copy(src, dst, loads.at[len(locals_)]))
        locals_[-1].start()
        return locals_[-1]

    first, sides, wanted = [], [], []
    for which, axis in enumerate(axes):
        right, left = step(axis, 1), step(axis, -1)
        far_place = step(axis, 2)
        first.append(
            (
                mover.copy(block(which, far_place, 0, 2), far.at[which, pl.ds(0, 2)], {axis: right}),
                mover.copy(block(which, far_place, 2, 2), far.at[which, pl.ds(2, 2)], {axis: left}),
            )
        )
        if loads is not None:
            wanted.append(
                (
                    load(block(which, right, 0, 2), near.at[which, 0]),
                    load(block(which, left, 2, 2), near.at[which, 1]),
                )
            )
    for which, axis in enumerate(axes):
        right, left = step(axis, 1), step(axis, -1)
        sides.append(
            [
                mover.copy(block(which, right, 2, 2), side.at[which, 0, pl.ds(2, 2)], {axis: right}),
                mover.copy(block(which, left, 0, 2), side.at[which, 1, pl.ds(0, 2)], {axis: left}),
            ]
        )
    yield
    owned = []
    for which, axis in enumerate(axes):
        for k, (d, lo) in enumerate(((1, 0), (-1, 2))):
            first[which][k].wait_recv()
            if loads is not None:
                wanted[which][k].wait()
                term = near[which, k]
            else:
                term = block(which, step(axis, d), lo, 2)[...]
            near[which, k] = (term.astype(F32) + far[which, lo : lo + 2].astype(F32)).astype(LOW)
            sides[which].append(
                mover.copy(near.at[which, k], side.at[which, k, pl.ds(lo, 2)], {axis: step(axis, d)})
            )
        if loads is not None:
            owned.append(load(block(which, places[which], 0, 4), far.at[which]))
    yield

    def summed(which, i):
        if loads is not None:
            term = far[which, i]
        else:
            rows = pl.ds(which * HALF, HALF)
            me = places[which]
            term = (g[me, i, rows] if which == 0 else g[i, me, rows])
        return (
            term.astype(F32) + side[which, 0, i].astype(F32) + side[which, 1, i].astype(F32)
        )

    second = []
    for which, axis in enumerate(axes):
        other = axes[1 - which]
        right, left = {other: step(other, 1)}, {other: step(other, -1)}
        for copy in sides[which]:
            copy.wait_recv()
        if loads is not None:
            owned[which].wait()
        far_two[which, 0] = summed(which, step(other, 2)).astype(LOW)
        upper, lower = pl.ds(0, PART), pl.ds(PART, HALF - PART)
        second.append(
            (
                mover.copy(far_two.at[which, 0, upper], far_two.at[which, 1, upper], right),
                mover.copy(far_two.at[which, 0, lower], far_two.at[which, 1, lower], left),
            )
        )
    yield
    last = []
    for which, axis in enumerate(axes):
        other = axes[1 - which]
        right, left = step(other, 1), step(other, -1)
        total = summed(which, right)
        second[which][0].wait_recv()
        side_two[which, 0, :PART] = (
            total[:PART] + far_two[which, 1, :PART].astype(F32)
        ).astype(LOW)
        side_two[which, 0, PART:] = total[PART:].astype(LOW)
        last.append(mover.copy(side_two.at[which, 0], side_two.at[which, 2], {other: right}))
        total = summed(which, left)
        second[which][1].wait_recv()
        side_two[which, 1, :PART] = total[:PART].astype(LOW)
        side_two[which, 1, PART:] = (
            total[PART:] + far_two[which, 1, PART:].astype(F32)
        ).astype(LOW)
        last.append(mover.copy(side_two.at[which, 1], side_two.at[which, 3], {other: left}))
    yield
    for which, axis in enumerate(axes):
        other = axes[1 - which]
        last[2 * which].wait_recv()
        last[2 * which + 1].wait_recv()
        res[which * HALF : (which + 1) * HALF] = (
            summed(which, lax.axis_index(other))
            + side_two[which, 2].astype(F32)
            + side_two[which, 3].astype(F32)
        )


def plane_reduce_scratch(columns):
    return [
        pltpu.VMEM((2, 4, HALF, columns), LOW),
        pltpu.VMEM((2, 2, 4, HALF, columns), LOW),
        pltpu.VMEM((2, 2, 2, HALF, columns), LOW),
        pltpu.VMEM((2, 2, HALF, columns), LOW),
        pltpu.VMEM((2, 4, HALF, columns), LOW),
        pltpu.VMEM((BLOCK, columns), F32),
    ]


def reduce_steps(mover, part, mine, bufs, out, make=None):
    other, total, part_a, part_b, from_left, from_right = bufs
    _, _, _, their_half = core_rows()
    me, left, right, far = (step("z", d) for d in (0, -1, 1, 2))
    blocks = (far, right, left, me)
    shares = []
    for slot, block in enumerate(blocks):
        if make is not None:
            make(block)
        shares.append(mover.copy(part.at[block, their_half], other.at[slot], sibling()))
    yield

    def both(slot):
        return mine(blocks[slot]).astype(F32) + other[slot].astype(F32)

    shares[0].wait_recv()
    total[0] = both(0).astype(LOW)
    far_right = mover.copy(total.at[0, pl.ds(0, PART)], part_a, {"z": right})
    far_left = mover.copy(total.at[0, pl.ds(PART, HALF - PART)], part_b, {"z": left})
    yield
    shares[1].wait_recv()
    shares[2].wait_recv()
    far_right.wait_recv()
    summed = both(1)
    total[1, :PART] = (summed[:PART] + part_a[...].astype(F32)).astype(LOW)
    total[1, PART:] = summed[PART:].astype(LOW)
    to_right = mover.copy(total.at[1], from_left, {"z": right})
    far_left.wait_recv()
    summed = both(2)
    total[2, :PART] = summed[:PART].astype(LOW)
    total[2, PART:] = (summed[PART:] + part_b[...].astype(F32)).astype(LOW)
    to_left = mover.copy(total.at[2], from_right, {"z": left})
    yield
    shares[3].wait_recv()
    to_right.wait_recv()
    to_left.wait_recv()
    out[...] = both(3) + from_left[...].astype(F32) + from_right[...].astype(F32)


def reduce_scratch():
    return [
        pltpu.VMEM((4, HALF, D), LOW),
        pltpu.VMEM((3, HALF, D), LOW),
        pltpu.VMEM((PART, D), LOW),
        pltpu.VMEM((HALF - PART, D), LOW),
        pltpu.VMEM((HALF, D), LOW),
        pltpu.VMEM((HALF, D), LOW),
    ]


def spread_rows(res, dst):
    for i in range(RING):
        rows = res[i * OWN : (i + 1) * OWN]
        dst[i] = jnp.concatenate([rows, jnp.zeros((PAD - OWN, rows.shape[1]), F32)]).astype(LOW)


def third_kernel(
    norm_part,
    feed_part,
    gateup_grads,
    cotangent,
    residual,
    gain_ref,
    attn_full,
    att_slice,
    query,
    keyvalue,
    log_total,
    attended,
    cos_ref,
    sin_ref,
    grad_rows,
    grad_out,
    grad_query,
    grad_kv,
    gateup_rows,
    output,
    send_sem,
    recv_sem,
    local_sem,
    norm_mine,
    feed_mine,
    grad_half,
    out_half,
    da_low,
    da_all,
    datt_send,
    datt_got,
    datt,
    delta,
    ds_all,
    p_all,
    dq,
    kv_pair,
    kv_in,
    *bufs,
):
    z, core = lax.axis_index("z"), lax.axis_index("tensor")
    x = lax.axis_index("x")
    half, _, _, their_half = core_rows()
    norm_bufs, out_bufs, rows_bufs = bufs[:6], bufs[6:12], bufs[12:17]
    rows_res = bufs[17]
    greet([{"z": step("z", d)} for d in (1, 2, 3)] + plane_peers(("dp", "x")) + [sibling()])
    mover = Mover(send_sem, recv_sem)
    norm_load = pltpu.make_async_copy(norm_part.at[:, half], norm_mine, local_sem.at[8])
    norm_load.start()
    feed_load = pltpu.make_async_copy(feed_part.at[:, half], feed_mine, local_sem.at[9])
    feed_load.start()
    norm_sum = reduce_steps(mover, norm_part, lambda i: norm_mine[i], norm_bufs, grad_half)
    advance(norm_sum)
    rows_sum = plane_reduce_steps(
        mover, ("dp", "x"), gateup_grads, rows_bufs, rows_res, loads=local_sem
    )
    advance(rows_sum)
    norm_load.wait()
    advance(norm_sum)
    advance(norm_sum)
    advance(norm_sum)

    rows = residual[half, :]
    inverse = lax.rsqrt(jnp.mean(rows * rows, axis=-1, keepdims=True) + eps_norm)
    unit = rows * inverse
    scaled = grad_half[...] * gain_ref[1:2, :]
    grad = cotangent[half, :] + inverse * (
        scaled - unit * jnp.mean(scaled * unit, axis=-1, keepdims=True)
    )
    grad_rows[...] = grad
    da_low[half, :] = grad.astype(LOW)
    da_share = mover.copy(da_low.at[half], da_low.at[half], sibling())
    da_gather = gather_steps(mover, da_low, da_all)
    advance(da_gather)
    feed_sum = reduce_steps(mover, feed_part, lambda i: feed_mine[i], out_bufs, out_half)
    da_share.wait_recv()
    da_all[z] = da_low[...]
    out_weight = attn_full[:, :, :, 384:].reshape(D, 384)
    datt_got[z] = dot(da_all[z], out_weight, (1, 0)).astype(LOW)
    advance(da_gather)
    advance(rows_sum)
    advance(da_gather)
    advance(da_gather)
    copies = []
    for d in (2, 1, 3):
        block = step("z", d)
        datt_send[block] = dot(da_all[block], out_weight, (1, 0)).astype(LOW)
        copies.append(mover.copy(datt_send.at[block], datt_got.at[z], {"z": block}))
    advance(feed_sum)
    slices = att_slice[...].reshape(RING * BLOCK, 384)
    wide = RING * BLOCK
    for i in range(RING):
        left_side = da_all[:, :, i * wide : (i + 1) * wide].reshape(wide, wide)
        grad_out[i] = dot(left_side, slices, (0, 0)).astype(LOW).reshape(RING, BLOCK, 384)
    for copy in copies:
        copy.wait_recv()
    feed_load.wait()
    advance(feed_sum)

    low_lanes = lanes((BLOCK, 128)) < TAIL
    for h in range(4):
        datt[h] = datt_got[h, :, :HD]
    for k in range(2):
        one, two = (datt_got[2 * k + i, :, HD:].astype(F32) for i in range(2))
        datt[4, :, k * 128 : (k + 1) * 128] = jnp.where(
            low_lanes, one, pltpu.roll(two, TAIL, 1)
        ).astype(LOW)
    for h in range(5):
        delta[h] = jnp.broadcast_to(
            jnp.sum(datt[h].astype(F32) * attended[h], axis=-1, keepdims=True), (BLOCK, 128)
        )
        dq[h] = jnp.zeros((BLOCK, HD), F32)
    start = (x * RING + z) * BLOCK
    chunk = RING * BLOCK

    def one_chunk(k, carry):
        keys = keyvalue[0, k].reshape(chunk, HD)
        values = keyvalue[1, k].reshape(chunk, HD)
        shape = (BLOCK, chunk)
        gap = (start - k * chunk) + (lax.broadcasted_iota(jnp.int32, shape, 0) - lanes(shape))
        visible = (gap >= 0) & (gap < WINDOW)

        def one_head(h, carry):
            scores = dot(query[h], keys, (1, 1))
            probs = jnp.where(visible, jnp.exp(scores - log_total[h, :, :1]), 0.0)
            grads = dot(datt[h], values, (1, 1))
            low = (probs * (grads - delta[h, :, :1])).astype(LOW)
            ds_all[h] = low
            p_all[h] = probs.astype(LOW)
            dq[h] = dq[h] + dot(low, keys, (1, 0))
            return carry

        lax.fori_loop(0, 5, one_head, 0)
        queries = query[...].reshape(5 * BLOCK, HD)
        outer = datt[...].reshape(5 * BLOCK, HD)
        kv_pair[0, k] = dot(ds_all[...].reshape(5 * BLOCK, chunk), queries, (0, 0)).astype(LOW).reshape(RING, BLOCK, HD)
        kv_pair[1, k] = dot(p_all[...].reshape(5 * BLOCK, chunk), outer, (0, 0)).astype(LOW).reshape(RING, BLOCK, HD)
        return carry

    lax.fori_loop(0, RING, one_chunk, 0)
    kv_swap = mover.copy(kv_pair.at[1 - core], kv_in, sibling())
    advance(feed_sum)
    advance(rows_sum)
    cos, sin = cos_ref[...], sin_ref[...]
    scale = HD ** (-0.5)
    for h in range(5):
        grad_query[h, :, :128] = turn(dq[h, :, :128] * scale, cos, -sin).astype(LOW)
        grad_query[h, :, 128:] = (dq[h, :, 128:] * scale).astype(LOW)
    kv_swap.wait_recv()
    grad_kv[...] = (kv_pair[core].astype(F32) + kv_in[...].astype(F32)).astype(LOW)
    advance(rows_sum)
    advance(feed_sum)
    output[half, :] = residual[half, :] + out_half[...]
    out_share = mover.copy(output.at[half], output.at[half], sibling())
    advance(rows_sum)
    spread_rows(rows_res, gateup_rows)
    out_share.wait_recv()
    mover.finish()


def fourth_kernel(
    grad_kv,
    grad_query,
    gateup_rows,
    down_grads,
    grad_out,
    attn_full,
    normed_one,
    grad_rows,
    tokens,
    gain_ref,
    cos_kv,
    sin_kv,
    grad_tokens,
    gateup_got,
    down_got,
    out_got,
    qkv_got,
    send_sem,
    recv_sem,
    local_sem,
    grad_send,
    grad_got,
    kv_low,
    part,
    grad_half,
    grad_qkv,
    down_send,
    out_send,
    qkv_send,
    *bufs,
):
    z = lax.axis_index("z")
    half, _, _, _ = core_rows()
    plane = ("dp", "x")
    sum_bufs = bufs[:6]
    kv_bufs, down_bufs, out_bufs, qkv_bufs = (bufs[6 + 6 * i : 12 + 6 * i] for i in range(4))
    greet([{"z": step("z", d)} for d in (1, 2, 3)] + plane_peers(plane) + [sibling()])
    mover = Mover(send_sem, recv_sem)
    kv_sum = plane_reduce_steps(mover, ("x", "z"), grad_kv, kv_bufs[:5], kv_bufs[5])
    advance(kv_sum)
    out_sum = plane_reduce_steps(mover, plane, grad_out, out_bufs[:5], out_bufs[5])
    down_sum = plane_reduce_steps(
        mover, plane, down_grads, down_bufs[:5], down_bufs[5], loads=local_sem
    )
    for k in range(5):
        grad_send_block(k, grad_query, grad_send)
    advance(kv_sum)
    advance(out_sum)
    advance(kv_sum)
    advance(out_sum)
    advance(kv_sum)
    advance(kv_sum)
    kv_rows = kv_bufs[5]
    kv_low[:, :128] = turn(kv_rows[:, :128], cos_kv[...], -sin_kv[...])
    kv_low[:, 128:] = kv_rows[:, 128:]
    low_lanes = lanes((BLOCK, 128)) < TAIL
    for j in range(RING):
        place = slice((j // 2) * 128, (j // 2 + 1) * 128)
        one = grad_query[4, :, place].astype(F32)
        two = kv_low[:, place]
        if j % 2:
            one = pltpu.roll(one, TAIL, 1)
        else:
            two = pltpu.roll(two, TAIL, 1)
        grad_send[j, :, HD:] = jnp.where(low_lanes, one, two).astype(LOW)
    swap = exchange_steps(mover, grad_send, grad_got)
    advance(swap)
    grad_got[z] = grad_send[z]
    advance(down_sum)
    advance(out_sum)
    gateup_swap = exchange_steps(mover, gateup_rows, gateup_got)
    advance(swap)

    qkv_weight = attn_full[:, :, :, :384].reshape(D, 384)

    def make(block):
        part[block] = dot(grad_got[block], qkv_weight, (1, 1)).astype(LOW)

    norm_sum = reduce_steps(mover, part, lambda i: part[i, half], sum_bufs, grad_half, make)
    advance(norm_sum)
    slices = grad_got[...].reshape(RING * BLOCK, 384)
    wide = RING * BLOCK
    for i in range(RING):
        left_side = normed_one[:, :, i * wide : (i + 1) * wide].reshape(wide, wide)
        grad_qkv[i] = dot(left_side, slices, (0, 0)).astype(LOW).reshape(RING, BLOCK, 384)
        if i == 0:
            advance(norm_sum)
    qkv_sum = plane_reduce_steps(mover, plane, grad_qkv, qkv_bufs[:5], qkv_bufs[5])
    advance(qkv_sum)
    advance(norm_sum)
    advance(out_sum)
    advance(down_sum)
    advance(gateup_swap)
    gateup_got[z] = gateup_rows[z]
    advance(qkv_sum)
    advance(out_sum)
    spread_rows(out_bufs[5], out_send)
    out_swap = exchange_steps(mover, out_send, out_got)
    advance(out_swap)
    out_got[z] = out_send[z]
    advance(down_sum)
    advance(qkv_sum)
    advance(norm_sum)
    rows = tokens[half, :]
    inverse = lax.rsqrt(jnp.mean(rows * rows, axis=-1, keepdims=True) + eps_norm)
    unit = rows * inverse
    scaled = grad_half[...] * gain_ref[0:1, :]
    grad_tokens[half, :] = grad_rows[...] + inverse * (
        scaled - unit * jnp.mean(scaled * unit, axis=-1, keepdims=True)
    )
    share = mover.copy(grad_tokens.at[half], grad_tokens.at[half], sibling())
    advance(qkv_sum)
    advance(down_sum)
    advance(qkv_sum)
    spread_rows(qkv_bufs[5], qkv_send)
    qkv_swap = exchange_steps(mover, qkv_send, qkv_got)
    advance(qkv_swap)
    qkv_got[z] = qkv_send[z]
    advance(down_sum)
    spread_rows(down_bufs[5], down_send)
    down_swap = exchange_steps(mover, down_send, down_got)
    advance(down_swap)
    down_got[z] = down_send[z]
    for steps in (gateup_swap, out_swap, qkv_swap, down_swap):
        advance(steps)
    share.wait_recv()
    mover.finish()


def grad_send_block(h, grad_query, grad_send):
    if h < 4:
        grad_send[h, :, :HD] = grad_query[h]


def call(kernel, ident, copies, out, scratch, operands, spaces):
    results = pl.pallas_call(
        kernel,
        out_shape=[jax.ShapeDtypeStruct(shape, kind) for shape, kind in out.values()],
        in_specs=[pl.BlockSpec(memory_space=space) for space in spaces],
        out_specs=[pl.BlockSpec(memory_space=pltpu.VMEM) for _ in out],
        scratch_shapes=[
            pltpu.SemaphoreType.DMA((copies,)),
            pltpu.SemaphoreType.DMA((copies,)),
            pltpu.SemaphoreType.DMA((10,)),
            *scratch,
        ],
        compiler_params=pltpu.CompilerParams(
            collective_id=ident, has_side_effects=True, vmem_limit_bytes=60 * 1024 * 1024
        ),
    )(*operands)
    return dict(zip(out, results, strict=True))


def run_third(*operands):
    out = {
        "grad_rows": ((HALF, D), F32),
        "grad_out": ((RING, RING, BLOCK, 384), LOW),
        "grad_query": ((5, BLOCK, HD), LOW),
        "grad_kv": ((RING, RING, BLOCK, HD), LOW),
        "gateup_rows": ((RING, PAD, 2 * (MAIN + TAIL)), LOW),
        "output": ((BLOCK, D), F32),
    }
    scratch = [
        pltpu.VMEM((RING, HALF, D), LOW),
        pltpu.VMEM((RING, HALF, D), LOW),
        pltpu.VMEM((HALF, D), F32),
        pltpu.VMEM((HALF, D), F32),
        pltpu.VMEM((BLOCK, D), LOW),
        pltpu.VMEM((RING, BLOCK, D), LOW),
        pltpu.VMEM((RING, BLOCK, 384), LOW),
        pltpu.VMEM((RING, BLOCK, 384), LOW),
        pltpu.VMEM((5, BLOCK, HD), LOW),
        pltpu.VMEM((5, BLOCK, 128), F32),
        pltpu.VMEM((5, BLOCK, RING * BLOCK), LOW),
        pltpu.VMEM((5, BLOCK, RING * BLOCK), LOW),
        pltpu.VMEM((5, BLOCK, HD), F32),
        pltpu.VMEM((2, RING, RING, BLOCK, HD), LOW),
        pltpu.VMEM((RING, RING, BLOCK, HD), LOW),
        *reduce_scratch(),
        *reduce_scratch(),
        *plane_reduce_scratch(2 * (MAIN + TAIL)),
    ]
    spaces = [pl.ANY] * 3 + [pltpu.VMEM] * 11
    return call(third_kernel, 2, 90, out, scratch, operands, spaces)


def run_fourth(*operands):
    out = {
        "grad_tokens": ((BLOCK, D), F32),
        "gateup_got": ((RING, PAD, 2 * (MAIN + TAIL)), LOW),
        "down_got": ((RING, PAD, 1024), LOW),
        "out_got": ((RING, PAD, 384), LOW),
        "qkv_got": ((RING, PAD, 384), LOW),
    }
    scratch = [
        pltpu.VMEM((RING, BLOCK, 384), LOW),
        pltpu.VMEM((RING, BLOCK, 384), LOW),
        pltpu.VMEM((BLOCK, HD), F32),
        pltpu.VMEM((RING, BLOCK, D), LOW),
        pltpu.VMEM((HALF, D), F32),
        pltpu.VMEM((RING, RING, BLOCK, 384), LOW),
        pltpu.VMEM((RING, PAD, 1024), LOW),
        pltpu.VMEM((RING, PAD, 384), LOW),
        pltpu.VMEM((RING, PAD, 384), LOW),
        *reduce_scratch(),
        *plane_reduce_scratch(HD),
        *plane_reduce_scratch(1024),
        *plane_reduce_scratch(384),
        *plane_reduce_scratch(384),
    ]
    spaces = [pltpu.VMEM] * 3 + [pl.ANY] + [pltpu.VMEM] * 8
    return call(fourth_kernel, 3, 130, out, scratch, operands, spaces)


def adam_update(weight, gradient, first_moment, second_moment, learn_rate, decay_rate):
    first_moment = first_decay * first_moment + (1.0 - first_decay) * gradient
    second_moment = second_decay * second_moment + (1.0 - second_decay) * gradient * gradient
    corrected = (
        first_moment
        / (1.0 - first_decay**STEP)
        / (jnp.sqrt(second_moment / (1.0 - second_decay**STEP)) + adam_eps)
    )
    return (weight - learn_rate * (corrected + decay_rate * weight), first_moment, second_moment)


def out_fan_in(seq_length):
    return max(1, H * HD * 4 // min(WINDOW, seq_length))


def activate(gate_part, upper_part):
    return jax.nn.gelu(gate_part, approximate=True) * upper_part


def quarters(rows):
    return rows.reshape(OWN, RING, -1).transpose(1, 0, 2)


def head_quarters(rows):
    split = rows.reshape(rows.shape[0], 5, HD)
    last = split[:, 4].reshape(-1, RING, TAIL)
    return jnp.concatenate([split[:, :4], last], axis=2).transpose(1, 0, 2)


def whole_heads(slices):
    slices = slices.transpose(1, 0, 2)
    rows = slices.shape[0]
    return jnp.concatenate(
        [slices[..., :HD].reshape(rows, -1), slices[..., HD:].reshape(rows, -1)], axis=1
    )


def whole(slices):
    return slices.transpose(1, 0, 2).reshape(slices.shape[1], -1)


def pad_to(x, axis, size):
    widths = [(0, 0)] * x.ndim
    widths[axis] = (0, size - x.shape[axis])
    return jnp.pad(x, widths)


def per_device(
    tokens,
    cotangent,
    w_query,
    w_keyvalue,
    w_out,
    w_gateup,
    w_down,
    norm_scales,
    first_query,
    first_keyvalue,
    first_out,
    first_gateup,
    first_down,
    first_scales,
    second_query,
    second_keyvalue,
    second_out,
    second_gateup,
    second_down,
    second_scales,
):
    core = lax.axis_index("tensor")
    seq_index = lax.axis_index("x") * RING + lax.axis_index("z")
    positions = seq_index * BLOCK + jnp.arange(BLOCK, dtype=jnp.int32)
    seq_length = BLOCK * RING * RING

    keyvalue_part = lax.dynamic_index_in_dim(w_keyvalue, core, 1, keepdims=False)
    scale_columns = jnp.broadcast_to(norm_scales.T[None], (RING, OWN, 2))
    attn_rows = jnp.concatenate(
        [head_quarters(w_query), quarters(keyvalue_part), head_quarters(w_out.T), scale_columns],
        axis=2,
    ).astype(LOW)
    attn_rows = pad_to(pad_to(attn_rows, 2, 768), 1, PAD)
    gateup = w_gateup.astype(LOW).reshape(OWN, 2, RING, MAIN + TAIL).transpose(2, 0, 1, 3)
    feed_rows = jnp.concatenate(
        [
            gateup[..., :MAIN].reshape(RING, OWN, 2 * MAIN),
            gateup[..., MAIN:].reshape(RING, OWN, 2 * TAIL),
            quarters(w_down.T).astype(LOW),
        ],
        axis=2,
    )
    feed_rows = pad_to(pad_to(feed_rows, 2, 2944), 1, PAD)
    frequency = 10000.0 ** (-jnp.arange(TAIL, dtype=F32) / TAIL)
    angles = positions.astype(F32)[:, None] * frequency[None, :]
    cos_table = jnp.tile(jnp.cos(angles), (1, 2))
    sin_table = jnp.concatenate([-jnp.sin(angles), jnp.sin(angles)], axis=1)
    cos_kv = jnp.where(core == 0, cos_table, 1.0)
    sin_kv = jnp.where(core == 0, sin_table, 0.0)
    first = run_first(
        attn_rows, feed_rows, tokens, cotangent.astype(LOW), cos_table, sin_table, cos_kv, sin_kv
    )
    feed_full = first["feed_full"].reshape(D, 2944)
    gateup_full = feed_full[:, : 2 * (MAIN + TAIL)]
    down_full = feed_full[:, 2 * (MAIN + TAIL) :]
    dy_all = first["dy_all"].reshape(-1, D)
    normed_two = first["normed_two"].reshape(-1, D)

    gateup = dot(normed_two, gateup_full, (1, 0))
    gate = jnp.concatenate([gateup[:, :MAIN], gateup[:, 2 * MAIN : 2 * MAIN + TAIL]], axis=1)
    upper = jnp.concatenate([gateup[:, MAIN : 2 * MAIN], gateup[:, 2 * MAIN + TAIL :]], axis=1)
    hidden, activate_back = jax.vjp(activate, gate, upper)
    hidden_low = pad_to(hidden.astype(LOW), 1, 1024)
    grad_hidden = dot(dy_all, down_full, (1, 0))[:, : MAIN + TAIL]
    grad_gate, grad_upper = activate_back(grad_hidden)
    grad_gateup_low = jnp.concatenate(
        [grad_gate[:, :MAIN], grad_upper[:, :MAIN], grad_gate[:, MAIN:], grad_upper[:, MAIN:]], axis=1
    ).astype(LOW)
    norm_part = dot(grad_gateup_low, gateup_full, (1, 1)).astype(LOW).reshape(RING, BLOCK, D)
    feed_part = dot(hidden_low, down_full, (1, 1)).astype(LOW).reshape(RING, BLOCK, D)
    gateup_grads = dot(normed_two, grad_gateup_low, (0, 0)).astype(LOW)
    down_grads = dot(dy_all, hidden_low, (0, 0)).astype(LOW)
    third = run_third(
        norm_part,
        feed_part,
        gateup_grads.reshape(RING, RING, BLOCK, -1),
        cotangent,
        first["residual"],
        first["gains"],
        first["attn_full"],
        first["att_slice"],
        first["query"],
        first["keyvalue"],
        first["log_total"],
        first["attended"],
        cos_table,
        sin_table,
    )
    fourth = run_fourth(
        third["grad_kv"],
        third["grad_query"],
        third["gateup_rows"],
        down_grads.reshape(RING, RING, BLOCK, -1),
        third["grad_out"],
        first["attn_full"],
        first["normed_one"],
        third["grad_rows"],
        tokens,
        first["gains"],
        cos_kv,
        sin_kv,
    )
    output, grad_tokens = third["output"], fourth["grad_tokens"]

    gateup_shard = fourth["gateup_got"][:, :OWN].astype(F32)
    gateup_shard = jnp.concatenate(
        [
            gateup_shard[..., : 2 * MAIN].reshape(RING, OWN, 2, MAIN),
            gateup_shard[..., 2 * MAIN :].reshape(RING, OWN, 2, TAIL),
        ],
        axis=3,
    ).transpose(1, 2, 0, 3).reshape(OWN, 2, -1)
    down_shard = whole(fourth["down_got"][:, :OWN, : MAIN + TAIL].astype(F32)).T
    out_shard = whole_heads(fourth["out_got"][:, :OWN, :320].astype(F32)).T
    qkv_shard = fourth["qkv_got"][:, :OWN].astype(F32)
    query_shard = whole_heads(qkv_shard[..., :320])
    kv_half = whole(qkv_shard[..., 320:])
    gain_rows = 1.0 + norm_scales.astype(LOW).astype(F32)

    def with_weight(weight, grads):
        return jnp.sum((weight.astype(LOW).astype(F32) * grads).reshape(OWN, -1), axis=1)

    scale_parts = jnp.stack(
        [
            with_weight(w_query, query_shard) + with_weight(keyvalue_part, kv_half),
            with_weight(w_gateup, gateup_shard),
        ],
        axis=1,
    )
    packed = pad_to(jnp.concatenate([kv_half, pad_to(scale_parts, 1, 128)], axis=1), 0, PAD)
    theirs = swap_cores(packed, 4)[:OWN]
    kv_other = theirs[:, :HD]
    scale_grads = (scale_parts + theirs[:, HD : HD + 2]).T / gain_rows
    keyvalue_shard = jnp.stack(
        [jnp.where(core == 0, kv_half, kv_other), jnp.where(core == 0, kv_other, kv_half)], axis=1
    )

    matrix_rate = 2.0 * D ** (-0.5)
    out_rate = 2.0 * out_fan_in(seq_length) ** (-0.5)
    down_rate = 2.0 * (FF // 2) ** (-0.5)
    triples = [
        adam_update(w_query, query_shard, first_query, second_query, matrix_rate, weight_decay),
        adam_update(
            w_keyvalue, keyvalue_shard, first_keyvalue, second_keyvalue, matrix_rate, weight_decay
        ),
        adam_update(w_out, out_shard, first_out, second_out, out_rate, weight_decay),
        adam_update(w_gateup, gateup_shard, first_gateup, second_gateup, matrix_rate, weight_decay),
        adam_update(w_down, down_shard, first_down, second_down, down_rate, weight_decay),
        adam_update(norm_scales, scale_grads, first_scales, second_scales, gain_rate, 0.0),
    ]
    return (output, grad_tokens, *(triple[i] for i in range(3) for triple in triples))


def solution(mesh):
    split = Mesh(
        mesh.devices.reshape(RING, RING, RING, 2), ("dp", "x", "z", "tensor")
    )
    rows = ("dp", "x", "z")
    matrices = (
        P(rows, "tensor"),
        P(rows, None, None),
        P("tensor", rows),
        P(rows, None, "tensor"),
        P("tensor", rows),
        P(None, rows),
    )
    in_specs = (P(rows, None), P(rows, None), *matrices, *matrices, *matrices)
    out_specs = in_specs
    return jax.shard_map(
        per_device, mesh=split, in_specs=in_specs, out_specs=out_specs, check_vma=False
    )
```

time: 563 us -> 462 us (0.82)
  local copies, waits for them, and re-layouts: 56.8 us -> 32.5 us
  matrix products: 81.1 us -> 59.1 us
  Pallas kernels: 360 us -> 339 us
  other arithmetic: 41.7 us -> 25.5 us
  between operations: 15.8 us -> 1.82 us
    pallas_call x13 -> x3, Pallas kernels: 194 us -> 173 us  [the longest x2 166 us: call(): pl.pallas_call(kernel, out_shape=[jax.ShapeDtypeStruct(shape, kind) for s...]
    dot_general x5 -> x0, matrix products: 17.1 us -> none  [the longest x1 5.6 us: per_device(): jnp.einsum('hcd,kd->hck', query_low, key_rows, preferred_element_type=F32)]
    unnamed x98 -> x64, local copies, waits for them, and re-layouts: 17.4 us -> 8.16 us
    concatenate x2 -> x0, local copies, waits for them, and re-layouts: 9.09 us -> none  [the longest x1 6.3 us: per_device(): jnp.concatenate([grad_qkv_w, grad_out, pad_to(grad_scales, 1, 64)], axis=1)]
    convert_element_type x7 -> x3, other arithmetic: 9.82 us -> 2.14 us  [the longest x1 1.15 us: per_device(): gateup_shard = fourth['gateup_got'][:, :OWN].astype(F32)]
    dot_general x10 -> x6, matrix products: 64 us -> 59.1 us  [dot(): lax.dot_general(left_side, right_side, ((contract[:1], contract[1:]), (()...]
  transfers between devices with their start and end apart: 2 -> 0, of which waited for: 0 -> 0; matrix products, arithmetic and copies ran while one was open for 21% -> 0% of each run, Pallas kernels for 33% -> 0%
where the time goes in v3:
time: 462 us; the launch traced here: 458 us
  Pallas kernels  339 us (73%)
  matrix products  59.1 us (13%)
  local copies, waits for them, and re-layouts  32.5 us (7%)
  other arithmetic  25.5 us (6%)
    pallas_call x1, Pallas kernels, run_first(): pl.pallas_call(first_kernel, out_shape=[jax.ShapeDtypeStruct(shape, kind)...  166 us
    pallas_call x2, Pallas kernels, call(): pl.pallas_call(kernel, out_shape=[jax.ShapeDtypeStruct(shape, kind) for s...  166 us
    dot_general x6, matrix products, dot(): lax.dot_general(left_side, right_side, ((contract[:1], contract[1:]), (()...  59.1 us
    sub x6, other arithmetic, adam_update(): weight - learn_rate * (corrected + decay_rate * weight)  12.7 us

profile of v3, /device:TPU:1, one launch (start us, length us, event | category | flops | bytes accessed | tf_op | source)
XLA Modules:
  0.0 457.7 jit_solution(14631599871015749251)
XLA Ops:
  9.3 1.2 slice.141
  10.5 3.1 reshape.170
  13.6 1.3 fusion.28
  18.4 166.0 %shard_map.347 = (bf16[4,4,160,2944]{3,2,1,0:T(8,128)(2,1)}, bf16[4,4,160,768]{3,2,1,0:T(8,128)(2,1)}, bf16[4,160,2560]{2,1,0:T(8,128)(2,1)}, bf16[4,160,2560]{2...) custom-call(bf16[4,48,768]{2,1,0:T(8,128)(2,1)} %pad.29.attn_rows, ...), custom_call_target="tpu_custom_call" | custom-call | tf_op jit(solution)/shard_map/pallas_call | solution.py:487
  184.4 11.8 %fusion.2 = f32[640,1920]{0,1:T(8,128)S(1)} fusion(bf16[640,2560]{1,0:T(8,128)(2,1)} %bitcast.97, bf16[2560,2944]{1,0:T(8,128)(2,1)} %bitcast.91), kind=kOutput, calls=%fused_computation.3 | convolution fusion | flops 6291456000 | bytes 18022400 | tf_op jit(solution)/shard_map/dot_general | solution.py:53
  196.5 1.6 copy-done.21
  198.2 8.7 %multiply_convert_fusion = (bf16[640,960]{0,1:T(8,128)(2,1)S(1)}, bf16[640,960]{0,1:T(8,128)(2,1)S(1)}, bf16[640,960]{0,1:T(8,128)(2,1)S(1)}) fusion(f32[640,64]{0,1:T(8,128)S(1)} %get-tuple-element.174, f32[640,896]{0,1:T(8,128)S(1)} %get-tuple-element.172, f32[640,64]{0,1:T(8,128)S(1)} %get-tuple-element.175, f32[640,896]{0,1:T(8,128)S(1)} %get-tuple-element.173, ...), kind=kOutput, calls=%fused_computation.24 | convolution fusion | flops 3162931200 | bytes 17121280 | tf_op jit(solution)/shard_map/dot_general | solution.py:53
  207.1 11.4 %fusion.8 = bf16[640,2560]{1,0:T(8,128)(2,1)} fusion(bf16[2560,2944]{1,0:T(8,128)(2,1)} %bitcast.93, bf16[640,64]{0,1:T(8,128)(2,1)S(1)} %slice.152, bf16[640,64]{0,1:T(8,128)(2,1)S(1)} %slice.151, bf16[640,896]{0,1:T(8,128)(2,1)S(1)} %slice.150, bf16[640,896]{0,1:T(8,128)(2,1)S(1)} %slice.149), kind=kOutput, calls=%fused_computation.10 | convolution fusion | flops 6302924800 | bytes 15564800 | tf_op jit(solution)/shard_map/dot_general | solution.py:53
  218.5 8.1 %fusion.11 = bf16[640,2560]{1,0:T(8,128)(2,1)} fusion(bf16[2560,2944]{1,0:T(8,128)(2,1)} %bitcast.94, bf16[640,960]{0,1:T(8,128)(2,1)S(1)} %get-tuple-element.169), kind=kOutput, calls=%fused_computation.11 | convolution fusion | flops 3357081600 | bytes 9748480 | tf_op jit(solution)/shard_map/dot_general | solution.py:53
  226.6 10.9 %convolution_convert_fusion = bf16[2560,1920]{1,0:T(8,128)(2,1)} fusion(bf16[640,2560]{1,0:T(8,128)(2,1)S(1)} %bitcast.98, bf16[640,64]{0,1:T(8,128)(2,1)S(1)} %slice.152, bf16[640,64]{0,1:T(8,128)(2,1)S(1)} %slice.151, bf16[640,896]{0,1:T(8,128)(2,1)S(1)} %slice.150, bf16[640,896]{0,1:T(8,128)(2,1)S(1)} %slice.149), kind=kOutput, calls=%fused_computation | convolution fusion | flops 6306201600 | bytes 15564800 | tf_op jit(solution)/shard_map/dot_general | solution.py:53
  237.6 92.8 %shard_map.348 = (f32[80,2560]{1,0:T(8,128)}, bf16[4,4,160,384]{3,2,1,0:T(8,128)(2,1)}, bf16[5,160,256]{2,1,0:T(8,128)(2,1)}, bf16[4,4,160,256]{3,2,1,0:T(8,128)...) custom-call(bf16[4,160,2560]{2,1,0:T(8,128)(2,1)} %bitcast.80, bf16[4,160,2560]{2,1,0:T(8,128)(2,1)} %bitcast.81, ...), custom_call_target="tpu_custom_call" | custom-call | tf_op jit(solution)/shard_map/pallas_call | solution.py:1005
  330.4 8.3 %convolution_convert_fusion.1 = bf16[2560,1024]{1,0:T(8,128)(2,1)} fusion(bf16[640,2560]{1,0:T(8,128)(2,1)} %bitcast.95, bf16[640,960]{0,1:T(8,128)(2,1)S(1)} %copy-done.24), kind=kOutput, calls=%fused_computation.5 | convolution fusion | flops 3358064640 | bytes 9748480 | tf_op jit(solution)/shard_map/dot_general | solution.py:53
  338.7 73.0 %shard_map.349 = (f32[160,2560]{1,0:T(8,128)}, bf16[4,48,1920]{2,1,0:T(8,128)(2,1)}, bf16[4,48,1024]{2,1,0:T(8,128)(2,1)}, bf16[4,48,384]{2,1,0:T(8,128)(2,1)}, bf16[4,48,384]{2,1,0:T(8,128)(2,1)}) custom-call(bf16[4,4,160,256]{3,2,1,0:T(8,128)(2,1)} %get-tuple-element.55.grad_kv, bf16[5,160,256]{2,1,0:T(8,128)(2,1)} %get-tuple-element.56.grad_query, ...), custom_call_target="tpu_custom_call" | custom-call | tf_op jit(solution)/shard_map/pallas_call | solution.py:1005
  414.2 1.2 slice_convert_fusion
  416.2 1.1 slice.158
  417.3 2.2 reshape.182
  419.4 1.5 maximum_bitcast_fusion
  421.8 2.6 reshape.184
  424.4 7.7 %multiply_subtract_fusion = (f32[40,2,3840]{2,1,0:T(2,128)}, f32[40,2,3840]{2,1,0:T(2,128)}, f32[40,2,3840]{2,1,0:T(2,128)}, f32[40]{0:T(128)S(1)}) fusion(f32[40,2,3840]{2,1,0:T(2,128)S(1)} %copy-done.1, f32[40,2,3840]{2,1,0:T(2,128)} %reshape.184, f32[40,2,3840]{2,1,0:T(2,128)} %param.31, f32[40,2,3840]{2,1,0:T(2,128)} %param.37), kind=kLoop, calls=%fused_computation.34 | loop fusion | flops 5836760 | bytes 8601760 | tf_op jit(solution)/shard_map/sub | solution.py:1092
  433.1 6.9 %shard_map.350 = f32[48,384]{1,0:T(8,128)} custom-call(f32[48,384]{1,0:T(8,128)} %pad.34.x_ref), custom_call_target="tpu_custom_call" | custom-call | tf_op jit(solution)/shard_map/pallas_call | solution.py:97
  444.0 3.0 multiply_subtract_fusion.1
  448.5 1.4 sqrt_add_fusion
  454.9 1.2 copy.236
  456.1 1.2 copy.237
  (146 shorter events, 27.9 us)
Async XLA Ops:
  0.7 3.7 copy-start.13
  0.7 4.8 %copy-start.2 = (f32[3840,40]{0,1:T(8,128)S(1)}, f32[3840,40]{0,1:T(8,128)}, u32[]{:S(2)}) copy-start(f32[3840,40]{0,1:T(8,128)} %param.26) | copy-start | bytes 1843204
  3.9 2.9 copy-start.1
  10.5 5.4 %copy-start = (f32[160,2560]{1,0:T(8,128)S(1)}, f32[160,2560]{1,0:T(8,128)}, u32[]{:S(2)}) copy-start(f32[160,2560]{1,0:T(8,128)} %cotangent.1) | copy-start | bytes 4915204
  196.2 1.9 copy-start.21
  206.8 11.7 %copy-start.23 = (bf16[640,960]{0,1:T(8,128)(2,1)}, bf16[640,960]{0,1:T(8,128)(2,1)S(1)}, u32[]{:S(2)}) copy-start(bf16[640,960]{0,1:T(8,128)(2,1)S(1)} %get-tuple-element.169) | copy-start | bytes 3686404
  218.5 8.1 %copy-start.22 = (bf16[4,160,2560]{2,1,0:T(8,128)(2,1)S(1)}, bf16[4,160,2560]{2,1,0:T(8,128)(2,1)}, u32[]{:S(2)}) copy-start(bf16[4,160,2560]{2,1,0:T(8,128)(2,1)} %get-tuple-element.45) | copy-start | bytes 9830404
  237.6 92.8 %copy-start.24 = (bf16[640,960]{0,1:T(8,128)(2,1)S(1)}, bf16[640,960]{0,1:T(8,128)(2,1)}, u32[]{:S(2)}) copy-start(bf16[640,960]{0,1:T(8,128)(2,1)} %copy-done.23) | copy-start | bytes 3686404
  411.7 1.3 copy-start.6
  411.7 1.3 copy-start.9
  411.7 1.3 copy-start.10
  424.4 16.4 %copy-start.14 = (f32[40,2,256]{2,1,0:T(2,128)S(1)}, f32[40,2,256]{2,1,0:T(2,128)}, u32[]{:S(2)}) copy-start(f32[40,2,256]{2,1,0:T(2,128)} %param.23) | copy-start | bytes 245764
  424.4 16.4 %copy-start.16 = (f32[40,2,256]{2,1,0:T(2,128)S(1)}, f32[40,2,256]{2,1,0:T(2,128)}, u32[]{:S(2)}) copy-start(f32[40,2,256]{2,1,0:T(2,128)} %param.29) | copy-start | bytes 245764
  424.4 16.4 %copy-start.17 = (f32[40,2,256]{2,1,0:T(2,128)S(1)}, f32[40,2,256]{2,1,0:T(2,128)}, u32[]{:S(2)}) copy-start(f32[40,2,256]{2,1,0:T(2,128)} %param.35) | copy-start | bytes 245764
  424.4 17.2 %copy-start.15 = (bf16[4,48,384]{2,1,0:T(8,128)(2,1)S(1)}, bf16[4,48,384]{2,1,0:T(8,128)(2,1)}, u32[]{:S(2)}) copy-start(bf16[4,48,384]{2,1,0:T(8,128)(2,1)} %get-tuple-element.64) | copy-start | bytes 442372
  432.1 9.7 %copy-start.7 = (f32[1280,40]{0,1:T(8,128)S(1)}, f32[1280,40]{0,1:T(8,128)}, u32[]{:S(2)}) copy-start(f32[1280,40]{0,1:T(8,128)} %param.24) | copy-start | bytes 614404
  432.1 9.7 %copy-start.11 = (f32[1280,40]{0,1:T(8,128)S(1)}, f32[1280,40]{0,1:T(8,128)}, u32[]{:S(2)}) copy-start(f32[1280,40]{0,1:T(8,128)} %param.30) | copy-start | bytes 614404
  432.1 9.7 %copy-start.12 = (f32[1280,40]{0,1:T(8,128)S(1)}, f32[1280,40]{0,1:T(8,128)}, u32[]{:S(2)}) copy-start(f32[1280,40]{0,1:T(8,128)} %param.36) | copy-start | bytes 614404
  432.1 10.6 %copy-start.8 = (bf16[4,48,1024]{2,1,0:T(8,128)(2,1)S(1)}, bf16[4,48,1024]{2,1,0:T(8,128)(2,1)}, u32[]{:S(2)}) copy-start(bf16[4,48,1024]{2,1,0:T(8,128)(2,1)} %get-tuple-element.65) | copy-start | bytes 1179652
  443.9 3.0 copy-start.18
  443.9 3.1 copy-start.19
  443.9 3.9 copy-start.20
  444.0 10.9 %copy-start.3 = (f32[160,2560]{1,0:T(8,128)S(1)}, f32[160,2560]{1,0:T(8,128)}, u32[]{:S(2)}) copy-start(f32[160,2560]{1,0:T(8,128)} %get-tuple-element.208) | copy-start | bytes 4915204
  446.9 9.2 %copy-start.4 = (f32[160,2560]{1,0:T(8,128)S(1)}, f32[160,2560]{1,0:T(8,128)}, u32[]{:S(2)}) copy-start(f32[160,2560]{1,0:T(8,128)} %get-tuple-element.209) | copy-start | bytes 4915204
  (1 other events, 0.8 us)

commit v4 on v3

--- a/solution.py
+++ b/solution.py
@@ -20,6 +20,8 @@
 adam_eps = 1e-08
 weight_decay = 0.1
 gain_rate = 0.2
+GELU_SCALE = (2.0 / 3.141592653589793) ** 0.5
+GELU_CUBE = 0.044715
 
 MESH = pl.DeviceIdType.MESH
 LOW = jnp.bfloat16
@@ -705,13 +707,151 @@
         dst[i] = jnp.concatenate([rows, jnp.zeros((PAD - OWN, rows.shape[1]), F32)]).astype(LOW)
 
 
-def third_kernel(
-    norm_part,
-    feed_part,
-    gateup_grads,
+def activation(gate, upper, grad):
+    square = gate * gate
+    tanh = jnp.tanh(GELU_SCALE * gate * (1.0 + GELU_CUBE * square))
+    half = 0.5 * (1.0 + tanh)
+    gelu = gate * half
+    slope = half + 0.5 * gate * (1.0 - tanh * tanh) * GELU_SCALE * (1.0 + 3.0 * GELU_CUBE * square)
+    return gelu * upper, grad * upper * slope, grad * gelu
+
+
+def second_kernel(
+    feed_full,
+    normed_two,
+    dy_all,
     cotangent,
     residual,
     gain_ref,
+    grad_rows,
+    da_all,
+    feed_part,
+    gateup_grads,
+    down_rows,
+    send_sem,
+    recv_sem,
+    local_sem,
+    gateup_weight,
+    down_weight,
+    hidden,
+    dgu,
+    norm_part,
+    stage,
+    grad_half,
+    cot_half,
+    res_half,
+    da_low,
+    *bufs,
+):
+    z = lax.axis_index("z")
+    half, _, _, _ = core_rows()
+    plane = ("dp", "x")
+    gu_width = 2 * (MAIN + TAIL)
+    wide = RING * BLOCK
+    loads = [
+        pltpu.make_async_copy(feed_full.at[:, :, :, pl.ds(0, gu_width)], gateup_weight, local_sem.at[0]),
+        pltpu.make_async_copy(
+            feed_full.at[:, :, :, pl.ds(gu_width, 1024)], down_weight, local_sem.at[1]
+        ),
+        pltpu.make_async_copy(cotangent.at[half], cot_half, local_sem.at[2]),
+        pltpu.make_async_copy(residual.at[half], res_half, local_sem.at[3]),
+    ]
+    for load in loads:
+        load.start()
+    greet(plane_peers(("z",)) + plane_peers(plane) + [sibling()])
+    mover = Mover(send_sem, recv_sem)
+    for load in loads:
+        load.wait()
+
+    def product(rows, weight, lo, n):
+        left_side = rows[...].reshape(wide, D)
+        return dot(left_side, weight[:, :, :, lo : lo + n].reshape(D, n), (1, 0))
+
+    for lo, n in ((0, 256), (256, 256), (512, 256), (768, 128)):
+        value, grad_gate, grad_upper = activation(
+            product(normed_two, gateup_weight, lo, n),
+            product(normed_two, gateup_weight, MAIN + lo, n),
+            product(dy_all, down_weight, lo, n),
+        )
+        hidden[:, lo : lo + n] = value.astype(LOW)
+        dgu[:, lo : lo + n] = grad_gate.astype(LOW)
+        dgu[:, MAIN + lo : MAIN + lo + n] = grad_upper.astype(LOW)
+    both = product(normed_two, gateup_weight, 2 * MAIN, 2 * TAIL)
+    value, grad_gate, grad_upper = activation(
+        both, pltpu.roll(both, TAIL, 1), product(dy_all, down_weight, MAIN, 2 * TAIL)
+    )
+    low_lanes = lanes(both.shape) < TAIL
+    hidden[:, MAIN:] = jnp.where(low_lanes, value, 0.0).astype(LOW)
+    dgu[:, 2 * MAIN :] = jnp.where(low_lanes, grad_gate, pltpu.roll(grad_upper, TAIL, 1)).astype(LOW)
+
+    for i in range(RING):
+        part = dot(dgu[...], gateup_weight[i].reshape(wide, gu_width), (1, 1))
+        norm_part[:, :, i * wide : (i + 1) * wide] = part.astype(LOW).reshape(RING, BLOCK, wide)
+    norm_sum = reduce_steps(mover, norm_part, lambda i: norm_part[i, half], bufs[:6], grad_half)
+    advance(norm_sum)
+
+    for i in range(RING):
+        part = dot(hidden[...], down_weight[i].reshape(wide, 1024), (1, 1))
+        feed_part[:, :, i * wide : (i + 1) * wide] = part.astype(LOW).reshape(RING, BLOCK, wide)
+        if i == 0:
+            advance(norm_sum)
+
+    def columns(rows, i):
+        return rows[:, :, i * wide : (i + 1) * wide].reshape(wide, wide)
+
+    for i in range(RING):
+        grads = dot(columns(dy_all, i), hidden[...], (0, 0))
+        down_weight[i] = grads.astype(LOW).reshape(RING, BLOCK, 1024)
+        if i == 1:
+            advance(norm_sum)
+    down_sum = plane_reduce_steps(mover, plane, down_weight, bufs[6:11], bufs[11])
+    advance(down_sum)
+    saved = []
+
+    def gateup_block(i):
+        if saved:
+            saved[-1].wait()
+        grads = dot(columns(normed_two, i), dgu[...], (0, 0))
+        stage[...] = grads.astype(LOW).reshape(RING, BLOCK, gu_width)
+        saved.append(pltpu.make_async_copy(stage, gateup_grads.at[i], local_sem.at[4 + i]))
+        saved[-1].start()
+
+    gateup_block(0)
+    advance(norm_sum)
+    rows = res_half[...]
+    inverse = lax.rsqrt(jnp.mean(rows * rows, axis=-1, keepdims=True) + eps_norm)
+    unit = rows * inverse
+    scaled = grad_half[...] * gain_ref[1:2, :]
+    grad = cot_half[...] + inverse * (
+        scaled - unit * jnp.mean(scaled * unit, axis=-1, keepdims=True)
+    )
+    grad_rows[...] = grad
+    da_low[half, :] = grad.astype(LOW)
+    da_share = mover.copy(da_low.at[half], da_low.at[half], sibling())
+    da_gather = gather_steps(mover, da_low, da_all)
+    advance(da_gather)
+    advance(down_sum)
+    gateup_block(1)
+    da_share.wait_recv()
+    da_all[z] = da_low[...]
+    advance(da_gather)
+    gateup_block(2)
+    advance(down_sum)
+    advance(da_gather)
+    gateup_block(3)
+    advance(down_sum)
+    advance(da_gather)
+    advance(down_sum)
+    spread_rows(bufs[11], down_rows)
+    saved[-1].wait()
+    mover.finish()
+
+
+def third_kernel(
+    feed_part,
+    gateup_grads,
+    da_all,
+    residual,
     attn_full,
     att_slice,
     query,
@@ -720,21 +860,17 @@
     attended,
     cos_ref,
     sin_ref,
-    grad_rows,
+    cos_kv,
+    sin_kv,
     grad_out,
-    grad_query,
-    grad_kv,
+    grad_got,
     gateup_rows,
     output,
     send_sem,
     recv_sem,
     local_sem,
-    norm_mine,
     feed_mine,
-    grad_half,
     out_half,
-    da_low,
-    da_all,
     datt_send,
     datt_got,
     datt,
@@ -744,56 +880,34 @@
     dq,
     kv_pair,
     kv_in,
+    grad_kv,
+    grad_query,
+    grad_send,
+    kv_low,
     *bufs,
 ):
     z, core = lax.axis_index("z"), lax.axis_index("tensor")
     x = lax.axis_index("x")
     half, _, _, their_half = core_rows()
-    norm_bufs, out_bufs, rows_bufs = bufs[:6], bufs[6:12], bufs[12:17]
-    rows_res = bufs[17]
+    out_bufs, rows_bufs, rows_res = bufs[:6], bufs[6:11], bufs[11]
+    kv_bufs, kv_rows = bufs[12:17], bufs[17]
+    feed_load = pltpu.make_async_copy(feed_part.at[:, half], feed_mine, local_sem.at[9])
+    feed_load.start()
     greet([{"z": step("z", d)} for d in (1, 2, 3)] + plane_peers(("dp", "x")) + [sibling()])
     mover = Mover(send_sem, recv_sem)
-    norm_load = pltpu.make_async_copy(norm_part.at[:, half], norm_mine, local_sem.at[8])
-    norm_load.start()
-    feed_load = pltpu.make_async_copy(feed_part.at[:, half], feed_mine, local_sem.at[9])
-    feed_load.start()
-    norm_sum = reduce_steps(mover, norm_part, lambda i: norm_mine[i], norm_bufs, grad_half)
-    advance(norm_sum)
     rows_sum = plane_reduce_steps(
         mover, ("dp", "x"), gateup_grads, rows_bufs, rows_res, loads=local_sem
     )
     advance(rows_sum)
-    norm_load.wait()
-    advance(norm_sum)
-    advance(norm_sum)
-    advance(norm_sum)
-
-    rows = residual[half, :]
-    inverse = lax.rsqrt(jnp.mean(rows * rows, axis=-1, keepdims=True) + eps_norm)
-    unit = rows * inverse
-    scaled = grad_half[...] * gain_ref[1:2, :]
-    grad = cotangent[half, :] + inverse * (
-        scaled - unit * jnp.mean(scaled * unit, axis=-1, keepdims=True)
-    )
-    grad_rows[...] = grad
-    da_low[half, :] = grad.astype(LOW)
-    da_share = mover.copy(da_low.at[half], da_low.at[half], sibling())
-    da_gather = gather_steps(mover, da_low, da_all)
-    advance(da_gather)
     feed_sum = reduce_steps(mover, feed_part, lambda i: feed_mine[i], out_bufs, out_half)
-    da_share.wait_recv()
-    da_all[z] = da_low[...]
     out_weight = attn_full[:, :, :, 384:].reshape(D, 384)
-    datt_got[z] = dot(da_all[z], out_weight, (1, 0)).astype(LOW)
-    advance(da_gather)
-    advance(rows_sum)
-    advance(da_gather)
-    advance(da_gather)
     copies = []
-    for d in (2, 1, 3):
+    for d in (2, 1, 3, 0):
         block = step("z", d)
         datt_send[block] = dot(da_all[block], out_weight, (1, 0)).astype(LOW)
-        copies.append(mover.copy(datt_send.at[block], datt_got.at[z], {"z": block}))
+        if d:
+            copies.append(mover.copy(datt_send.at[block], datt_got.at[z], {"z": block}))
+    datt_got[z] = datt_send[z]
     advance(feed_sum)
     slices = att_slice[...].reshape(RING * BLOCK, 384)
     wide = RING * BLOCK
@@ -848,37 +962,57 @@
     lax.fori_loop(0, RING, one_chunk, 0)
     kv_swap = mover.copy(kv_pair.at[1 - core], kv_in, sibling())
     advance(feed_sum)
-    advance(rows_sum)
     cos, sin = cos_ref[...], sin_ref[...]
     scale = HD ** (-0.5)
     for h in range(5):
-        grad_query[h, :, :128] = turn(dq[h, :, :128] * scale, cos, -sin).astype(LOW)
-        grad_query[h, :, 128:] = (dq[h, :, 128:] * scale).astype(LOW)
+        grad_query[h, :, :128] = turn(dq[h, :, :128] * scale, cos, -sin)
+        grad_query[h, :, 128:] = dq[h, :, 128:] * scale
     kv_swap.wait_recv()
     grad_kv[...] = (kv_pair[core].astype(F32) + kv_in[...].astype(F32)).astype(LOW)
+    kv_sum = plane_reduce_steps(mover, ("x", "z"), grad_kv, kv_bufs, kv_rows)
+    advance(kv_sum)
     advance(rows_sum)
+    for h in range(4):
+        grad_send[h, :, :HD] = grad_query[h].astype(LOW)
+    advance(kv_sum)
+    advance(kv_sum)
+    advance(kv_sum)
+    advance(kv_sum)
+    kv_low[:, :128] = turn(kv_rows[:, :128], cos_kv[...], -sin_kv[...])
+    kv_low[:, 128:] = kv_rows[:, 128:]
+    for j in range(RING):
+        place = slice((j // 2) * 128, (j // 2 + 1) * 128)
+        one, two = grad_query[4, :, place], kv_low[:, place]
+        if j % 2:
+            one = pltpu.roll(one, TAIL, 1)
+        else:
+            two = pltpu.roll(two, TAIL, 1)
+        grad_send[j, :, HD:] = jnp.where(low_lanes, one, two).astype(LOW)
+    swap = exchange_steps(mover, grad_send, grad_got)
+    advance(swap)
+    grad_got[z] = grad_send[z]
     advance(feed_sum)
     output[half, :] = residual[half, :] + out_half[...]
     out_share = mover.copy(output.at[half], output.at[half], sibling())
     advance(rows_sum)
+    advance(swap)
+    advance(rows_sum)
+    advance(rows_sum)
     spread_rows(rows_res, gateup_rows)
     out_share.wait_recv()
     mover.finish()
 
 
 def fourth_kernel(
-    grad_kv,
-    grad_query,
+    grad_got,
     gateup_rows,
-    down_grads,
+    down_rows,
     grad_out,
     attn_full,
     normed_one,
     grad_rows,
     tokens,
     gain_ref,
-    cos_kv,
-    sin_kv,
     grad_tokens,
     gateup_got,
     down_got,
@@ -887,13 +1021,9 @@
     send_sem,
     recv_sem,
     local_sem,
-    grad_send,
-    grad_got,
-    kv_low,
     part,
     grad_half,
     grad_qkv,
-    down_send,
     out_send,
     qkv_send,
     *bufs,
@@ -902,44 +1032,13 @@
     half, _, _, _ = core_rows()
     plane = ("dp", "x")
     sum_bufs = bufs[:6]
-    kv_bufs, down_bufs, out_bufs, qkv_bufs = (bufs[6 + 6 * i : 12 + 6 * i] for i in range(4))
+    out_bufs, qkv_bufs = bufs[6:12], bufs[12:18]
     greet([{"z": step("z", d)} for d in (1, 2, 3)] + plane_peers(plane) + [sibling()])
     mover = Mover(send_sem, recv_sem)
-    kv_sum = plane_reduce_steps(mover, ("x", "z"), grad_kv, kv_bufs[:5], kv_bufs[5])
-    advance(kv_sum)
     out_sum = plane_reduce_steps(mover, plane, grad_out, out_bufs[:5], out_bufs[5])
-    down_sum = plane_reduce_steps(
-        mover, plane, down_grads, down_bufs[:5], down_bufs[5], loads=local_sem
-    )
-    for k in range(5):
-        grad_send_block(k, grad_query, grad_send)
-    advance(kv_sum)
     advance(out_sum)
-    advance(kv_sum)
-    advance(out_sum)
-    advance(kv_sum)
-    advance(kv_sum)
-    kv_rows = kv_bufs[5]
-    kv_low[:, :128] = turn(kv_rows[:, :128], cos_kv[...], -sin_kv[...])
-    kv_low[:, 128:] = kv_rows[:, 128:]
-    low_lanes = lanes((BLOCK, 128)) < TAIL
-    for j in range(RING):
-        place = slice((j // 2) * 128, (j // 2 + 1) * 128)
-        one = grad_query[4, :, place].astype(F32)
-        two = kv_low[:, place]
-        if j % 2:
-            one = pltpu.roll(one, TAIL, 1)
-        else:
-            two = pltpu.roll(two, TAIL, 1)
-        grad_send[j, :, HD:] = jnp.where(low_lanes, one, two).astype(LOW)
-    swap = exchange_steps(mover, grad_send, grad_got)
-    advance(swap)
-    grad_got[z] = grad_send[z]
-    advance(down_sum)
-    advance(out_sum)
-    gateup_swap = exchange_steps(mover, gateup_rows, gateup_got)
-    advance(swap)
-
+    slices = grad_got[...].reshape(RING * BLOCK, 384)
+    wide = RING * BLOCK
     qkv_weight = attn_full[:, :, :, :384].reshape(D, 384)
 
     def make(block):
@@ -947,8 +1046,7 @@
 
     norm_sum = reduce_steps(mover, part, lambda i: part[i, half], sum_bufs, grad_half, make)
     advance(norm_sum)
-    slices = grad_got[...].reshape(RING * BLOCK, 384)
-    wide = RING * BLOCK
+    advance(out_sum)
     for i in range(RING):
         left_side = normed_one[:, :, i * wide : (i + 1) * wide].reshape(wide, wide)
         grad_qkv[i] = dot(left_side, slices, (0, 0)).astype(LOW).reshape(RING, BLOCK, 384)
@@ -958,16 +1056,19 @@
     advance(qkv_sum)
     advance(norm_sum)
     advance(out_sum)
-    advance(down_sum)
+    gateup_swap = exchange_steps(mover, gateup_rows, gateup_got)
     advance(gateup_swap)
+    down_swap = exchange_steps(mover, down_rows, down_got)
+    advance(down_swap)
     gateup_got[z] = gateup_rows[z]
+    down_got[z] = down_rows[z]
     advance(qkv_sum)
+    advance(out_sum)
     advance(out_sum)
     spread_rows(out_bufs[5], out_send)
     out_swap = exchange_steps(mover, out_send, out_got)
     advance(out_swap)
     out_got[z] = out_send[z]
-    advance(down_sum)
     advance(qkv_sum)
     advance(norm_sum)
     rows = tokens[half, :]
@@ -979,34 +1080,23 @@
     )
     share = mover.copy(grad_tokens.at[half], grad_tokens.at[half], sibling())
     advance(qkv_sum)
-    advance(down_sum)
     advance(qkv_sum)
     spread_rows(qkv_bufs[5], qkv_send)
     qkv_swap = exchange_steps(mover, qkv_send, qkv_got)
     advance(qkv_swap)
     qkv_got[z] = qkv_send[z]
-    advance(down_sum)
-    spread_rows(down_bufs[5], down_send)
-    down_swap = exchange_steps(mover, down_send, down_got)
-    advance(down_swap)
-    down_got[z] = down_send[z]
-    for steps in (gateup_swap, out_swap, qkv_swap, down_swap):
+    for steps in (gateup_swap, down_swap, out_swap, qkv_swap):
         advance(steps)
     share.wait_recv()
     mover.finish()
 
 
-def grad_send_block(h, grad_query, grad_send):
-    if h < 4:
-        grad_send[h, :, :HD] = grad_query[h]
-
-
-def call(kernel, ident, copies, out, scratch, operands, spaces):
+def call(kernel, ident, copies, out, scratch, operands, spaces, out_spaces=None):
     results = pl.pallas_call(
         kernel,
         out_shape=[jax.ShapeDtypeStruct(shape, kind) for shape, kind in out.values()],
         in_specs=[pl.BlockSpec(memory_space=space) for space in spaces],
-        out_specs=[pl.BlockSpec(memory_space=pltpu.VMEM) for _ in out],
+        out_specs=[pl.BlockSpec(memory_space=(out_spaces or {}).get(name, pltpu.VMEM)) for name in out],
         scratch_shapes=[
             pltpu.SemaphoreType.DMA((copies,)),
             pltpu.SemaphoreType.DMA((copies,)),
@@ -1020,22 +1110,44 @@
     return dict(zip(out, results, strict=True))
 
 
+def run_second(*operands):
+    out = {
+        "grad_rows": ((HALF, D), F32),
+        "da_all": ((RING, BLOCK, D), LOW),
+        "feed_part": ((RING, BLOCK, D), LOW),
+        "gateup_grads": ((RING, RING, BLOCK, 2 * (MAIN + TAIL)), LOW),
+        "down_rows": ((RING, PAD, 1024), LOW),
+    }
+    scratch = [
+        pltpu.VMEM((RING, RING, BLOCK, 2 * (MAIN + TAIL)), LOW),
+        pltpu.VMEM((RING, RING, BLOCK, 1024), LOW),
+        pltpu.VMEM((RING * BLOCK, 1024), LOW),
+        pltpu.VMEM((RING * BLOCK, 2 * (MAIN + TAIL)), LOW),
+        pltpu.VMEM((RING, BLOCK, D), LOW),
+        pltpu.VMEM((RING, BLOCK, 2 * (MAIN + TAIL)), LOW),
+        pltpu.VMEM((HALF, D), F32),
+        pltpu.VMEM((HALF, D), F32),
+        pltpu.VMEM((HALF, D), F32),
+        pltpu.VMEM((BLOCK, D), LOW),
+        *reduce_scratch(),
+        *plane_reduce_scratch(1024),
+    ]
+    spaces = [pl.ANY, pltpu.VMEM, pltpu.VMEM, pl.ANY, pl.ANY, pltpu.VMEM]
+    return call(
+        second_kernel, 5, 60, out, scratch, operands, spaces, {"gateup_grads": pl.ANY}
+    )
+
+
 def run_third(*operands):
     out = {
-        "grad_rows": ((HALF, D), F32),
         "grad_out": ((RING, RING, BLOCK, 384), LOW),
-        "grad_query": ((5, BLOCK, HD), LOW),
-        "grad_kv": ((RING, RING, BLOCK, HD), LOW),
+        "grad_got": ((RING, BLOCK, 384), LOW),
         "gateup_rows": ((RING, PAD, 2 * (MAIN + TAIL)), LOW),
         "output": ((BLOCK, D), F32),
     }
     scratch = [
         pltpu.VMEM((RING, HALF, D), LOW),
-        pltpu.VMEM((RING, HALF, D), LOW),
         pltpu.VMEM((HALF, D), F32),
-        pltpu.VMEM((HALF, D), F32),
-        pltpu.VMEM((BLOCK, D), LOW),
-        pltpu.VMEM((RING, BLOCK, D), LOW),
         pltpu.VMEM((RING, BLOCK, 384), LOW),
         pltpu.VMEM((RING, BLOCK, 384), LOW),
         pltpu.VMEM((5, BLOCK, HD), LOW),
@@ -1045,12 +1157,16 @@
         pltpu.VMEM((5, BLOCK, HD), F32),
         pltpu.VMEM((2, RING, RING, BLOCK, HD), LOW),
         pltpu.VMEM((RING, RING, BLOCK, HD), LOW),
-        *reduce_scratch(),
+        pltpu.VMEM((RING, RING, BLOCK, HD), LOW),
+        pltpu.VMEM((5, BLOCK, HD), F32),
+        pltpu.VMEM((RING, BLOCK, 384), LOW),
+        pltpu.VMEM((BLOCK, HD), F32),
         *reduce_scratch(),
         *plane_reduce_scratch(2 * (MAIN + TAIL)),
+        *plane_reduce_scratch(HD),
     ]
-    spaces = [pl.ANY] * 3 + [pltpu.VMEM] * 11
-    return call(third_kernel, 2, 90, out, scratch, operands, spaces)
+    spaces = [pl.ANY] * 2 + [pltpu.VMEM] * 12
+    return call(third_kernel, 2, 100, out, scratch, operands, spaces)
 
 
 def run_fourth(*operands):
@@ -1062,23 +1178,17 @@
         "qkv_got": ((RING, PAD, 384), LOW),
     }
     scratch = [
-        pltpu.VMEM((RING, BLOCK, 384), LOW),
-        pltpu.VMEM((RING, BLOCK, 384), LOW),
-        pltpu.VMEM((BLOCK, HD), F32),
         pltpu.VMEM((RING, BLOCK, D), LOW),
         pltpu.VMEM((HALF, D), F32),
         pltpu.VMEM((RING, RING, BLOCK, 384), LOW),
-        pltpu.VMEM((RING, PAD, 1024), LOW),
         pltpu.VMEM((RING, PAD, 384), LOW),
         pltpu.VMEM((RING, PAD, 384), LOW),
         *reduce_scratch(),
-        *plane_reduce_scratch(HD),
-        *plane_reduce_scratch(1024),
         *plane_reduce_scratch(384),
         *plane_reduce_scratch(384),
     ]
-    spaces = [pltpu.VMEM] * 3 + [pl.ANY] + [pltpu.VMEM] * 8
-    return call(fourth_kernel, 3, 130, out, scratch, operands, spaces)
+    spaces = [pltpu.VMEM] * 9
+    return call(fourth_kernel, 3, 80, out, scratch, operands, spaces)
 
 
 def adam_update(weight, gradient, first_moment, second_moment, learn_rate, decay_rate):
@@ -1094,10 +1204,6 @@
 
 def out_fan_in(seq_length):
     return max(1, H * HD * 4 // min(WINDOW, seq_length))
-
-
-def activate(gate_part, upper_part):
-    return jax.nn.gelu(gate_part, approximate=True) * upper_part
 
 
 def quarters(rows):
@@ -1162,12 +1268,16 @@
         axis=2,
     ).astype(LOW)
     attn_rows = pad_to(pad_to(attn_rows, 2, 768), 1, PAD)
-    gateup = w_gateup.astype(LOW).reshape(OWN, 2, RING, MAIN + TAIL).transpose(2, 0, 1, 3)
+    gateup = w_gateup.astype(LOW)
+    mains = RING * MAIN
     feed_rows = jnp.concatenate(
         [
-            gateup[..., :MAIN].reshape(RING, OWN, 2 * MAIN),
-            gateup[..., MAIN:].reshape(RING, OWN, 2 * TAIL),
-            quarters(w_down.T).astype(LOW),
+            quarters(gateup[:, 0, :mains]),
+            quarters(gateup[:, 1, :mains]),
+            quarters(gateup[:, 0, mains:]),
+            quarters(gateup[:, 1, mains:]),
+            quarters(w_down.T[:, :mains].astype(LOW)),
+            quarters(w_down.T[:, mains:].astype(LOW)),
         ],
         axis=2,
     )
@@ -1181,33 +1291,19 @@
     first = run_first(
         attn_rows, feed_rows, tokens, cotangent.astype(LOW), cos_table, sin_table, cos_kv, sin_kv
     )
-    feed_full = first["feed_full"].reshape(D, 2944)
-    gateup_full = feed_full[:, : 2 * (MAIN + TAIL)]
-    down_full = feed_full[:, 2 * (MAIN + TAIL) :]
-    dy_all = first["dy_all"].reshape(-1, D)
-    normed_two = first["normed_two"].reshape(-1, D)
-
-    gateup = dot(normed_two, gateup_full, (1, 0))
-    gate = jnp.concatenate([gateup[:, :MAIN], gateup[:, 2 * MAIN : 2 * MAIN + TAIL]], axis=1)
-    upper = jnp.concatenate([gateup[:, MAIN : 2 * MAIN], gateup[:, 2 * MAIN + TAIL :]], axis=1)
-    hidden, activate_back = jax.vjp(activate, gate, upper)
-    hidden_low = pad_to(hidden.astype(LOW), 1, 1024)
-    grad_hidden = dot(dy_all, down_full, (1, 0))[:, : MAIN + TAIL]
-    grad_gate, grad_upper = activate_back(grad_hidden)
-    grad_gateup_low = jnp.concatenate(
-        [grad_gate[:, :MAIN], grad_upper[:, :MAIN], grad_gate[:, MAIN:], grad_upper[:, MAIN:]], axis=1
-    ).astype(LOW)
-    norm_part = dot(grad_gateup_low, gateup_full, (1, 1)).astype(LOW).reshape(RING, BLOCK, D)
-    feed_part = dot(hidden_low, down_full, (1, 1)).astype(LOW).reshape(RING, BLOCK, D)
-    gateup_grads = dot(normed_two, grad_gateup_low, (0, 0)).astype(LOW)
-    down_grads = dot(dy_all, hidden_low, (0, 0)).astype(LOW)
-    third = run_third(
-        norm_part,
-        feed_part,
-        gateup_grads.reshape(RING, RING, BLOCK, -1),
+    second = run_second(
+        first["feed_full"],
+        first["normed_two"],
+        first["dy_all"],
         cotangent,
         first["residual"],
         first["gains"],
+    )
+    third = run_third(
+        second["feed_part"],
+        second["gateup_grads"],
+        second["da_all"],
+        first["residual"],
         first["attn_full"],
         first["att_slice"],
         first["query"],
@@ -1216,32 +1312,38 @@
         first["attended"],
         cos_table,
         sin_table,
+        cos_kv,
+        sin_kv,
     )
     fourth = run_fourth(
-        third["grad_kv"],
-        third["grad_query"],
+        third["grad_got"],
         third["gateup_rows"],
-        down_grads.reshape(RING, RING, BLOCK, -1),
+        second["down_rows"],
         third["grad_out"],
         first["attn_full"],
         first["normed_one"],
-        third["grad_rows"],
+        second["grad_rows"],
         tokens,
         first["gains"],
-        cos_kv,
-        sin_kv,
     )
     output, grad_tokens = third["output"], fourth["grad_tokens"]
 
     gateup_shard = fourth["gateup_got"][:, :OWN].astype(F32)
-    gateup_shard = jnp.concatenate(
+    down_shard = fourth["down_got"][:, :OWN].astype(F32)
+
+    def hidden_units(grads, main, tail):
+        return jnp.concatenate(
+            [whole(grads[..., main : main + MAIN]), whole(grads[..., tail : tail + TAIL])], axis=1
+        )
+
+    gateup_shard = jnp.stack(
         [
-            gateup_shard[..., : 2 * MAIN].reshape(RING, OWN, 2, MAIN),
-            gateup_shard[..., 2 * MAIN :].reshape(RING, OWN, 2, TAIL),
+            hidden_units(gateup_shard, 0, 2 * MAIN),
+            hidden_units(gateup_shard, MAIN, 2 * MAIN + TAIL),
         ],
-        axis=3,
-    ).transpose(1, 2, 0, 3).reshape(OWN, 2, -1)
-    down_shard = whole(fourth["down_got"][:, :OWN, : MAIN + TAIL].astype(F32)).T
+        axis=1,
+    )
+    down_shard = hidden_units(down_shard, 0, MAIN).T
     out_shard = whole_heads(fourth["out_got"][:, :OWN, :320].astype(F32)).T
     qkv_shard = fourth["qkv_got"][:, :OWN].astype(F32)
     query_shard = whole_heads(qkv_shard[..., :320])

time: 462 us -> 426 us (0.922)
  matrix products: 59.1 us -> 0 us
  Pallas kernels: 339 us -> 381 us
  other arithmetic: 25.5 us -> 13.1 us
  local copies, waits for them, and re-layouts: 32.5 us -> 24.5 us
    dot_general x6 -> x0, matrix products: 59.1 us -> none  [dot(): lax.dot_general(left_side, right_side, ((contract[:1], contract[1:]), (()...]
    pallas_call x2 -> x3, Pallas kernels: 166 us -> 207 us  [call(): pl.pallas_call(kernel, out_shape=[jax.ShapeDtypeStruct(shape, kind) for s...]
    reshape x7 -> x2, local copies, waits for them, and re-layouts: 10.7 us -> 0.12 us  [quarters(): return rows.reshape(OWN, RING, -1).transpose(1, 0, 2)]
    unnamed x64 -> x82, local copies, waits for them, and re-layouts: 8.16 us -> 17.1 us
where the time goes in v4:
time: 426 us; the launch traced here: 420 us
  Pallas kernels  381 us (89%)
  local copies, waits for them, and re-layouts  24.5 us (6%)
  other arithmetic  13.1 us (3%)
    pallas_call x3, Pallas kernels, call(): pl.pallas_call(kernel, out_shape=[jax.ShapeDtypeStruct(shape, kind) for s...  207 us
    pallas_call x1, Pallas kernels, run_first(): pl.pallas_call(first_kernel, out_shape=[jax.ShapeDtypeStruct(shape, kind)...  166 us
    unnamed x82, local copies, waits for them, and re-layouts  17.1 us

profile of v4, /device:TPU:1, one launch (start us, length us, event | category | flops | bytes accessed | tf_op | source)
XLA Modules:
  0.0 420.2 jit_solution(9008122447719312805)
XLA Ops:
  1.3 0.8 broadcast_select_fusion
  4.7 0.8 copy_bitcast_fusion
  6.9 1.1 pad.60.feed_rows
  7.9 0.8 copy-done
  8.7 1.0 convert_element_type.61.dy
  9.7 166.3 %shard_map.347 = (bf16[4,4,160,2944]{3,2,1,0:T(8,128)(2,1)}, bf16[4,4,160,768]{3,2,1,0:T(8,128)(2,1)}, bf16[4,160,2560]{2,1,0:T(8,128)(2,1)}, bf16[4,160,2560]{2...) custom-call(bf16[4,48,768]{2,1,0:T(8,128)(2,1)} %pad.25.attn_rows, ...), custom_call_target="tpu_custom_call" | custom-call | tf_op jit(solution)/shard_map/pallas_call | solution.py:489
  176.0 79.0 %shard_map.348 = (f32[80,2560]{1,0:T(8,128)}, bf16[4,160,2560]{2,1,0:T(8,128)(2,1)}, bf16[4,160,2560]{2,1,0:T(8,128)(2,1)}, bf16[4,4,160,1920]{3,2,1,0:T(8,128)(2,1)}, bf16[4,48,1024]{2,1,0:T(8,128)(2,1)}) custom-call(bf16[4,4,160,2944]{3,2,1,0:T(8,128)(2,1)} %get-tuple-element.46.feed_full, bf16[4,160,2560]{2,1,0:T(8,128)(2,1)} %get-tuple-element.47.normed_two, ...), custom_call_target="tpu_custom_call" | custom-call | tf_op jit(solution)/shard_map/pallas_call | solution.py:1095
  255.0 79.8 %shard_map.349 = (bf16[4,4,160,384]{3,2,1,0:T(8,128)(2,1)}, bf16[4,160,384]{2,1,0:T(8,128)(2,1)}, bf16[4,48,1920]{2,1,0:T(8,128)(2,1)}, f32[160,2560]{1,0:T(8,128)}) custom-call(bf16[4,160,2560]{2,1,0:T(8,128)(2,1)} %get-tuple-element.51.feed_part, bf16[4,4,160,1920]{3,2,1,0:T(8,128)(2,1)} %get-tuple-element.52.gateup_grads, ...), custom_call_target="tpu_custom_call" | custom-call | tf_op jit(solution)/shard_map/pallas_call | solution.py:1095
  334.8 48.2 %shard_map.350 = (f32[160,2560]{1,0:T(8,128)}, bf16[4,48,1920]{2,1,0:T(8,128)(2,1)}, bf16[4,48,1024]{2,1,0:T(8,128)(2,1)}, bf16[4,48,384]{2,1,0:T(8,128)(2,1)}, bf16[4,48,384]{2,1,0:T(8,128)(2,1)}) custom-call(bf16[4,160,384]{2,1,0:T(8,128)(2,1)} %get-tuple-element.61.grad_got, bf16[4,48,1920]{2,1,0:T(8,128)(2,1)} %get-tuple-element.62.gateup_rows, ...), custom_call_target="tpu_custom_call" | custom-call | tf_op jit(solution)/shard_map/pallas_call | solution.py:1095
  383.0 1.0 slice_convert_fusion.2
  384.3 1.0 multiply_subtract_fusion.3
  386.5 1.2 copy-done.9
  387.7 3.8 multiply_subtract_fusion
  392.6 7.5 %shard_map.351 = f32[48,384]{1,0:T(8,128)} custom-call(f32[48,384]{1,0:T(8,128)} %pad.29.x_ref), custom_call_target="tpu_custom_call" | custom-call | tf_op jit(solution)/shard_map/pallas_call | solution.py:99
  400.3 0.8 sqrt_add_fusion
  403.7 0.8 copy-done.5
  404.7 2.6 multiply_subtract_fusion.1
  408.5 0.9 multiply_subtract_fusion.2
  409.4 1.7 copy.234
  411.1 1.7 copy.237
  412.7 1.7 copy.240
  416.6 1.2 copy.285
  417.7 0.9 copy-done.7
  418.6 1.2 copy.286
  (161 shorter events, 12.8 us)
Async XLA Ops:
  0.7 1.5 copy-start.23
  0.7 1.7 copy-start.11
  0.7 1.9 copy-start.13
  1.3 1.6 copy-start.8
  2.8 1.6 copy-start.1
  6.8 1.8 copy-start
  383.0 1.3 copy-start.12
  383.0 1.3 copy-start.19
  383.0 1.3 copy-start.20
  384.0 1.5 copy-start.16
  386.5 1.3 copy-start.9
  387.7 12.4 %copy-start.29 = (f32[2,40]{1,0:T(2,128)S(1)}, f32[2,40]{1,0:T(2,128)}, u32[]{:S(2)}) copy-start(f32[2,40]{1,0:T(2,128)} %param.33) | copy-start | bytes 964
  387.7 12.5 %copy-start.30 = (f32[2,40]{1,0:T(2,128)S(1)}, f32[2,40]{1,0:T(2,128)}, u32[]{:S(2)}) copy-start(f32[2,40]{1,0:T(2,128)} %param.39) | copy-start | bytes 964
  391.6 11.8 %copy-start.17 = (bf16[4,48,1024]{2,1,0:T(8,128)(2,1)S(1)}, bf16[4,48,1024]{2,1,0:T(8,128)(2,1)}, u32[]{:S(2)}) copy-start(bf16[4,48,1024]{2,1,0:T(8,128)(2,1)} %get-tuple-element.71) | copy-start | bytes 1179652
  403.5 1.3 copy-start.15
  404.7 2.6 copy-start.25
  407.4 2.0 copy-start.3
  409.4 1.7 copy-start.2
  412.7 1.7 copy-start.18
  412.7 1.7 copy-start.24
  412.7 1.7 copy-start.26
  412.7 1.7 copy-start.27
  412.7 3.8 copy-start.6
  416.6 2.0 copy-start.7
  (7 other events, 7.2 us)

commit v5 on v4

--- a/solution.py
+++ b/solution.py
@@ -32,6 +32,7 @@
 PART = 48
 OWN = 40
 PAD = 48
+SPANS = ((0, 48, 32), (48, 32, 16))
 MAIN = 896
 TAIL = 64
 
@@ -116,19 +117,23 @@
         copy.wait_recv()
 
 
-def core_rows():
-    base = pl.multiple_of(lax.axis_index("tensor") * HALF, 16)
+def core_rows(lo=0, n=HALF, part=PART):
+    base = lax.axis_index("tensor") * HALF
+
+    def rows(start, size):
+        return pl.ds(pl.multiple_of(start, 16), size)
+
     return (
-        pl.ds(base, HALF),
-        pl.ds(base, PART),
-        pl.ds(pl.multiple_of(base + PART, 16), HALF - PART),
-        pl.ds(pl.multiple_of(HALF - base, 16), HALF),
-    )
-
-
-def gather_steps(mover, x, out):
+        rows(base + lo, n),
+        rows(base + lo, part),
+        rows(base + (lo + part), n - part),
+        rows(HALF - base + lo, n),
+    )
+
+
+def gather_steps(mover, x, out, span=(0, HALF, PART)):
     me, left, right, far = (step("z", d) for d in (0, -1, 1, 2))
-    half, first, last, _ = core_rows()
+    half, first, last, _ = core_rows(*span)
     to_right = mover.copy(x.at[half], out.at[me, half], {"z": right})
     to_left = mover.copy(x.at[half], out.at[me, half], {"z": left})
     yield
@@ -241,11 +246,12 @@
     cos_kv,
     sin_kv,
     feed_full,
-    attn_full,
+    attn_a,
+    attn_b,
     normed_one,
     dy_all,
     query,
-    keyvalue,
+    kv_out,
     log_total,
     att_slice,
     residual,
@@ -256,88 +262,92 @@
     recv_sem,
     local_sem,
     attn_got,
-    attn_mine,
+    mine_a,
+    mine_b,
+    weight_a,
+    weight_b,
     attn_stage,
     feed_got,
     feed_mine,
     feed_stage,
     unit_low,
     unit_all,
+    normed,
     qkv_send,
     qkv_got,
     kv_own,
+    keyvalue,
     scores,
     att_send,
     part,
-    other,
-    total,
-    part_a,
-    part_b,
-    from_left,
-    from_right,
+    sum_half,
     normed_low,
+    *bufs,
 ):
     z, x, y, core = (lax.axis_index(axis) for axis in ("z", "x", "dp", "tensor"))
-    left, right, far = (step("z", d) for d in (-1, 1, 2))
-    half, _, _, their_half = core_rows()
     plane = ("dp", "x")
-    greet(
-        [{"z": step("z", d)} for d in (1, 2, 3)] + plane_peers(("dp", "x")) + [sibling()]
-    )
+    saves = []
+
+    def save(src, dst):
+        saves.append(pltpu.make_async_copy(src, dst, local_sem.at[len(saves)]))
+        saves[-1].start()
+        return saves[-1]
+
+    greet([{"z": step("z", d)} for d in (1, 2, 3)] + plane_peers(plane) + [sibling()])
     mover = Mover(send_sem, recv_sem)
 
     attn_swap = exchange_steps(mover, attn_rows, attn_got)
     advance(attn_swap)
+    feed_swap = exchange_steps(mover, feed_rows, feed_got)
+    advance(feed_swap)
     values = tokens[...]
     unit = values * lax.rsqrt(jnp.mean(values * values, axis=-1, keepdims=True) + eps_norm)
     unit_low[...] = unit.astype(LOW)
     unit_gather = gather_steps(mover, unit_low, unit_all)
     advance(unit_gather)
-    feed_swap = exchange_steps(mover, feed_rows, feed_got)
-    advance(feed_swap)
-    unit_all[z] = unit_low[...]
     attn_got[z] = attn_rows[z]
     advance(attn_swap)
-    whole_rows(attn_got, attn_stage, attn_mine)
-    attn_gather = plane_gather_steps(mover, plane, attn_mine, attn_full)
-    advance(attn_gather)
-    attn_full[y, x] = attn_mine[...]
-    advance(unit_gather)
-    advance(attn_gather)
-    advance(attn_gather)
-    advance(attn_gather)
+    for i in range(RING):
+        attn_stage[i * OWN : (i + 1) * OWN] = attn_got[i].astype(F32)[:OWN]
+    mine_a[...] = attn_stage[:, :512].astype(LOW)
+    mine_b[...] = attn_stage[:, 512:].astype(LOW)
+    a_gather = plane_gather_steps(mover, plane, mine_a, weight_a)
+    advance(a_gather)
+    weight_a[y, x] = mine_a[...]
+    unit_all[z] = unit_low[...]
+    advance(a_gather)
     feed_got[z] = feed_rows[z]
-    advance(unit_gather)
+    advance(a_gather)
+    advance(a_gather)
     advance(feed_swap)
     whole_rows(feed_got, feed_stage, feed_mine)
-    feed_own = pltpu.make_async_copy(feed_mine, feed_full.at[y, x], local_sem.at[0])
-    feed_own.start()
-    advance(attn_gather)
-    advance(attn_gather)
-    feed_gather = plane_gather_steps(mover, plane, feed_mine, feed_full, cut=64, order=(1, 0))
+    feed_own = save(feed_mine, feed_full.at[y, x])
+    advance(unit_gather)
+    advance(a_gather)
+    advance(a_gather)
+    feed_gather = plane_gather_steps(mover, plane, feed_mine, feed_full)
     advance(feed_gather)
-    dy_gather = gather_steps(mover, dy, dy_all)
-    advance(dy_gather)
-    dy_own = pltpu.make_async_copy(dy, dy_all.at[z], local_sem.at[1])
-    dy_own.start()
     advance(unit_gather)
-    advance(attn_gather)
-
-    scale_cols = attn_full[:, :, :, 640:768].reshape(D, 128)
-    pick = (lanes((8, 128)) == 64 + lax.broadcasted_iota(jnp.int32, (8, 128), 0)).astype(LOW)
+    advance(unit_gather)
+    advance(a_gather)
+    save(weight_a, attn_a)
+
+    scale_cols = weight_a[:, :, :, 384:].reshape(D, 128)
+    pick = (lanes((8, 128)) == TAIL + lax.broadcasted_iota(jnp.int32, (8, 128), 0)).astype(LOW)
     gain_ref[...] = 1.0 + dot(pick, scale_cols, (1, 1))
-    qkv_weight = attn_full[:, :, :, :384].reshape(D, 384)
+    qkv_weight = weight_a[:, :, :, :384].reshape(D, 384)
     copies = []
     for d in (2, 1, 3, 0):
         block = step("z", d)
-        normed = (unit_all[block].astype(F32) * gain_ref[0:1, :]).astype(LOW)
-        normed_one[block] = normed
-        qkv_send[block] = dot(normed, qkv_weight, (1, 0)).astype(LOW)
+        rows = (unit_all[block].astype(F32) * gain_ref[0:1, :]).astype(LOW)
+        normed[block] = rows
+        qkv_send[block] = dot(rows, qkv_weight, (1, 0)).astype(LOW)
         if d:
             copies.append(mover.copy(qkv_send.at[block], qkv_got.at[z], {"z": block}))
+    save(normed, normed_one)
     qkv_got[z] = qkv_send[z]
+    feed_own.wait()
     advance(feed_gather)
-    feed_own.wait()
     for copy in copies:
         copy.wait_recv()
     low_lanes = lanes((BLOCK, 128)) < TAIL
@@ -362,15 +372,24 @@
         query[h, :, 128:] = (qkv_got[h, :, 128:256].astype(F32) * scale).astype(LOW)
     query[4, :, :128] = (turn(joined(0, 0), cos, sin) * scale).astype(LOW)
     query[4, :, 128:] = (joined(2, 0) * scale).astype(LOW)
+    b_gather = plane_gather_steps(mover, plane, mine_b, weight_b)
+    advance(b_gather)
+    weight_b[y, x] = mine_b[...]
     advance(kv_gather)
-    advance(feed_gather)
+    advance(b_gather)
+    for _ in range(2):
+        advance(kv_gather)
+        advance(b_gather)
+    for _ in range(2):
+        advance(kv_gather)
+        advance(b_gather)
+    for _ in range(2):
+        advance(feed_gather)
+    dy_gather = gather_steps(mover, dy, dy_all)
+    advance(dy_gather)
+    save(dy, dy_all.at[z])
     advance(kv_gather)
-    advance(kv_gather)
-    advance(kv_gather)
-    advance(kv_gather)
-    advance(feed_gather)
-    advance(dy_gather)
-    advance(kv_gather)
+    save(keyvalue, kv_out)
 
     start = (x * RING + z) * BLOCK
     chunk = RING * BLOCK
@@ -403,125 +422,122 @@
 
     lax.fori_loop(0, 5, one_head, 0)
     for j in range(RING):
-        att_send[j, :, :256] = attended[j].astype(LOW)
+        att_send[j, :, 128:] = attended[j].astype(LOW)
         tile = attended[4, :, (j // 2) * 128 : (j // 2 + 1) * 128]
         tile = pltpu.roll(tile, TAIL, 1) if j % 2 else tile
-        att_send[j, :, 256:] = jnp.where(low_lanes, tile, 0.0).astype(LOW)
+        att_send[j, :, :128] = jnp.where(low_lanes, tile, 0.0).astype(LOW)
     att_swap = exchange_steps(mover, att_send, att_slice)
     advance(att_swap)
     att_slice[z] = att_send[z]
-    advance(dy_gather)
     advance(att_swap)
 
-    out_weight = attn_full[:, :, :, 384:].reshape(D, 384)
-    blocks = (far, right, left, z)
+    advance(b_gather)
+    save(weight_b, attn_b)
+
+    last_weight = weight_a[:, :, :, 384:].reshape(D, 128)
+    main_weight = weight_b[...].reshape(D, HD)
+
+    def make(block):
+        rows = dot(att_slice[block, :, :128], last_weight, (1, 1))
+        part[block] = (rows + dot(att_slice[block, :, 128:], main_weight, (1, 1))).astype(LOW)
+
     shares = []
-    for slot, block in enumerate(blocks):
-        part[block] = dot(att_slice[block], out_weight, (1, 1)).astype(LOW)
-        shares.append(mover.copy(part.at[block, their_half], other.at[slot], sibling()))
-
-    def both(slot):
-        return part[blocks[slot], half].astype(F32) + other[slot].astype(F32)
-
-    shares[0].wait_recv()
-    total[0] = both(0).astype(LOW)
-    far_right = mover.copy(total.at[0, pl.ds(0, PART)], part_a, {"z": right})
-    far_left = mover.copy(total.at[0, pl.ds(PART, HALF - PART)], part_b, {"z": left})
-    shares[1].wait_recv()
-    shares[2].wait_recv()
-    far_right.wait_recv()
-    summed = both(1)
-    total[1, :PART] = (summed[:PART] + part_a[...].astype(F32)).astype(LOW)
-    total[1, PART:] = summed[PART:].astype(LOW)
-    to_right = mover.copy(total.at[1], from_left, {"z": right})
-    far_left.wait_recv()
-    summed = both(2)
-    total[2, :PART] = summed[:PART].astype(LOW)
-    total[2, PART:] = (summed[PART:] + part_b[...].astype(F32)).astype(LOW)
-    to_left = mover.copy(total.at[2], from_right, {"z": left})
-    shares[3].wait_recv()
-    to_right.wait_recv()
-    to_left.wait_recv()
-    rows = tokens[half, :] + (
-        both(3) + from_left[...].astype(F32) + from_right[...].astype(F32)
-    )
-    residual[half, :] = rows
-    res_share = mover.copy(residual.at[half], residual.at[half], sibling())
+    sharing = share_steps(mover, part, bufs[0], shares, make)
+    advance(sharing)
+    advance(sharing)
+    sums = [
+        reduce_steps(mover, own_rows(part), shares[i], bufs, sum_half, span)
+        for i, span in enumerate(SPANS)
+    ]
+    for one in sums:
+        advance(one)
+    advance(sharing)
+    advance(sharing)
+    for one in sums:
+        advance(one)
 
     def normed_rows(rows):
         unit = rows * lax.rsqrt(jnp.mean(rows * rows, axis=-1, keepdims=True) + eps_norm)
         return (unit * gain_ref[1:2, :]).astype(LOW)
 
-    normed_low[half, :] = normed_rows(rows)
-    normed_gather = gather_steps(mover, normed_low, normed_two)
-    advance(normed_gather)
-    res_share.wait_recv()
-    normed_low[their_half, :] = normed_rows(residual[their_half, :])
-    normed_two[z] = normed_low[...]
-    advance(normed_gather)
+    gathers, res_shares = [], []
+    for one, span in zip(sums, SPANS, strict=True):
+        advance(one)
+        place = core_rows(*span)[0]
+        rows = tokens[place, :] + sum_half[span[0] : span[0] + span[1]]
+        residual[place, :] = rows
+        normed_low[place, :] = normed_rows(rows)
+        gathers.append(gather_steps(mover, normed_low, normed_two, span))
+        advance(gathers[-1])
+        res_shares.append(mover.copy(residual.at[place], residual.at[place], sibling()))
+    advance(dy_gather)
+    for copy in res_shares:
+        copy.wait_recv()
+    theirs = core_rows()[3]
+    normed_low[theirs, :] = normed_rows(residual[theirs, :])
+    save(normed_low, normed_two.at[z])
+    for one in gathers:
+        advance(one)
     advance(feed_gather)
-    advance(normed_gather)
     advance(feed_gather)
+    for one in gathers:
+        advance(one)
     advance(dy_gather)
-    advance(normed_gather)
+    for one in gathers:
+        advance(one)
+    advance(dy_gather)
     advance(feed_gather)
-    dy_own.wait()
+    for one in saves:
+        if one is not feed_own:
+            one.wait()
     mover.finish()
 
 
 def run_first(*operands):
     out = {
-        "feed_full": ((RING, RING, BLOCK, 2944), LOW, pl.ANY),
-        "attn_full": ((RING, RING, BLOCK, 768), LOW, pltpu.VMEM),
-        "normed_one": ((RING, BLOCK, D), LOW, pltpu.VMEM),
-        "dy_all": ((RING, BLOCK, D), LOW, pl.ANY),
-        "query": ((5, BLOCK, HD), LOW, pltpu.VMEM),
-        "keyvalue": ((2, RING, RING, BLOCK, HD), LOW, pltpu.VMEM),
-        "log_total": ((5, BLOCK, 128), F32, pltpu.VMEM),
-        "att_slice": ((RING, BLOCK, 384), LOW, pltpu.VMEM),
-        "residual": ((BLOCK, D), F32, pltpu.VMEM),
-        "normed_two": ((RING, BLOCK, D), LOW, pltpu.VMEM),
-        "attended": ((5, BLOCK, HD), F32, pltpu.VMEM),
-        "gains": ((8, D), F32, pltpu.VMEM),
+        "feed_full": ((RING, RING, BLOCK, 2944), LOW),
+        "attn_a": ((RING, RING, BLOCK, 512), LOW),
+        "attn_b": ((RING, RING, BLOCK, HD), LOW),
+        "normed_one": ((RING, BLOCK, D), LOW),
+        "dy_all": ((RING, BLOCK, D), LOW),
+        "query": ((5, BLOCK, HD), LOW),
+        "keyvalue": ((2, RING, RING, BLOCK, HD), LOW),
+        "log_total": ((5, BLOCK, 128), F32),
+        "att_slice": ((RING, BLOCK, 384), LOW),
+        "residual": ((BLOCK, D), F32),
+        "normed_two": ((RING, BLOCK, D), LOW),
+        "attended": ((5, BLOCK, HD), F32),
+        "gains": ((8, D), F32),
     }
+    remote = ("feed_full", "attn_a", "attn_b", "normed_one", "dy_all", "keyvalue", "normed_two")
     spaces = [pltpu.VMEM, pltpu.VMEM, pltpu.VMEM, pl.ANY] + [pltpu.VMEM] * 4
-    copies = 120
-    results = pl.pallas_call(
-        first_kernel,
-        out_shape=[jax.ShapeDtypeStruct(shape, kind) for shape, kind, _ in out.values()],
-        in_specs=[pl.BlockSpec(memory_space=space) for space in spaces],
-        out_specs=[pl.BlockSpec(memory_space=space) for _, _, space in out.values()],
-        scratch_shapes=[
-            pltpu.SemaphoreType.DMA((copies,)),
-            pltpu.SemaphoreType.DMA((copies,)),
-            pltpu.SemaphoreType.DMA((2,)),
-            pltpu.VMEM((RING, PAD, 768), LOW),
-            pltpu.VMEM((BLOCK, 768), LOW),
-            pltpu.VMEM((BLOCK, 768), F32),
-            pltpu.VMEM((RING, PAD, 2944), LOW),
-            pltpu.VMEM((BLOCK, 2944), LOW),
-            pltpu.VMEM((BLOCK, 2944), F32),
-            pltpu.VMEM((BLOCK, D), LOW),
-            pltpu.VMEM((RING, BLOCK, D), LOW),
-            pltpu.VMEM((RING, BLOCK, 384), LOW),
-            pltpu.VMEM((RING, BLOCK, 384), LOW),
-            pltpu.VMEM((BLOCK, HD), LOW),
-            pltpu.VMEM((BLOCK, RING * RING * BLOCK), F32),
-            pltpu.VMEM((RING, BLOCK, 384), LOW),
-            pltpu.VMEM((RING, BLOCK, D), LOW),
-            pltpu.VMEM((4, HALF, D), LOW),
-            pltpu.VMEM((3, HALF, D), LOW),
-            pltpu.VMEM((PART, D), LOW),
-            pltpu.VMEM((HALF - PART, D), LOW),
-            pltpu.VMEM((HALF, D), LOW),
-            pltpu.VMEM((HALF, D), LOW),
-            pltpu.VMEM((BLOCK, D), LOW),
-        ],
-        compiler_params=pltpu.CompilerParams(
-            collective_id=1, has_side_effects=True, vmem_limit_bytes=60 * 1024 * 1024
-        ),
-    )(*operands)
-    return dict(zip(out, results, strict=True))
+    scratch = [
+        pltpu.VMEM((RING, PAD, 768), LOW),
+        pltpu.VMEM((BLOCK, 512), LOW),
+        pltpu.VMEM((BLOCK, HD), LOW),
+        pltpu.VMEM((RING, RING, BLOCK, 512), LOW),
+        pltpu.VMEM((RING, RING, BLOCK, HD), LOW),
+        pltpu.VMEM((BLOCK, 768), F32),
+        pltpu.VMEM((RING, PAD, 2944), LOW),
+        pltpu.VMEM((BLOCK, 2944), LOW),
+        pltpu.VMEM((BLOCK, 2944), F32),
+        pltpu.VMEM((BLOCK, D), LOW),
+        pltpu.VMEM((RING, BLOCK, D), LOW),
+        pltpu.VMEM((RING, BLOCK, D), LOW),
+        pltpu.VMEM((RING, BLOCK, 384), LOW),
+        pltpu.VMEM((RING, BLOCK, 384), LOW),
+        pltpu.VMEM((BLOCK, HD), LOW),
+        pltpu.VMEM((2, RING, RING, BLOCK, HD), LOW),
+        pltpu.VMEM((BLOCK, RING * RING * BLOCK), F32),
+        pltpu.VMEM((RING, BLOCK, 384), LOW),
+        pltpu.VMEM((RING, BLOCK, D), LOW),
+        pltpu.VMEM((HALF, D), F32),
+        pltpu.VMEM((BLOCK, D), LOW),
+        *reduce_scratch(),
+    ]
+    return call(
+        first_kernel, 1, 150, out, scratch, operands, spaces, {name: pl.ANY for name in remote}
+    )
 
 
 def plane_reduce_steps(mover, axes, g, bufs, res, loads=None):
@@ -651,51 +667,68 @@
     ]
 
 
-def reduce_steps(mover, part, mine, bufs, out, make=None):
-    other, total, part_a, part_b, from_left, from_right = bufs
-    _, _, _, their_half = core_rows()
+def share_steps(mover, part, other, shares, make=None, spans=SPANS):
+    me, left, right, far = (step("z", d) for d in (0, -1, 1, 2))
+    shares.extend([] for _ in spans)
+    for slot, block in enumerate((far, right, left, me)):
+        if make is not None:
+            make(block)
+        for copies, (lo, n, first) in zip(shares, spans, strict=True):
+            theirs = core_rows(lo, n, first)[3]
+            copies.append(
+                mover.copy(part.at[block, theirs], other.at[slot, pl.ds(lo, n)], sibling())
+            )
+        yield
+
+
+def reduce_steps(mover, mine, shares, bufs, out, span):
+    other, total, far_in, from_left, from_right = bufs
+    lo, n, part = span
     me, left, right, far = (step("z", d) for d in (0, -1, 1, 2))
     blocks = (far, right, left, me)
-    shares = []
-    for slot, block in enumerate(blocks):
-        if make is not None:
-            make(block)
-        shares.append(mover.copy(part.at[block, their_half], other.at[slot], sibling()))
-    yield
+    rows, first, last = pl.ds(lo, n), pl.ds(lo, part), pl.ds(lo + part, n - part)
 
     def both(slot):
-        return mine(blocks[slot]).astype(F32) + other[slot].astype(F32)
+        return mine(blocks[slot], span).astype(F32) + other[slot, rows].astype(F32)
 
     shares[0].wait_recv()
-    total[0] = both(0).astype(LOW)
-    far_right = mover.copy(total.at[0, pl.ds(0, PART)], part_a, {"z": right})
-    far_left = mover.copy(total.at[0, pl.ds(PART, HALF - PART)], part_b, {"z": left})
+    total[0, rows] = both(0).astype(LOW)
+    far_right = mover.copy(total.at[0, first], far_in.at[first], {"z": right})
+    far_left = mover.copy(total.at[0, last], far_in.at[last], {"z": left})
     yield
     shares[1].wait_recv()
+    summed = both(1)
+    far_right.wait_recv()
+    total[1, first] = (summed[:part] + far_in[first].astype(F32)).astype(LOW)
+    total[1, last] = summed[part:].astype(LOW)
+    to_right = mover.copy(total.at[1, rows], from_left.at[rows], {"z": right})
     shares[2].wait_recv()
-    far_right.wait_recv()
-    summed = both(1)
-    total[1, :PART] = (summed[:PART] + part_a[...].astype(F32)).astype(LOW)
-    total[1, PART:] = summed[PART:].astype(LOW)
-    to_right = mover.copy(total.at[1], from_left, {"z": right})
+    summed = both(2)
     far_left.wait_recv()
-    summed = both(2)
-    total[2, :PART] = summed[:PART].astype(LOW)
-    total[2, PART:] = (summed[PART:] + part_b[...].astype(F32)).astype(LOW)
-    to_left = mover.copy(total.at[2], from_right, {"z": left})
+    total[2, first] = summed[:part].astype(LOW)
+    total[2, last] = (summed[part:] + far_in[last].astype(F32)).astype(LOW)
+    to_left = mover.copy(total.at[2, rows], from_right.at[rows], {"z": left})
     yield
     shares[3].wait_recv()
+    summed = both(3)
     to_right.wait_recv()
     to_left.wait_recv()
-    out[...] = both(3) + from_left[...].astype(F32) + from_right[...].astype(F32)
+    out[rows] = summed + from_left[rows].astype(F32) + from_right[rows].astype(F32)
+
+
+def own_rows(ref):
+    return lambda block, span: ref[block, core_rows(*span)[0]]
+
+
+def half_rows(ref):
+    return lambda block, span: ref[block, pl.ds(span[0], span[1])]
 
 
 def reduce_scratch():
     return [
         pltpu.VMEM((4, HALF, D), LOW),
         pltpu.VMEM((3, HALF, D), LOW),
-        pltpu.VMEM((PART, D), LOW),
-        pltpu.VMEM((HALF - PART, D), LOW),
+        pltpu.VMEM((HALF, D), LOW),
         pltpu.VMEM((HALF, D), LOW),
         pltpu.VMEM((HALF, D), LOW),
     ]
@@ -731,6 +764,8 @@
     send_sem,
     recv_sem,
     local_sem,
+    normed_in,
+    dy_in,
     gateup_weight,
     down_weight,
     hidden,
@@ -749,12 +784,17 @@
     gu_width = 2 * (MAIN + TAIL)
     wide = RING * BLOCK
     loads = [
-        pltpu.make_async_copy(feed_full.at[:, :, :, pl.ds(0, gu_width)], gateup_weight, local_sem.at[0]),
-        pltpu.make_async_copy(
-            feed_full.at[:, :, :, pl.ds(gu_width, 1024)], down_weight, local_sem.at[1]
-        ),
-        pltpu.make_async_copy(cotangent.at[half], cot_half, local_sem.at[2]),
-        pltpu.make_async_copy(residual.at[half], res_half, local_sem.at[3]),
+        pltpu.make_async_copy(src, dst, local_sem.at[i])
+        for i, (src, dst) in enumerate(
+            (
+                (normed_two, normed_in),
+                (feed_full.at[:, :, :, pl.ds(0, gu_width)], gateup_weight),
+                (dy_all, dy_in),
+                (feed_full.at[:, :, :, pl.ds(gu_width, 1024)], down_weight),
+                (cotangent.at[half], cot_half),
+                (residual.at[half], res_half),
+            )
+        )
     ]
     for load in loads:
         load.start()
@@ -769,16 +809,16 @@
 
     for lo, n in ((0, 256), (256, 256), (512, 256), (768, 128)):
         value, grad_gate, grad_upper = activation(
-            product(normed_two, gateup_weight, lo, n),
-            product(normed_two, gateup_weight, MAIN + lo, n),
-            product(dy_all, down_weight, lo, n),
+            product(normed_in, gateup_weight, lo, n),
+            product(normed_in, gateup_weight, MAIN + lo, n),
+            product(dy_in, down_weight, lo, n),
         )
         hidden[:, lo : lo + n] = value.astype(LOW)
         dgu[:, lo : lo + n] = grad_gate.astype(LOW)
         dgu[:, MAIN + lo : MAIN + lo + n] = grad_upper.astype(LOW)
-    both = product(normed_two, gateup_weight, 2 * MAIN, 2 * TAIL)
+    both = product(normed_in, gateup_weight, 2 * MAIN, 2 * TAIL)
     value, grad_gate, grad_upper = activation(
-        both, pltpu.roll(both, TAIL, 1), product(dy_all, down_weight, MAIN, 2 * TAIL)
+        both, pltpu.roll(both, TAIL, 1), product(dy_in, down_weight, MAIN, 2 * TAIL)
     )
     low_lanes = lanes(both.shape) < TAIL
     hidden[:, MAIN:] = jnp.where(low_lanes, value, 0.0).astype(LOW)
@@ -787,63 +827,79 @@
     for i in range(RING):
         part = dot(dgu[...], gateup_weight[i].reshape(wide, gu_width), (1, 1))
         norm_part[:, :, i * wide : (i + 1) * wide] = part.astype(LOW).reshape(RING, BLOCK, wide)
-    norm_sum = reduce_steps(mover, norm_part, lambda i: norm_part[i, half], bufs[:6], grad_half)
-    advance(norm_sum)
+    shares = []
+    sharing = share_steps(mover, norm_part, bufs[0], shares)
+    for _ in range(RING):
+        advance(sharing)
+    sums = [
+        reduce_steps(mover, own_rows(norm_part), shares[i], bufs[:5], grad_half, span)
+        for i, span in enumerate(SPANS)
+    ]
 
     for i in range(RING):
-        part = dot(hidden[...], down_weight[i].reshape(wide, 1024), (1, 1))
-        feed_part[:, :, i * wide : (i + 1) * wide] = part.astype(LOW).reshape(RING, BLOCK, wide)
-        if i == 0:
-            advance(norm_sum)
+        terms = dot(hidden[...], down_weight[i].reshape(wide, 1024), (1, 1))
+        feed_part[:, :, i * wide : (i + 1) * wide] = terms.astype(LOW).reshape(RING, BLOCK, wide)
+        if i < 2:
+            advance(sums[i])
 
     def columns(rows, i):
         return rows[:, :, i * wide : (i + 1) * wide].reshape(wide, wide)
 
     for i in range(RING):
-        grads = dot(columns(dy_all, i), hidden[...], (0, 0))
+        grads = dot(columns(dy_in, i), hidden[...], (0, 0))
         down_weight[i] = grads.astype(LOW).reshape(RING, BLOCK, 1024)
-        if i == 1:
-            advance(norm_sum)
-    down_sum = plane_reduce_steps(mover, plane, down_weight, bufs[6:11], bufs[11])
+        if i < 2:
+            advance(sums[i])
+    down_sum = plane_reduce_steps(mover, plane, down_weight, bufs[5:10], bufs[10])
     advance(down_sum)
     saved = []
 
     def gateup_block(i):
         if saved:
             saved[-1].wait()
-        grads = dot(columns(normed_two, i), dgu[...], (0, 0))
+        grads = dot(columns(normed_in, i), dgu[...], (0, 0))
         stage[...] = grads.astype(LOW).reshape(RING, BLOCK, gu_width)
-        saved.append(pltpu.make_async_copy(stage, gateup_grads.at[i], local_sem.at[4 + i]))
+        saved.append(pltpu.make_async_copy(stage, gateup_grads.at[i], local_sem.at[10 + i]))
         saved[-1].start()
 
     gateup_block(0)
-    advance(norm_sum)
-    rows = res_half[...]
-    inverse = lax.rsqrt(jnp.mean(rows * rows, axis=-1, keepdims=True) + eps_norm)
-    unit = rows * inverse
-    scaled = grad_half[...] * gain_ref[1:2, :]
-    grad = cot_half[...] + inverse * (
-        scaled - unit * jnp.mean(scaled * unit, axis=-1, keepdims=True)
-    )
-    grad_rows[...] = grad
-    da_low[half, :] = grad.astype(LOW)
-    da_share = mover.copy(da_low.at[half], da_low.at[half], sibling())
-    da_gather = gather_steps(mover, da_low, da_all)
-    advance(da_gather)
+    gathers, da_shares = [], []
+    for one, span in zip(sums, SPANS, strict=True):
+        advance(one)
+        piece = pl.ds(span[0], span[1])
+        place = core_rows(*span)[0]
+        rows = res_half[piece, :]
+        inverse = lax.rsqrt(jnp.mean(rows * rows, axis=-1, keepdims=True) + eps_norm)
+        unit = rows * inverse
+        scaled = grad_half[piece, :] * gain_ref[1:2, :]
+        grad = cot_half[piece, :] + inverse * (
+            scaled - unit * jnp.mean(scaled * unit, axis=-1, keepdims=True)
+        )
+        grad_rows[piece, :] = grad
+        da_low[place, :] = grad.astype(LOW)
+        gathers.append(gather_steps(mover, da_low, da_all, span))
+        advance(gathers[-1])
+        da_shares.append(mover.copy(da_low.at[place], da_low.at[place], sibling()))
     advance(down_sum)
     gateup_block(1)
-    da_share.wait_recv()
-    da_all[z] = da_low[...]
-    advance(da_gather)
+    for copy in da_shares:
+        copy.wait_recv()
+    da_own = pltpu.make_async_copy(da_low, da_all.at[z], local_sem.at[9])
+    da_own.start()
+    for one in gathers:
+        advance(one)
     gateup_block(2)
     advance(down_sum)
-    advance(da_gather)
+    for one in gathers:
+        advance(one)
     gateup_block(3)
     advance(down_sum)
-    advance(da_gather)
+    for one in gathers:
+        advance(one)
     advance(down_sum)
-    spread_rows(bufs[11], down_rows)
+    spread_rows(bufs[10], down_rows)
     saved[-1].wait()
+    da_own.wait()
     mover.finish()
 
 
@@ -852,10 +908,11 @@
     gateup_grads,
     da_all,
     residual,
-    attn_full,
+    attn_a,
+    attn_b,
     att_slice,
     query,
-    keyvalue,
+    kv_hbm,
     log_total,
     attended,
     cos_ref,
@@ -869,6 +926,10 @@
     send_sem,
     recv_sem,
     local_sem,
+    da_in,
+    last_weight,
+    main_weight,
+    keyvalue,
     feed_mine,
     out_half,
     datt_send,
@@ -888,42 +949,66 @@
 ):
     z, core = lax.axis_index("z"), lax.axis_index("tensor")
     x = lax.axis_index("x")
-    half, _, _, their_half = core_rows()
-    out_bufs, rows_bufs, rows_res = bufs[:6], bufs[6:11], bufs[11]
-    kv_bufs, kv_rows = bufs[12:17], bufs[17]
-    feed_load = pltpu.make_async_copy(feed_part.at[:, half], feed_mine, local_sem.at[9])
-    feed_load.start()
+    half = core_rows()[0]
+    whole_span = ((0, HALF, PART),)
+    out_bufs, rows_bufs, rows_res = bufs[:5], bufs[5:10], bufs[10]
+    kv_bufs, kv_rows = bufs[11:16], bufs[16]
+    loads = [
+        pltpu.make_async_copy(src, dst, local_sem.at[8 + i])
+        for i, (src, dst) in enumerate(
+            (
+                (da_all, da_in),
+                (attn_a.at[:, :, :, pl.ds(384, 128)], last_weight),
+                (attn_b, main_weight),
+                (kv_hbm, keyvalue),
+                (feed_part.at[:, half], feed_mine),
+            )
+        )
+    ]
+    for load in loads:
+        load.start()
     greet([{"z": step("z", d)} for d in (1, 2, 3)] + plane_peers(("dp", "x")) + [sibling()])
     mover = Mover(send_sem, recv_sem)
     rows_sum = plane_reduce_steps(
         mover, ("dp", "x"), gateup_grads, rows_bufs, rows_res, loads=local_sem
     )
     advance(rows_sum)
-    feed_sum = reduce_steps(mover, feed_part, lambda i: feed_mine[i], out_bufs, out_half)
-    out_weight = attn_full[:, :, :, 384:].reshape(D, 384)
+    for load in loads[:3]:
+        load.wait()
+    last = last_weight[...].reshape(D, 128)
+    main = main_weight[...].reshape(D, HD)
     copies = []
     for d in (2, 1, 3, 0):
         block = step("z", d)
-        datt_send[block] = dot(da_all[block], out_weight, (1, 0)).astype(LOW)
+        datt_send[block, :, :128] = dot(da_in[block], last, (1, 0)).astype(LOW)
+        datt_send[block, :, 128:] = dot(da_in[block], main, (1, 0)).astype(LOW)
         if d:
             copies.append(mover.copy(datt_send.at[block], datt_got.at[z], {"z": block}))
     datt_got[z] = datt_send[z]
-    advance(feed_sum)
+    shares = []
+    sharing = share_steps(mover, feed_part, out_bufs[0], shares, spans=whole_span)
+    for _ in range(RING):
+        advance(sharing)
+    feed_sum = reduce_steps(
+        mover, half_rows(feed_mine), shares[0], out_bufs, out_half, whole_span[0]
+    )
     slices = att_slice[...].reshape(RING * BLOCK, 384)
     wide = RING * BLOCK
     for i in range(RING):
-        left_side = da_all[:, :, i * wide : (i + 1) * wide].reshape(wide, wide)
+        left_side = da_in[:, :, i * wide : (i + 1) * wide].reshape(wide, wide)
         grad_out[i] = dot(left_side, slices, (0, 0)).astype(LOW).reshape(RING, BLOCK, 384)
     for copy in copies:
         copy.wait_recv()
-    feed_load.wait()
+    for load in loads[3:]:
+        load.wait()
     advance(feed_sum)
+    advance(rows_sum)
 
     low_lanes = lanes((BLOCK, 128)) < TAIL
     for h in range(4):
-        datt[h] = datt_got[h, :, :HD]
+        datt[h] = datt_got[h, :, 128:]
     for k in range(2):
-        one, two = (datt_got[2 * k + i, :, HD:].astype(F32) for i in range(2))
+        one, two = (datt_got[2 * k + i, :, :128].astype(F32) for i in range(2))
         datt[4, :, k * 128 : (k + 1) * 128] = jnp.where(
             low_lanes, one, pltpu.roll(two, TAIL, 1)
         ).astype(LOW)
@@ -971,7 +1056,6 @@
     grad_kv[...] = (kv_pair[core].astype(F32) + kv_in[...].astype(F32)).astype(LOW)
     kv_sum = plane_reduce_steps(mover, ("x", "z"), grad_kv, kv_bufs, kv_rows)
     advance(kv_sum)
-    advance(rows_sum)
     for h in range(4):
         grad_send[h, :, :HD] = grad_query[h].astype(LOW)
     advance(kv_sum)
@@ -1008,8 +1092,8 @@
     gateup_rows,
     down_rows,
     grad_out,
-    attn_full,
-    normed_one,
+    attn_a,
+    normed_hbm,
     grad_rows,
     tokens,
     gain_ref,
@@ -1021,6 +1105,8 @@
     send_sem,
     recv_sem,
     local_sem,
+    qkv_weight,
+    normed_one,
     part,
     grad_half,
     grad_qkv,
@@ -1031,30 +1117,47 @@
     z = lax.axis_index("z")
     half, _, _, _ = core_rows()
     plane = ("dp", "x")
-    sum_bufs = bufs[:6]
-    out_bufs, qkv_bufs = bufs[6:12], bufs[12:18]
+    sum_bufs = bufs[:5]
+    out_bufs, qkv_bufs = bufs[5:11], bufs[11:17]
+    loads = [
+        pltpu.make_async_copy(attn_a.at[:, :, :, pl.ds(0, 384)], qkv_weight, local_sem.at[0]),
+        pltpu.make_async_copy(normed_hbm, normed_one, local_sem.at[1]),
+    ]
+    for load in loads:
+        load.start()
     greet([{"z": step("z", d)} for d in (1, 2, 3)] + plane_peers(plane) + [sibling()])
     mover = Mover(send_sem, recv_sem)
     out_sum = plane_reduce_steps(mover, plane, grad_out, out_bufs[:5], out_bufs[5])
     advance(out_sum)
     slices = grad_got[...].reshape(RING * BLOCK, 384)
     wide = RING * BLOCK
-    qkv_weight = attn_full[:, :, :, :384].reshape(D, 384)
+    loads[0].wait()
+    weight = qkv_weight[...].reshape(D, 384)
 
     def make(block):
-        part[block] = dot(grad_got[block], qkv_weight, (1, 1)).astype(LOW)
-
-    norm_sum = reduce_steps(mover, part, lambda i: part[i, half], sum_bufs, grad_half, make)
-    advance(norm_sum)
+        part[block] = dot(grad_got[block], weight, (1, 1)).astype(LOW)
+
+    shares = []
+    sharing = share_steps(mover, part, sum_bufs[0], shares, make)
+    advance(sharing)
+    advance(sharing)
+    sums = [
+        reduce_steps(mover, own_rows(part), shares[i], sum_bufs, grad_half, span)
+        for i, span in enumerate(SPANS)
+    ]
+    for one in sums:
+        advance(one)
+    advance(sharing)
+    advance(sharing)
     advance(out_sum)
+    loads[1].wait()
     for i in range(RING):
         left_side = normed_one[:, :, i * wide : (i + 1) * wide].reshape(wide, wide)
         grad_qkv[i] = dot(left_side, slices, (0, 0)).astype(LOW).reshape(RING, BLOCK, 384)
-        if i == 0:
-            advance(norm_sum)
+        if i % 2:
+            advance(sums[i // 2])
     qkv_sum = plane_reduce_steps(mover, plane, grad_qkv, qkv_bufs[:5], qkv_bufs[5])
     advance(qkv_sum)
-    advance(norm_sum)
     advance(out_sum)
     gateup_swap = exchange_steps(mover, gateup_rows, gateup_got)
     advance(gateup_swap)
@@ -1070,7 +1173,8 @@
     advance(out_swap)
     out_got[z] = out_send[z]
     advance(qkv_sum)
-    advance(norm_sum)
+    for one in sums:
+        advance(one)
     rows = tokens[half, :]
     inverse = lax.rsqrt(jnp.mean(rows * rows, axis=-1, keepdims=True) + eps_norm)
     unit = rows * inverse
@@ -1100,7 +1204,7 @@
         scratch_shapes=[
             pltpu.SemaphoreType.DMA((copies,)),
             pltpu.SemaphoreType.DMA((copies,)),
-            pltpu.SemaphoreType.DMA((10,)),
+            pltpu.SemaphoreType.DMA((16,)),
             *scratch,
         ],
         compiler_params=pltpu.CompilerParams(
@@ -1119,6 +1223,8 @@
         "down_rows": ((RING, PAD, 1024), LOW),
     }
     scratch = [
+        pltpu.VMEM((RING, BLOCK, D), LOW),
+        pltpu.VMEM((RING, BLOCK, D), LOW),
         pltpu.VMEM((RING, RING, BLOCK, 2 * (MAIN + TAIL)), LOW),
         pltpu.VMEM((RING, RING, BLOCK, 1024), LOW),
         pltpu.VMEM((RING * BLOCK, 1024), LOW),
@@ -1132,9 +1238,9 @@
         *reduce_scratch(),
         *plane_reduce_scratch(1024),
     ]
-    spaces = [pl.ANY, pltpu.VMEM, pltpu.VMEM, pl.ANY, pl.ANY, pltpu.VMEM]
+    spaces = [pl.ANY] * 5 + [pltpu.VMEM]
     return call(
-        second_kernel, 5, 60, out, scratch, operands, spaces, {"gateup_grads": pl.ANY}
+        second_kernel, 5, 80, out, scratch, operands, spaces, {"gateup_grads": pl.ANY, "da_all": pl.ANY}
     )
 
 
@@ -1146,6 +1252,10 @@
         "output": ((BLOCK, D), F32),
     }
     scratch = [
+        pltpu.VMEM((RING, BLOCK, D), LOW),
+        pltpu.VMEM((RING, RING, BLOCK, 128), LOW),
+        pltpu.VMEM((RING, RING, BLOCK, HD), LOW),
+        pltpu.VMEM((2, RING, RING, BLOCK, HD), LOW),
         pltpu.VMEM((RING, HALF, D), LOW),
         pltpu.VMEM((HALF, D), F32),
         pltpu.VMEM((RING, BLOCK, 384), LOW),
@@ -1165,7 +1275,7 @@
         *plane_reduce_scratch(2 * (MAIN + TAIL)),
         *plane_reduce_scratch(HD),
     ]
-    spaces = [pl.ANY] * 2 + [pltpu.VMEM] * 12
+    spaces = [pl.ANY] * 3 + [pltpu.VMEM] + [pl.ANY] * 2 + [pltpu.VMEM] * 2 + [pl.ANY] + [pltpu.VMEM] * 6
     return call(third_kernel, 2, 100, out, scratch, operands, spaces)
 
 
@@ -1178,6 +1288,8 @@
         "qkv_got": ((RING, PAD, 384), LOW),
     }
     scratch = [
+        pltpu.VMEM((RING, RING, BLOCK, 384), LOW),
+        pltpu.VMEM((RING, BLOCK, D), LOW),
         pltpu.VMEM((RING, BLOCK, D), LOW),
         pltpu.VMEM((HALF, D), F32),
         pltpu.VMEM((RING, RING, BLOCK, 384), LOW),
@@ -1187,7 +1299,7 @@
         *plane_reduce_scratch(384),
         *plane_reduce_scratch(384),
     ]
-    spaces = [pltpu.VMEM] * 9
+    spaces = [pltpu.VMEM] * 4 + [pl.ANY] * 2 + [pltpu.VMEM] * 3
     return call(fourth_kernel, 3, 80, out, scratch, operands, spaces)
 
 
@@ -1263,11 +1375,18 @@
 
     keyvalue_part = lax.dynamic_index_in_dim(w_keyvalue, core, 1, keepdims=False)
     scale_columns = jnp.broadcast_to(norm_scales.T[None], (RING, OWN, 2))
+    out_quarters = head_quarters(w_out.T)
     attn_rows = jnp.concatenate(
-        [head_quarters(w_query), quarters(keyvalue_part), head_quarters(w_out.T), scale_columns],
+        [
+            head_quarters(w_query),
+            quarters(keyvalue_part),
+            out_quarters[..., HD:],
+            pad_to(scale_columns, 2, TAIL),
+            out_quarters[..., :HD],
+        ],
         axis=2,
     ).astype(LOW)
-    attn_rows = pad_to(pad_to(attn_rows, 2, 768), 1, PAD)
+    attn_rows = pad_to(attn_rows, 1, PAD)
     gateup = w_gateup.astype(LOW)
     mains = RING * MAIN
     feed_rows = jnp.concatenate(
@@ -1304,7 +1423,8 @@
         second["gateup_grads"],
         second["da_all"],
         first["residual"],
-        first["attn_full"],
+        first["attn_a"],
+        first["attn_b"],
         first["att_slice"],
         first["query"],
         first["keyvalue"],
@@ -1320,7 +1440,7 @@
         third["gateup_rows"],
         second["down_rows"],
         third["grad_out"],
-        first["attn_full"],
+        first["attn_a"],
         first["normed_one"],
         second["grad_rows"],
         tokens,
@@ -1344,7 +1464,8 @@
         axis=1,
     )
     down_shard = hidden_units(down_shard, 0, MAIN).T
-    out_shard = whole_heads(fourth["out_got"][:, :OWN, :320].astype(F32)).T
+    out_got = fourth["out_got"][:, :OWN].astype(F32)
+    out_shard = jnp.concatenate([whole(out_got[..., 128:]), whole(out_got[..., :TAIL])], axis=1).T
     qkv_shard = fourth["qkv_got"][:, :OWN].astype(F32)
     query_shard = whole_heads(qkv_shard[..., :320])
     kv_half = whole(qkv_shard[..., 320:])

time: 426 us -> 399 us (0.937)
  Pallas kernels: 381 us -> 353 us
    pallas_call x1 -> x0, Pallas kernels: 166 us -> none  [run_first(): pl.pallas_call(first_kernel, out_shape=[jax.ShapeDtypeStruct(shape, kind)...]
    pallas_call x3 -> x4, Pallas kernels: 207 us -> 349 us  [call(): pl.pallas_call(kernel, out_shape=[jax.ShapeDtypeStruct(shape, kind) for s...]
where the time goes in v5:
time: 399 us; the launch traced here: 393 us
  Pallas kernels  353 us (88%)
  local copies, waits for them, and re-layouts  24.3 us (6%)
  other arithmetic  13.2 us (3%)
    pallas_call x4, Pallas kernels, call(): pl.pallas_call(kernel, out_shape=[jax.ShapeDtypeStruct(shape, kind) for s...  349 us
    unnamed x82, local copies, waits for them, and re-layouts  17.1 us
    sub x6, other arithmetic, adam_update(): weight - learn_rate * (corrected + decay_rate * weight)  8.75 us

profile of v5, /device:TPU:1, one launch (start us, length us, event | category | flops | bytes accessed | tf_op | source)
XLA Modules:
  0.0 392.5 jit_solution(13000825500583761535)
XLA Ops:
  1.3 0.8 broadcast_select_fusion
  4.6 0.8 copy_bitcast_fusion
  6.8 1.1 pad.53.feed_rows
  7.9 0.8 copy-done
  8.7 1.0 convert_element_type.63.dy
  9.6 145.2 %shard_map.347 = (bf16[4,4,160,2944]{3,2,1,0:T(8,128)(2,1)}, bf16[4,4,160,512]{3,2,1,0:T(8,128)(2,1)}, bf16[4,4,160,256]{3,2,1,0:T(8,128)(2,1)}, bf16[4,160,2560...) custom-call(bf16[4,48,768]{2,1,0:T(8,128)(2,1)} %pad.26.attn_rows, ...), custom_call_target="tpu_custom_call" | custom-call | tf_op jit(solution)/shard_map/pallas_call | solution.py:1199
  154.8 79.4 %shard_map.348 = (f32[80,2560]{1,0:T(8,128)}, bf16[4,160,2560]{2,1,0:T(8,128)(2,1)}, bf16[4,160,2560]{2,1,0:T(8,128)(2,1)}, bf16[4,4,160,1920]{3,2,1,0:T(8,128)(2,1)}, bf16[4,48,1024]{2,1,0:T(8,128)(2,1)}) custom-call(bf16[4,4,160,2944]{3,2,1,0:T(8,128)(2,1)} %get-tuple-element.47.feed_full, bf16[4,160,2560]{2,1,0:T(8,128)(2,1)} %get-tuple-element.48.normed_two, ...), custom_call_target="tpu_custom_call" | custom-call | tf_op jit(solution)/shard_map/pallas_call | solution.py:1199
  234.2 77.0 %shard_map.349 = (bf16[4,4,160,384]{3,2,1,0:T(8,128)(2,1)}, bf16[4,160,384]{2,1,0:T(8,128)(2,1)}, bf16[4,48,1920]{2,1,0:T(8,128)(2,1)}, f32[160,2560]{1,0:T(8,128)}) custom-call(bf16[4,160,2560]{2,1,0:T(8,128)(2,1)} %get-tuple-element.52.feed_part, bf16[4,4,160,1920]{3,2,1,0:T(8,128)(2,1)} %get-tuple-element.53.gateup_grads, ...), custom_call_target="tpu_custom_call" | custom-call | tf_op jit(solution)/shard_map/pallas_call | solution.py:1199
  311.2 47.7 %shard_map.350 = (f32[160,2560]{1,0:T(8,128)}, bf16[4,48,1920]{2,1,0:T(8,128)(2,1)}, bf16[4,48,1024]{2,1,0:T(8,128)(2,1)}, bf16[4,48,384]{2,1,0:T(8,128)(2,1)}, bf16[4,48,384]{2,1,0:T(8,128)(2,1)}) custom-call(bf16[4,160,384]{2,1,0:T(8,128)(2,1)} %get-tuple-element.63.grad_got, bf16[4,48,1920]{2,1,0:T(8,128)(2,1)} %get-tuple-element.64.gateup_rows, ...), custom_call_target="tpu_custom_call" | custom-call | tf_op jit(solution)/shard_map/pallas_call | solution.py:1199
  359.0 1.0 slice_convert_fusion.3
  360.3 1.0 multiply_subtract_fusion.3
  362.2 1.2 copy-done.9
  363.5 4.1 %multiply_subtract_fusion = (f32[40,2,3840]{2,0,1:T(8,128)}, f32[40,2,3840]{2,0,1:T(8,128)}, f32[40,2,3840]{2,0,1:T(8,128)S(1)}, f32[40]{0:T(128)S(1)}) fusion(f32[40,2,3840]{2,1,0:T(2,128)S(1)} %copy-done.1, f32[40,1,3840]{2,0,1:T(8,128)S(1)} %maximum_bitcast_fusion.1, f32[40,1,3840]{2,0,1:T(8,128)S(1)} %maximum_bitcast_fusion, ...), kind=kLoop, calls=%fused_computation.6 | loop fusion | flops 5836760 | bytes 8601760 | tf_op jit(solution)/shard_map/sub | solution.py:1314
  368.6 3.8 shard_map.351
  372.7 0.8 sqrt_add_fusion
  376.1 0.8 copy-done.5
  377.0 2.6 multiply_subtract_fusion.1
  380.8 0.9 multiply_subtract_fusion.2
  381.7 1.7 copy.234
  383.4 1.7 copy.237
  385.1 1.7 copy.240
  388.9 1.2 copy.285
  390.1 0.9 copy-done.7
  390.9 1.2 copy.286
  (164 shorter events, 12.5 us)
Async XLA Ops:
  0.7 1.5 copy-start.23
  0.7 1.7 copy-start.13
  1.2 1.6 copy-start.11
  1.3 1.6 copy-start.8
  2.9 1.5 copy-start.1
  6.8 1.8 copy-start
  358.9 1.3 copy-start.12
  359.0 1.3 copy-start.19
  359.0 1.3 copy-start.20
  360.0 1.5 copy-start.16
  362.2 1.3 copy-start.9
  363.5 9.0 %copy-start.29 = (f32[2,40]{1,0:T(2,128)S(1)}, f32[2,40]{1,0:T(2,128)}, u32[]{:S(2)}) copy-start(f32[2,40]{1,0:T(2,128)} %param.33) | copy-start | bytes 964
  363.5 9.1 %copy-start.30 = (f32[2,40]{1,0:T(2,128)S(1)}, f32[2,40]{1,0:T(2,128)}, u32[]{:S(2)}) copy-start(f32[2,40]{1,0:T(2,128)} %param.39) | copy-start | bytes 964
  367.6 8.1 %copy-start.17 = (bf16[4,48,1024]{2,1,0:T(8,128)(2,1)S(1)}, bf16[4,48,1024]{2,1,0:T(8,128)(2,1)}, u32[]{:S(2)}) copy-start(bf16[4,48,1024]{2,1,0:T(8,128)(2,1)} %get-tuple-element.73) | copy-start | bytes 1179652
  375.8 1.3 copy-start.15
  377.0 2.6 copy-start.25
  379.7 2.0 copy-start.3
  381.7 1.7 copy-start.2
  385.1 1.7 copy-start.18
  385.1 1.7 copy-start.24
  385.1 1.7 copy-start.26
  385.1 1.7 copy-start.27
  385.1 3.8 copy-start.6
  388.9 2.0 copy-start.7
  (7 other events, 7.1 us)
